TPU v7x, 32 devices: a whole 2x2x4 slice. The times are simulated.
32 devices in a mesh: mode: 2 (over x), ax: 8 (over z, y), rad: 2 (over core).
Axes of the slice: x: 2, y: 2, z: 4, core: 2. Of those that a mesh axis runs over, the one named last changes fastest.
Arguments:
- adjoint: float32 [5, 256, 32, 256], P(None, 'mode', 'ax', 'rad'), may hold values from -6 to 6
- state: float32 [5, 256, 32, 256], P(None, 'mode', 'ax', 'rad'), may hold values from -6 to 6
- wake: float32 [256, 32, 256], P('mode', 'ax', 'rad'), may hold values from 0.2 to 1.5
- jac_axial: float32 [5, 5], replicated, may hold values from -2.5 to 2.5
- jac_radial: float32 [5, 5], replicated, may hold values from -2.5 to 2.5
- jac_swirl: float32 [5, 5], replicated, may hold values from -2.5 to 2.5
- wake_coupling: float32 [5, 5], replicated, may hold values from -2.5 to 2.5
Outputs:
- adjoint_in: float32 [5, 256, 32, 256], P(None, 'mode', 'ax', 'rad')
- wake_grad: float32 [256, 32, 256], P('mode', 'ax', 'rad')
All inputs are finite; a program needn't handle non-finite values.
Results may differ from a plain program's by a relative error of at most 0.000098.
Values sent between devices are 32-bit elements; how exact they have to be, the bound alone decides.
No kernel may reach another device: no remote copies, remote signals or barrier semaphores. Data moves between devices by JAX's collectives and lax.ppermute only.
A program may use at most 64 MiB of HBM per device.

v0:
```python
import math

import jax
import jax.numpy as jnp
from jax import lax
from jax.sharding import PartitionSpec as P

exact_prec = lax.Precision.HIGHEST


def with_halo(block, sides, width):
    for axis, dim in sides:
        count = lax.axis_size(axis)
        forward = [(i, i + 1) for i in range(count - 1)]
        backward = [(target, source) for source, target in forward]
        low = lax.ppermute(
            lax.slice_in_dim(block, block.shape[dim] - width, None, axis=dim), axis, forward
        )
        high = lax.ppermute(lax.slice_in_dim(block, 0, width, axis=dim), axis, backward)
        block = jnp.concatenate([low, block, high], axis=dim)
    return block


def fourier_basis(mode_count):
    angle_idx = jnp.arange(mode_count, dtype=jnp.int32)[:, None]
    coef_idx = jnp.arange(mode_count, dtype=jnp.int32)[None, :]
    orders = coef_idx // 2
    phases = (orders * angle_idx % mode_count).astype(jnp.float32) * jnp.float32(
        2.0 * math.pi / mode_count
    )
    scale_two = jnp.float32(math.sqrt(2.0 / mode_count))
    scale_one = jnp.float32(1.0 / math.sqrt(mode_count))
    table = jnp.where(coef_idx % 2 == 0, scale_two * jnp.cos(phases), scale_two * jnp.sin(phases))
    table = jnp.where(coef_idx == 0, scale_one, table)
    signs = jnp.where(angle_idx % 2 == 0, scale_one, -scale_one)
    table = jnp.where(coef_idx == 1, signs, table)
    return table


def rotate(field, first_order, mode_count):
    fields, modes_here, cells_ax, cells_rad = field.shape
    paired = field.reshape(fields, modes_here // 2, 2, cells_ax, cells_rad)
    orders = (first_order + jnp.arange(modes_here // 2, dtype=jnp.int32)).astype(
        jnp.float32
    ) / jnp.float32(mode_count // 2)
    orders = orders[None, :, None, None]
    turned = jnp.stack([orders * paired[:, :, 1], -orders * paired[:, :, 0]], axis=2)
    return turned.reshape(fields, modes_here, cells_ax, cells_rad)


def body(adjoint, state, wake, jac_axial, jac_radial, jac_swirl, wake_coupling):
    fields, modes_here, cells_ax, cells_rad = adjoint.shape
    mode_groups = lax.axis_size("mode")
    mode_count = modes_here * mode_groups
    points = cells_ax * cells_rad
    padded = with_halo(adjoint, (("ax", 2), ("rad", 3)), 1)
    axial_diff = 0.5 * (padded[:, :, 2:, 1:-1] - padded[:, :, :-2, 1:-1])
    radial_diff = 0.5 * (padded[:, :, 1:-1, 2:] - padded[:, :, 1:-1, :-2])
    rad_first = lax.axis_index("rad") * cells_rad
    radial_total = cells_rad * lax.axis_size("rad")
    radius = 0.5 + (
        (rad_first + jnp.arange(cells_rad, dtype=jnp.int32)).astype(jnp.float32) + 0.5
    ) / jnp.float32(2.0 * radial_total)
    swirl_rate = 0.25 / radius
    turned = rotate(adjoint, lax.axis_index("mode") * (modes_here // 2), mode_count) * swirl_rate
    transport = jnp.einsum("ef,ekxr->fkxr", jac_axial, axial_diff, precision=exact_prec)
    transport = transport + jnp.einsum(
        "ef,ekxr->fkxr", jac_radial, radial_diff, precision=exact_prec
    )
    transport = transport + jnp.einsum("ef,ekxr->fkxr", jac_swirl, turned, precision=exact_prec)
    coupled = jnp.einsum("fe,ekxr->fkxr", wake_coupling, state, precision=exact_prec)
    flat_adj = adjoint.reshape(fields, modes_here, points)
    flat_cpl = coupled.reshape(fields, modes_here, points)
    flat_wake = wake.reshape(1, modes_here, points)
    basis_table = fourier_basis(mode_count)
    split_rad = lax.axis_size("rad")
    column_count = points // (mode_groups * split_rad)
    adj_recv, cpl_recv, wake_recv = (
        lax.all_to_all(flat_adj, ("mode", "rad"), split_axis=2, concat_axis=1, tiled=True),
        lax.all_to_all(flat_cpl, ("mode", "rad"), split_axis=2, concat_axis=1, tiled=True),
        lax.all_to_all(flat_wake, ("mode", "rad"), split_axis=2, concat_axis=1, tiled=True),
    )
    adj_five = adj_recv.reshape(fields, mode_groups, split_rad, modes_here, column_count)
    cpl_five = cpl_recv.reshape(fields, mode_groups, split_rad, modes_here, column_count)
    wake_five = wake_recv.reshape(1, mode_groups, split_rad, modes_here, column_count)
    basis_four = basis_table.reshape(mode_groups, modes_here, mode_groups, modes_here)
    adj_angle = jnp.einsum("abcd,fcsdp->fasbp", basis_four, adj_five, precision=exact_prec)
    cpl_angle = jnp.einsum("abcd,fcsdp->fasbp", basis_four, cpl_five, precision=exact_prec)
    grad_here = -jnp.sum(adj_angle * cpl_angle, axis=0, keepdims=True)
    returned = jnp.einsum(
        "abcd,fasbp->fcsdp", basis_four, wake_five * adj_angle, precision=exact_prec
    )
    returned_flat = returned.reshape(fields, mode_count * split_rad, column_count)
    grad_flat = grad_here.reshape(1, mode_count * split_rad, column_count)
    back_home, grad_home = (
        lax.all_to_all(returned_flat, ("mode", "rad"), split_axis=1, concat_axis=2, tiled=True),
        lax.all_to_all(grad_flat, ("mode", "rad"), split_axis=1, concat_axis=2, tiled=True),
    )
    back_field = back_home.reshape(fields, modes_here, cells_ax, cells_rad)
    wake_grad = grad_home.reshape(modes_here, cells_ax, cells_rad)
    adjoint_in = (
        adjoint
        + transport
        - jnp.einsum("ef,ekxr->fkxr", wake_coupling, back_field, precision=exact_prec)
    )
    return (adjoint_in, wake_grad)


def solution(mesh):
    return jax.shard_map(
        body,
        mesh=mesh,
        in_specs=(
            P(None, "mode", "ax", "rad"),
            P(None, "mode", "ax", "rad"),
            P("mode", "ax", "rad"),
            P(),
            P(),
            P(),
            P(),
        ),
        out_specs=(P(None, "mode", "ax", "rad"), P("mode", "ax", "rad")),
        check_vma=False,
    )
```

profile of v0, /device:TPU:0, one launch (start us, length us, event | category | flops | bytes accessed | tf_op | source)
XLA Modules:
  0.0 145.4 jit_solution(18316870669848469350)
XLA Ops:
  0.6 0.0 copy-start
  0.6 0.0 copy-start.1
  0.7 1.9 %copy.127 = f32[128,4,128]{0,2,1:T(8,128)} copy(f32[128,4,128]{2,1,0:T(4,128)} %param.9) | data formatting | bytes 524288 | tf_op args[2]
  2.6 4.2 %all-to-all-start = ((f32[1,128,512]{1,0,2:T(1,128)}), f32[1,128,512]{1,0,2:T(1,128)S(1)}, u32[]{:S(2)}, u32[]{:S(2)}) async-start(f32[1,128,512]{1,0,2:T(1,128)} %bitcast.6), calls=%async_computation | async-start | bytes 524288 | tf_op jit(solution)/shard_map/all_to_all | solution.py:81
  6.8 3.3 %fusion.48 = (f32[5,128,1,128]{3,2,1,0:T(1,128)}, f32[5,128,1,128]{3,2,1,0:T(1,128)}) fusion(f32[5,128,4,128]{3,2,1,0:T(4,128)} %param.7), kind=kLoop, calls=%fused_computation.74 | loop fusion | bytes 1310720 | tf_op jit(solution)/shard_map/slice | solution.py:19
  10.1 4.8 %collective-permute-start.1 = (f32[5,128,1,128]{3,1,2,0:T(8,128)}, f32[5,128,1,128]{3,1,2,0:T(8,128)}, u32[]{:S(2)}, u32[]{:S(2)}) collective-permute-start(f32[5,128,1,128]{3,1,2,0:T(8,128)} %bitcast.58), channel_id=1, source_target_pairs={{0,2},{2,4},{4,6},{6,8},{8,10},{10,12},{12,14},{1,3},{3,5},{5,7},{... | collective-permute-start | bytes 983048 | tf_op jit(solution)/shard_map/ppermute | solution.py:16
  14.9 1.3 collective-permute-start
  16.2 0.0 copy-done.1
  16.2 1.2 slice_multiply_fusion.1
  17.4 2.0 %copy.129 = f32[5,128,4,128]{1,0,3,2:T(8,128)} copy(f32[5,128,4,128]{3,2,1,0:T(4,128)S(1)} %copy-done.1) | data formatting | bytes 2621440 | tf_op args[0]
  19.4 1.7 %copy.116 = f32[5,128,4,128]{1,2,3,0:T(4,128)} copy(f32[5,128,4,128]{3,2,1,0:T(4,128)S(1)} %copy-done.1) | data formatting | bytes 2621440 | tf_op args[0]
  21.0 1.6 %copy.108 = f32[5,128,4,128]{1,3,2,0:T(8,128)} copy(f32[5,128,4,128]{3,2,1,0:T(4,128)S(1)} %copy-done.1) | data formatting | bytes 2621440 | tf_op args[0]
  22.7 1.4 pad_maximum_fusion.5
  24.1 2.1 %copy.124 = f32[5,64,2,4,128]{4,0,3,2,1:T(8,128)} copy(f32[5,64,2,4,128]{4,3,2,1,0:T(4,128)S(1)} %pad_maximum_fusion.5) | data formatting | bytes 2621440 | tf_op jit(solution)/shard_map/stack | solution.py:47
  26.2 0.0 all-to-all-done
  26.2 0.7 copy-done.3
  26.9 4.4 %all-to-all-start.1 = ((f32[5,128,512]{1,0,2:T(8,128)}), f32[5,128,512]{1,0,2:T(8,128)}, u32[]{:S(2)}, u32[]{:S(2)}) async-start(f32[5,128,512]{1,0,2:T(8,128)} %bitcast.102), calls=%async_computation.1 | async-start | bytes 4194304 | tf_op jit(solution)/shard_map/all_to_all | solution.py:79
  31.4 3.9 %fusion.3 = f32[5,128,4,128]{3,0,2,1:T(8,128)} fusion(f32[5,128,4,128]{3,2,1,0:T(4,128)S(1)} %copy-done, f32[5,5]{1,0:T(8,128)S(1)} %copy-done.7), kind=kOutput, calls=%fused_computation.7 | convolution fusion | flops 19660800 | bytes 2621540 | tf_op jit(solution)/shard_map/fe,ekxr->fkxr/dot_general | solution.py:71
  35.2 3.1 %copy.174 = f32[5,128,4,128]{1,0,3,2:T(8,128)} copy(f32[5,128,4,128]{3,0,2,1:T(8,128)} %fusion.3) | data formatting | bytes 2621440 | tf_op jit(solution)/shard_map/reshape | solution.py:73
  38.4 0.5 fusion.33
  38.9 0.6 broadcast_compare_fusion
  39.5 17.6 %all-to-all-done.1 = f32[5,128,512]{1,0,2:T(8,128)} async-done(((f32[5,128,512]{1,0,2:T(8,128)}), f32[5,128,512]{1,0,2:T(8,128)}, u32[]{:S(2)}, u32[]{:S(2)}) %all-to-all-start.1) | async-done | bytes 1310752 | tf_op jit(solution)/shard_map/all_to_all | solution.py:79
  57.1 4.6 %all-to-all-start.3 = ((f32[5,128,512]{1,0,2:T(8,128)}), f32[5,128,512]{1,0,2:T(8,128)}, u32[]{:S(2)}, u32[]{:S(2)}) async-start(f32[5,128,512]{1,0,2:T(8,128)} %bitcast.101), calls=%async_computation.3 | async-start | bytes 4194304 | tf_op jit(solution)/shard_map/all_to_all | solution.py:80
  61.7 0.0 copy-start.11
  61.7 1.8 %bitcast_multiply_fusion = f32[5,128,4,128]{3,0,2,1:T(8,128)S(1)} fusion(f32[5,64,2,4,128]{4,0,3,2,1:T(8,128)} %copy.124, f32[128]{0:T(128)S(1)} %add_divide_fusion), kind=kLoop, calls=%fused_computation.6 | loop fusion | flops 327680 | bytes 2621952 | tf_op jit(solution)/shard_map/mul | solution.py:65
  63.6 0.0 copy-start.4
  63.6 3.3 %fusion.27 = f32[128,4,128,5]{2,3,1,0:T(8,128)} fusion(f32[5,128,4,128]{3,0,2,1:T(8,128)S(1)} %bitcast_multiply_fusion, f32[5,5]{1,0:T(8,128)S(1)} %copy-done.11), kind=kOutput, calls=%fused_computation.44 | convolution fusion | flops 19660800 | bytes 2621540 | tf_op jit(solution)/shard_map/ef,ekxr->fkxr/dot_general | solution.py:70
  66.9 0.0 copy-done.4
  66.9 0.1 copy.128
  67.0 0.0 collective-permute-done.1
  67.0 1.1 copy.115
  68.2 0.0 collective-permute-done
  68.2 1.1 copy.117
  69.3 3.7 %pad_maximum_fusion = f32[5,128,6,128]{1,2,3,0:T(8,128)} fusion(f32[5,128,1,128]{1,2,3,0:T(1,128)S(1)} %copy.117, f32[5,128,4,128]{1,2,3,0:T(4,128)} %copy.116, f32[5,128,1,128]{1,2,3,0:T(1,128)S(1)} %copy.115), kind=kLoop, calls=%fused_computation | loop fusion | flops 983040 | bytes 3932160 | tf_op jit(solution)/shard_map/concatenate | solution.py:20
  73.0 2.6 %copy.132 = f32[5,2,2,128,128]{4,3,1,2,0:T(8,128)} copy(f32[5,2,2,128,128]{3,0,4,2,1:T(8,128)} %bitcast.16) | data formatting | bytes 2621440 | tf_op jit(solution)/shard_map/reshape | solution.py:83
  75.7 4.8 %convolution_bitcast_fusion.2 = f32[5,2,2,128,128]{4,3,2,0,1:T(8,128)} fusion(f32[5,2,2,128,128]{4,3,1,2,0:T(8,128)} %copy.132, s32[2,128]{1,0:T(2,128)S(1)} %multiply_add_fusion, s32[2,128]{1,0:T(2,128)S(1)} %and_select_fusion, f32[2,128]{1,0:T(2,128)S(1)} %broadcast_select_fusion, pred[2,128]{1,0:T(4,128)(4,1)S(1)} %copy-done.8, ...), kind=kOutput, calls=%fused_computation.12 | convolution fusion | flops 1007878144 | bytes 2625280 | tf_op jit(solution)/shard_map/abcd,fcsdp->fasbp/dot_general | solution.py:87
  80.4 6.9 %all-to-all-done.3 = f32[5,128,512]{1,0,2:T(8,128)} async-done(((f32[5,128,512]{1,0,2:T(8,128)}), f32[5,128,512]{1,0,2:T(8,128)}, u32[]{:S(2)}, u32[]{:S(2)}) %all-to-all-start.3) | async-done | bytes 1310752 | tf_op jit(solution)/shard_map/all_to_all | solution.py:80
  87.3 6.1 %fusion.15 = f32[2,2,128,128]{3,2,1,0:T(8,128)S(1)} fusion(f32[5,2,2,128,128]{4,3,2,0,1:T(8,128)} %convolution_bitcast_fusion.2, f32[5,2,2,128,128,1]{3,0,4,2,1,5:T(8,128)} %bitcast.40, s32[2,128]{1,0:T(2,128)S(1)} %multiply_add_fusion, s32[2,128]{1,0:T(2,128)S(1)} %and_select_fusion, f32[2,128]{1,0:T(2,128)S(1)} %broadcast_select_fusion, ...), kind=kOutput, calls=%fused_computation.26 | convolution fusion | flops 1008467968 | bytes 2887424 | tf_op jit(solution)/shard_map/abcd,fcsdp->fasbp/dot_general | solution.py:88
  93.4 0.7 neg.24
  94.1 3.4 %all-to-all-start.4 = ((f32[1,512,128]{2,0,1:T(1,128)}), f32[1,512,128]{2,0,1:T(1,128)S(1)}, u32[]{:S(2)}, u32[]{:S(2)}) async-start(f32[1,512,128]{2,0,1:T(1,128)} %bitcast.44), calls=%async_computation.4 | async-start | bytes 524288 | tf_op jit(solution)/shard_map/all_to_all | solution.py:97
  97.5 3.8 %convolution_bitcast_fusion.1 = f32[5,2,2,128,128]{4,3,1,2,0:T(8,128)S(1)} fusion(f32[5,2,2,128,128]{4,3,2,0,1:T(8,128)} %convolution_bitcast_fusion.2, f32[2,2,128,128]{3,2,1,0:T(8,128)S(1)} %bitcast.104, s32[2,128]{1,0:T(2,128)S(1)} %multiply_add_fusion, s32[2,128]{1,0:T(2,128)S(1)} %and_select_fusion, pred[2,128]{1,0:T(4,128)(4,1)S(1)} %copy-done.8, ...), kind=kOutput, calls=%fused_computation.11 | convolution fusion | flops 1008205824 | bytes 2887424 | tf_op jit(solution)/shard_map/abcd,fasbp->fcsdp/dot_general | solution.py:90
  101.4 0.1 copy.135
  101.5 2.2 %copy.136 = f32[5,512,128]{2,0,1:T(8,128)} copy(f32[5,512,128]{2,1,0:T(8,128)S(1)} %bitcast.103) | data formatting | bytes 2621440 | tf_op jit(solution)/shard_map/reshape | solution.py:93
  103.7 0.0 all-to-all-done.4
  103.7 0.7 copy-done.5
  104.4 4.5 %all-to-all-start.2 = ((f32[5,512,128]{2,0,1:T(8,128)}), f32[5,512,128]{2,0,1:T(8,128)}, u32[]{:S(2)}, u32[]{:S(2)}) async-start(f32[5,512,128]{2,0,1:T(8,128)} %copy.136), calls=%async_computation.2 | async-start | bytes 4194304 | tf_op jit(solution)/shard_map/all_to_all | solution.py:96
  108.9 0.8 fusion.47
  109.6 1.3 collective-permute-start.2
  110.9 3.2 %collective-permute-start.3 = (f32[5,128,6,1]{1,2,3,0:T(8,128)S(1)}, f32[5,128,6,1]{1,2,3,0:T(8,128)S(1)}, u32[]{:S(2)}, u32[]{:S(2)}) collective-permute-start(f32[5,128,6,1]{1,2,3,0:T(8,128)S(1)} %get-tuple-element.13), channel_id=1, source_target_pairs={{0,1},{2,3},{4,5},{6,7},{8,9},{10,11},{12,13},{14,15},{16,17},{18,... | collective-permute-start | bytes 46088 | tf_op jit(solution)/shard_map/ppermute | solution.py:16
  114.2 1.1 copy.109
  115.3 1.1 copy.111
  116.4 2.7 %fusion.11 = f32[5,128,4,128]{1,3,2,0:T(8,128)} fusion(f32[5,128,4,128]{1,3,2,0:T(8,128)} %copy.108, f32[5,128,1,128]{1,3,2,0:T(8,128)S(1)} %copy.111, f32[5,128,1,128]{1,3,2,0:T(8,128)S(1)} %copy.109), kind=kLoop, calls=%fused_computation.19 | loop fusion | flops 1310720 | bytes 3276800 | tf_op jit(solution)/shard_map/mul | solution.py:57
  119.2 2.9 %copy.113 = f32[5,128,4,128]{3,0,2,1:T(8,128)} copy(f32[5,128,4,128]{1,3,2,0:T(8,128)} %fusion.11) | data formatting | bytes 2621440 | tf_op jit(solution)/shard_map/mul | solution.py:57
  122.1 5.0 %fusion.31 = f32[128,4,128,5]{2,3,1,0:T(8,128)} fusion(f32[5,128,4,128]{3,0,2,1:T(8,128)} %copy.113, f32[5,5]{1,0:T(8,128)S(1)} %copy-done.12), kind=kOutput, calls=%fused_computation.48 | convolution fusion | flops 19660800 | bytes 2621540 | tf_op jit(solution)/shard_map/ef,ekxr->fkxr/dot_general | solution.py:66
  127.1 0.4 copy.118
  127.5 0.0 collective-permute-done.2
  127.5 0.0 collective-permute-done.3
  127.5 1.3 fusion.9
  128.9 2.9 %copy.122 = f32[5,128,4,128]{3,0,2,1:T(8,128)} copy(f32[5,128,4,128]{1,3,2,0:T(8,128)} %fusion.9) | data formatting | bytes 2621440 | tf_op jit(solution)/shard_map/mul | solution.py:58
  131.8 4.9 %fusion.29 = f32[128,4,128,5]{2,3,1,0:T(8,128)} fusion(f32[5,128,4,128]{3,0,2,1:T(8,128)} %copy.122, f32[5,5]{1,0:T(8,128)S(1)} %copy-done.13), kind=kOutput, calls=%fused_computation.46 | convolution fusion | flops 19660800 | bytes 2621540 | tf_op jit(solution)/shard_map/ef,ekxr->fkxr/dot_general | solution.py:67
  136.7 0.9 copy.148
  137.6 0.0 all-to-all-done.2
  137.6 6.4 %bitcast_subtract_fusion = f32[5,128,4,128]{3,0,2,1:T(8,128)S(1)} fusion(f32[5,128,4,128]{3,2,1,0:T(4,128)S(1)} %copy-done.1, f32[128,4,128,5]{2,3,1,0:T(8,128)} %fusion.27, f32[128,4,128,5]{2,3,1,0:T(8,128)} %fusion.31, f32[128,4,128,5]{2,3,1,0:T(8,128)} %fusion.29, f32[5,4,128,128]{3,0,2,1:T(8,128)} %bitcast.27, f32[5,5]{1,0:T(8,128)S(1)} %copy-done.7), kind=kOutput, calls=%fused_computation.1 | convolution fusion | flops 20971520 | bytes 7864420 | tf_op jit(solution)/shard_map/ef,ekxr->fkxr/dot_general | solution.py:104
  144.0 1.4 copy.147
  (27 shorter events, 0.1 us)
Async XLA Ops:
  0.6 30.7 %copy-start = (f32[5,128,4,128]{3,2,1,0:T(4,128)S(1)}, f32[5,128,4,128]{3,2,1,0:T(4,128)}, u32[]{:S(2)}) copy-start(f32[5,128,4,128]{3,2,1,0:T(4,128)} %param.8) | copy-start | bytes 3932164
  0.6 15.6 %copy-start.1 = (f32[5,128,4,128]{3,2,1,0:T(4,128)S(1)}, f32[5,128,4,128]{3,2,1,0:T(4,128)}, u32[]{:S(2)}) copy-start(f32[5,128,4,128]{3,2,1,0:T(4,128)} %param.7) | copy-start | bytes 3932164
  2.6 23.6 %all-to-all-start = ((f32[1,128,512]{1,0,2:T(1,128)}), f32[1,128,512]{1,0,2:T(1,128)S(1)}, u32[]{:S(2)}, u32[]{:S(2)}) async-start(f32[1,128,512]{1,0,2:T(1,128)} %bitcast.6), calls=%async_computation | async-start | bytes 524288 | tf_op jit(solution)/shard_map/all_to_all | solution.py:81
  10.1 56.9 %collective-permute-start.1 = (f32[5,128,1,128]{3,1,2,0:T(8,128)}, f32[5,128,1,128]{3,1,2,0:T(8,128)}, u32[]{:S(2)}, u32[]{:S(2)}) collective-permute-start(f32[5,128,1,128]{3,1,2,0:T(8,128)} %bitcast.58), channel_id=1, source_target_pairs={{0,2},{2,4},{4,6},{6,8},{8,10},{10,12},{12,14},{1,3},{3,5},{5,7},{... | collective-permute-start | bytes 983048 | tf_op jit(solution)/shard_map/ppermute | solution.py:16
  14.9 53.3 %collective-permute-start = (f32[5,128,1,128]{3,1,2,0:T(8,128)}, f32[5,128,1,128]{3,1,2,0:T(8,128)}, u32[]{:S(2)}, u32[]{:S(2)}) collective-permute-start(f32[5,128,1,128]{3,1,2,0:T(8,128)} %bitcast.57), channel_id=1, source_target_pairs={{2,0},{4,2},{6,4},{8,6},{10,8},{12,10},{14,12},{3,1},{5,3},{7,5},{... | collective-permute-start | bytes 983048 | tf_op jit(solution)/shard_map/ppermute | solution.py:19
  26.2 0.7 copy-start.3
  26.2 5.2 %copy-start.7 = (f32[5,5]{1,0:T(8,128)S(1)}, f32[5,5]{1,0:T(8,128)}, u32[]{:S(2)}) copy-start(f32[5,5]{1,0:T(8,128)} %param.13) | copy-start | bytes 304
  26.9 30.2 %all-to-all-start.1 = ((f32[5,128,512]{1,0,2:T(8,128)}), f32[5,128,512]{1,0,2:T(8,128)}, u32[]{:S(2)}, u32[]{:S(2)}) async-start(f32[5,128,512]{1,0,2:T(8,128)} %bitcast.102), calls=%async_computation.1 | async-start | bytes 4194304 | tf_op jit(solution)/shard_map/all_to_all | solution.py:79
  57.1 30.2 %all-to-all-start.3 = ((f32[5,128,512]{1,0,2:T(8,128)}), f32[5,128,512]{1,0,2:T(8,128)}, u32[]{:S(2)}, u32[]{:S(2)}) async-start(f32[5,128,512]{1,0,2:T(8,128)} %bitcast.101), calls=%async_computation.3 | async-start | bytes 4194304 | tf_op jit(solution)/shard_map/all_to_all | solution.py:80
  61.7 1.8 %copy-start.11 = (f32[5,5]{1,0:T(8,128)S(1)}, f32[5,5]{1,0:T(8,128)}, u32[]{:S(2)}) copy-start(f32[5,5]{1,0:T(8,128)} %param.12) | copy-start | bytes 304
  63.6 3.3 %copy-start.4 = (f32[1,128,512]{1,0,2:T(1,128)S(1)}, f32[1,128,512]{1,0,2:T(1,128)}, u32[]{:S(2)}) copy-start(f32[1,128,512]{1,0,2:T(1,128)} %copy-done.3) | copy-start | bytes 786436
  73.0 2.7 %copy-start.8 = (pred[2,128]{1,0:T(4,128)(4,1)S(1)}, pred[2,128]{1,0:T(4,128)(4,1)}, u32[]{:S(2)}) copy-start(pred[2,128]{1,0:T(4,128)(4,1)} %fusion.33) | copy-start | bytes 772
  73.0 2.7 %copy-start.9 = (pred[2,128]{1,0:T(4,128)(4,1)S(1)}, pred[2,128]{1,0:T(4,128)(4,1)}, u32[]{:S(2)}) copy-start(pred[2,128]{1,0:T(4,128)(4,1)} %get-tuple-element.20) | copy-start | bytes 772
  73.0 2.7 %copy-start.10 = (pred[2,128]{1,0:T(4,128)(4,1)S(1)}, pred[2,128]{1,0:T(4,128)(4,1)}, u32[]{:S(2)}) copy-start(pred[2,128]{1,0:T(4,128)(4,1)} %get-tuple-element.21) | copy-start | bytes 772
  94.1 9.6 %all-to-all-start.4 = ((f32[1,512,128]{2,0,1:T(1,128)}), f32[1,512,128]{2,0,1:T(1,128)S(1)}, u32[]{:S(2)}, u32[]{:S(2)}) async-start(f32[1,512,128]{2,0,1:T(1,128)} %bitcast.44), calls=%async_computation.4 | async-start | bytes 524288 | tf_op jit(solution)/shard_map/all_to_all | solution.py:97
  103.7 0.7 copy-start.5
  104.4 33.2 %all-to-all-start.2 = ((f32[5,512,128]{2,0,1:T(8,128)}), f32[5,512,128]{2,0,1:T(8,128)}, u32[]{:S(2)}, u32[]{:S(2)}) async-start(f32[5,512,128]{2,0,1:T(8,128)} %copy.136), calls=%async_computation.2 | async-start | bytes 4194304 | tf_op jit(solution)/shard_map/all_to_all | solution.py:96
  109.6 17.9 %collective-permute-start.2 = (f32[5,128,6,1]{1,2,3,0:T(8,128)S(1)}, f32[5,128,6,1]{1,2,3,0:T(8,128)S(1)}, u32[]{:S(2)}, u32[]{:S(2)}) collective-permute-start(f32[5,128,6,1]{1,2,3,0:T(8,128)S(1)} %get-tuple-element.12), channel_id=1, source_target_pairs={{1,0},{3,2},{5,4},{7,6},{9,8},{11,10},{13,12},{15,14},{17,16},{19,... | collective-permute-start | bytes 46088 | tf_op jit(solution)/shard_map/ppermute | solution.py:19
  110.9 16.6 %collective-permute-start.3 = (f32[5,128,6,1]{1,2,3,0:T(8,128)S(1)}, f32[5,128,6,1]{1,2,3,0:T(8,128)S(1)}, u32[]{:S(2)}, u32[]{:S(2)}) collective-permute-start(f32[5,128,6,1]{1,2,3,0:T(8,128)S(1)} %get-tuple-element.13), channel_id=1, source_target_pairs={{0,1},{2,3},{4,5},{6,7},{8,9},{10,11},{12,13},{14,15},{16,17},{18,... | collective-permute-start | bytes 46088 | tf_op jit(solution)/shard_map/ppermute | solution.py:16
  119.2 3.0 %copy-start.12 = (f32[5,5]{1,0:T(8,128)S(1)}, f32[5,5]{1,0:T(8,128)}, u32[]{:S(2)}) copy-start(f32[5,5]{1,0:T(8,128)} %param.10) | copy-start | bytes 304
  122.1 5.0 %copy-start.2 = (f32[5,128,6,128]{1,2,3,0:T(8,128)S(1)}, f32[5,128,6,128]{1,2,3,0:T(8,128)}, u32[]{:S(2)}) copy-start(f32[5,128,6,128]{1,2,3,0:T(8,128)} %pad_maximum_fusion) | copy-start | bytes 5898244
  128.9 3.0 %copy-start.13 = (f32[5,5]{1,0:T(8,128)S(1)}, f32[5,5]{1,0:T(8,128)}, u32[]{:S(2)}) copy-start(f32[5,5]{1,0:T(8,128)} %param.11) | copy-start | bytes 304
  131.8 4.9 %copy-start.6 = (f32[1,512,128]{2,0,1:T(1,128)S(1)}, f32[1,512,128]{2,0,1:T(1,128)}, u32[]{:S(2)}) copy-start(f32[1,512,128]{2,0,1:T(1,128)} %copy-done.5) | copy-start | bytes 786436
where the time goes:
time: 147 us; the launch traced here: 145 us
  matrix products  38.1 us (26%)
  local copies, waits for them, and re-layouts  36.1 us (25%)
  starting transfers between devices  31.8 us (22%)
  waiting for transfers between devices  24.5 us (17%)
  other arithmetic  13.9 us (9%)
    all_to_all x1, waiting for transfers between devices, body(): lax.all_to_all(flat_adj, ('mode', 'rad'), split_axis=2, concat_axis=1, ti...  17.6 us
    unnamed x34, local copies, waits for them, and re-layouts  11 us
    ppermute x2, starting transfers between devices, with_halo(): lax.ppermute(lax.slice_in_dim(block, block.shape[dim] - width, None, axis...  8.07 us
    all_to_all x1, waiting for transfers between devices, body(): lax.all_to_all(flat_cpl, ('mode', 'rad'), split_axis=2, concat_axis=1, ti...  6.88 us
    dot_general x1, matrix products, body(): jnp.einsum('ef,ekxr->fkxr', wake_coupling, back_field, precision=exact_prec)  6.37 us
    dot_general x1, matrix products, body(): jnp.einsum('abcd,fcsdp->fasbp', basis_four, cpl_five, precision=exact_prec)  6.08 us
    dot_general x1, matrix products, body(): jnp.einsum('ef,ekxr->fkxr', jac_axial, axial_diff, precision=exact_prec)  4.97 us
    dot_general x1, matrix products, body(): jnp.einsum('ef,ekxr->fkxr', jac_radial, radial_diff, precision=exact_prec)  4.9 us
  transfers between devices with their start and end apart: 9, of which 2 were waited for; matrix products, arithmetic and copies ran while one was open for 48% of the time, Pallas kernels for 0%

commit v1 on v0

v1 whole, which is shorter than its diff:
```python
import functools
import math

import jax
import jax.numpy as jnp
import ml_dtypes
import numpy as np
from jax import lax
from jax.experimental import pallas as pl
from jax.experimental.pallas import tpu as pltpu
from jax.sharding import PartitionSpec as P

VMEM_LIMIT = 32 * 1024 * 1024


def fourier_basis(count):
    angle = np.arange(count)[:, None]
    coef = np.arange(count)[None, :]
    phase = ((coef // 2) * angle % count) * (2.0 * math.pi / count)
    table = math.sqrt(2.0 / count) * np.where(coef % 2 == 0, np.cos(phase), np.sin(phase))
    table = np.where(coef == 0, 1.0 / math.sqrt(count), table)
    table = np.where(coef == 1, np.where(angle % 2 == 0, 1.0, -1.0) / math.sqrt(count), table)
    return table.astype(np.float32)


def three_terms(table):
    high = table.astype(ml_dtypes.bfloat16)
    low = (table - high.astype(np.float32)).astype(ml_dtypes.bfloat16)
    return np.concatenate([high, low, high], axis=-1)


def tables(groups, modes_here):
    count = groups * modes_here
    basis = fourier_basis(count)
    own, other, back = [], [], []
    for m in range(groups):
        rolled = np.roll(np.roll(basis, -m * modes_here, axis=0), -m * modes_here, axis=1)
        blocks = [rolled[:, s * modes_here : (s + 1) * modes_here] for s in range(groups)]
        own.append(three_terms(blocks[0]))
        other.append(np.stack([three_terms(block) for block in blocks[1:]]))
        back.append(three_terms(np.ascontiguousarray(blocks[0].T)))
    return np.stack(own), np.stack(other), np.stack(back)


def split(value):
    high = value.astype(jnp.bfloat16)
    low = (value - high.astype(jnp.float32)).astype(jnp.bfloat16)
    return high, low


def put_split(terms, row, rows, total, cols, value):
    high, low = split(value)
    terms[pl.ds(row, rows), cols] = high
    terms[pl.ds(total + row, rows), cols] = high
    terms[pl.ds(2 * total + row, rows), cols] = low


def own_kernel(dims, where, adj, state, coupling, table, a_out, c_out, terms_a, terms_c):
    fields, modes, cells_ax, width, cols_of = dims
    for j in range(width):
        x = pl.program_id(0) * width + j
        rows = pl.ds(x, modes, stride=cells_ax)
        for f in range(fields):
            put_split(terms_a, 0, modes, modes, cols_of(j, f), adj[f, rows, :])
    a_out[0] = jnp.dot(table[0], terms_a[...], preferred_element_type=jnp.float32)
    for j in range(width):
        x = pl.program_id(0) * width + j
        rows = pl.ds(x, modes, stride=cells_ax)
        for f in range(fields):
            mixed = coupling[f, 0] * state[0, rows, :]
            for e in range(1, fields):
                mixed = mixed + coupling[f, e] * state[e, rows, :]
            put_split(terms_c, 0, modes, modes, cols_of(j, f), mixed)
    c_out[0] = jnp.dot(table[0], terms_c[...], preferred_element_type=jnp.float32)


def join_kernel(dims, groups, where, *refs):
    fields, modes, cells_ax, width, cols_of = dims
    recv = refs[: groups - 1]
    a_own, c_own, table, a_out = refs[groups - 1 : groups + 3]
    h_out = refs[groups + 3 : 2 * groups + 3]
    terms = refs[2 * groups + 3]
    total = a_own[0]
    for s in range(groups - 1):
        for j in range(width):
            x = pl.program_id(0) * width + j
            rows = pl.ds(x, modes, stride=cells_ax)
            for f in range(fields):
                put_split(terms, 0, modes, modes, cols_of(j, f), recv[s][f, rows, :])
        total = total + jnp.dot(table[0, s], terms[...], preferred_element_type=jnp.float32)
    a_out[0] = total
    for j in range(width):
        x = pl.program_id(0) * width + j
        rows = pl.ds(x, modes, stride=cells_ax)
        for s in range(groups):
            here = pl.ds(s * modes, modes)
            part = a_out[0, here, cols_of(j, 0)] * c_own[0, here, cols_of(j, 0)]
            for f in range(1, fields):
                part = part + a_out[0, here, cols_of(j, f)] * c_own[0, here, cols_of(j, f)]
            h_out[s][rows, :] = part


def back_kernel(dims, groups, where, *refs):
    fields, modes, cells_ax, width, cols_of = dims
    wakes = refs[:groups]
    angle, base, coupling, table, out, terms = refs[groups:]
    count = groups * modes
    for j in range(width):
        x = pl.program_id(0) * width + j
        rows = pl.ds(x, modes, stride=cells_ax)
        for s in range(groups):
            wake = wakes[s][rows, :]
            for f in range(fields):
                scaled = wake * angle[0, pl.ds(s * modes, modes), cols_of(j, f)]
                put_split(terms, s * modes, modes, count, cols_of(j, f), scaled)
    returned = jnp.dot(table[0], terms[...], preferred_element_type=jnp.float32)
    for j in range(width):
        x = pl.program_id(0) * width + j
        rows = pl.ds(x, modes, stride=cells_ax)
        for f in range(fields):
            value = base[f, rows, :]
            for e in range(fields):
                value = value - coupling[e, f] * returned[:, cols_of(j, e)]
            out[f, rows, :] = value


def base_kernel(
    fields, modes, cells_ax, chunk, mode_total, rad_total, rad_size,
    where, adj, below, above, inner, outer, jac_axial, jac_radial, jac_swirl, out,
):
    lanes = adj.shape[2]
    half = modes // 2
    rad = where[1]
    lane = lax.broadcasted_iota(jnp.int32, (chunk, lanes), 1)
    row = lax.broadcasted_iota(jnp.int32, (chunk, lanes), 0)
    radius = 0.5 + ((rad * lanes + lane).astype(jnp.float32) + 0.5) / jnp.float32(2.0 * rad_total)
    swirl = 0.25 / radius
    has_inner = jnp.where((lane == 0) & (rad == 0), 0.0, 0.5)
    has_outer = jnp.where((lane == lanes - 1) & (rad == rad_size - 1), 0.0, 0.5)

    def step(i, carry):
        order = (where[0] * half + i * chunk + row).astype(jnp.float32) / jnp.float32(mode_total // 2)
        rate = swirl * order
        for p in range(2):
            halo = pl.ds(2 * i * chunk + p, chunk, stride=2)
            for x in range(cells_ax):
                def at(e, parity, cell):
                    start = (2 * i * chunk + parity) * cells_ax + cell
                    return adj[e, pl.ds(start, chunk, stride=2 * cells_ax), :]

                here = pl.ds((2 * i * chunk + p) * cells_ax + x, chunk, stride=2 * cells_ax)
                total = [None] * fields
                for e in range(fields):
                    centre = at(e, p, x)
                    low = below[e, halo, :] if x == 0 else at(e, p, x - 1)
                    high = above[e, halo, :] if x == cells_ax - 1 else at(e, p, x + 1)
                    axial = 0.5 * (high - low)
                    from_inner = jnp.where(lane == lanes - 1, inner[e, here, :], centre)
                    from_outer = jnp.where(lane == 0, outer[e, here, :], centre)
                    radial = has_outer * pltpu.roll(from_outer, lanes - 1, 1) - has_inner * pltpu.roll(
                        from_inner, 1, 1
                    )
                    turned = (rate if p == 0 else -rate) * at(e, 1 - p, x)
                    for f in range(fields):
                        term = (
                            jac_axial[e, f] * axial
                            + jac_radial[e, f] * radial
                            + jac_swirl[e, f] * turned
                        )
                        if f == e:
                            term = term + centre
                        total[f] = term if e == 0 else total[f] + term
                for f in range(fields):
                    out[f, here, :] = total[f]
        return carry

    lax.fori_loop(0, half // chunk, step, 0)


def whole(shape):
    return pl.BlockSpec(shape, lambda i, where: (0,) * len(shape))


def stepped(shape):
    return pl.BlockSpec((1, *shape[1:]), lambda i, where: (i,) + (0,) * (len(shape) - 1))


def chosen(shape):
    return pl.BlockSpec((1, *shape[1:]), lambda i, where: (where[0],) + (0,) * (len(shape) - 1))


SMEM = pl.BlockSpec(memory_space=pltpu.SMEM)


def call(kernel, steps, where, args, in_specs, outs, out_specs, scratch, flops):
    moved = sum(a.size * a.dtype.itemsize for a in args) + sum(o.size * o.dtype.itemsize for o in outs)
    return pl.pallas_call(
        kernel,
        grid_spec=pltpu.PrefetchScalarGridSpec(
            num_scalar_prefetch=1,
            grid=(steps,),
            in_specs=in_specs,
            out_specs=out_specs,
            scratch_shapes=scratch,
        ),
        out_shape=outs,
        compiler_params=pltpu.CompilerParams(vmem_limit_bytes=VMEM_LIMIT),
        cost_estimate=pl.CostEstimate(flops=flops, bytes_accessed=moved, transcendentals=0),
    )(where, *args)


def body(adjoint, state, wake, jac_axial, jac_radial, jac_swirl, wake_coupling):
    fields, modes, cells_ax, lanes = adjoint.shape
    groups = lax.axis_size("mode")
    count = groups * modes
    rad_size = lax.axis_size("rad")
    ax_size = lax.axis_size("ax")
    width = 2 if cells_ax % 2 == 0 else 1
    steps = cells_ax // width
    rows = modes * cells_ax
    cols = width * fields * lanes
    f32 = jnp.float32

    def cols_of(j, f):
        return pl.ds((j * fields + f) * lanes, lanes)

    dims = (fields, modes, cells_ax, width, cols_of)
    own_table, other_table, back_table = tables(groups, modes)
    where = jnp.stack([lax.axis_index("mode"), lax.axis_index("rad")]).astype(jnp.int32)

    adj = adjoint.reshape(fields, rows, lanes)
    st = state.reshape(fields, rows, lanes)
    wk = wake.reshape(rows, lanes)

    def fetch(value, s):
        return lax.ppermute(value, "mode", [((i + s) % groups, i) for i in range(groups)])

    def deliver(value, s):
        return lax.ppermute(value, "mode", [(i, (i + s) % groups) for i in range(groups)])

    adj_recv = [fetch(adj, s) for s in range(1, groups)]

    up = [(i, i + 1) for i in range(ax_size - 1)]
    down = [(i + 1, i) for i in range(ax_size - 1)]
    below = lax.ppermute(adjoint[:, :, cells_ax - 1, :], "ax", up)
    above = lax.ppermute(adjoint[:, :, 0, :], "ax", down)
    if rad_size == 2:
        inner = outer = lax.ppermute(adj, "rad", [(0, 1), (1, 0)])
    else:
        inner = lax.ppermute(adj, "rad", [(i, i + 1) for i in range(rad_size - 1)])
        outer = lax.ppermute(adj, "rad", [(i + 1, i) for i in range(rad_size - 1)])
    wake_recv = [fetch(wk, s) for s in range(1, groups)]

    field_shape = (fields, rows, lanes)
    angle_shape = (steps, count, cols)
    angle = jax.ShapeDtypeStruct(angle_shape, f32)
    field = jax.ShapeDtypeStruct(field_shape, f32)
    plane = jax.ShapeDtypeStruct((rows, lanes), f32)
    own_flops = 2 * 2 * 3 * count * modes * steps * cols

    a_own, c_own = call(
        functools.partial(own_kernel, dims), steps, where,
        (adj, st, wake_coupling, own_table),
        [whole(field_shape), whole(field_shape), SMEM, chosen(own_table.shape)],
        [angle, angle],
        [stepped(angle_shape), stepped(angle_shape)],
        [pltpu.VMEM((3 * modes, cols), jnp.bfloat16)] * 2,
        own_flops,
    )

    chunk = 16 if modes % 32 == 0 else 8
    base = call(
        functools.partial(
            base_kernel, fields, modes, cells_ax, chunk, count, lanes * rad_size, rad_size
        ),
        1, where,
        (adj, below, above, inner, outer, jac_axial, jac_radial, jac_swirl),
        [whole(field_shape), whole(below.shape), whole(above.shape)]
        + [whole(field_shape)] * 2 + [SMEM] * 3,
        [field], [whole(field_shape)], [],
        32 * fields * fields * rows * lanes,
    )[0]

    joined = call(
        functools.partial(join_kernel, dims, groups), steps, where,
        (*adj_recv, a_own, c_own, other_table),
        [whole(field_shape)] * (groups - 1)
        + [stepped(angle_shape), stepped(angle_shape), chosen(other_table.shape)],
        [angle] + [plane] * groups,
        [stepped(angle_shape)] + [whole((rows, lanes))] * groups,
        [pltpu.VMEM((3 * modes, cols), jnp.bfloat16)],
        (groups - 1) * own_flops // 2,
    )
    a_all, parts = joined[0], joined[1:]
    part_recv = [deliver(parts[s], s) for s in range(1, groups)]

    adjoint_in = call(
        functools.partial(back_kernel, dims, groups), steps, where,
        (wk, *wake_recv, a_all, base, wake_coupling, back_table),
        [whole((rows, lanes))] * groups
        + [stepped(angle_shape), whole(field_shape), SMEM, chosen(back_table.shape)],
        [field], [whole(field_shape)],
        [pltpu.VMEM((3 * count, cols), jnp.bfloat16)],
        own_flops // 2,
    )[0]

    total = parts[0]
    for part in part_recv:
        total = total + part
    return (
        adjoint_in.reshape(adjoint.shape),
        (-total).reshape(wake.shape),
    )


def solution(mesh):
    return jax.shard_map(
        body,
        mesh=mesh,
        in_specs=(
            P(None, "mode", "ax", "rad"),
            P(None, "mode", "ax", "rad"),
            P("mode", "ax", "rad"),
            P(),
            P(),
            P(),
            P(),
        ),
        out_specs=(P(None, "mode", "ax", "rad"), P("mode", "ax", "rad")),
        check_vma=False,
    )
```

time: 147 us -> 47.6 us (0.32)
  matrix products: 38.1 us -> 0 us
  local copies, waits for them, and re-layouts: 36.1 us -> 5.57 us
  starting transfers between devices: 31.8 us -> 10.5 us
  Pallas kernels: 0 us -> 13.8 us
  other arithmetic: 13.9 us -> 0.82 us
  waiting for transfers between devices: 24.5 us -> 15.9 us
    dot_general x8 -> x0, matrix products: 38.1 us -> none  [the longest x1 6.37 us: body(): jnp.einsum('ef,ekxr->fkxr', wake_coupling, back_field, precision=exact_prec)]
    all_to_all x5 -> x0, waiting for transfers between devices: 24.5 us -> none  [the longest x1 17.6 us: body(): lax.all_to_all(flat_adj, ('mode', 'rad'), split_axis=2, concat_axis=1, ti...]
    all_to_all x5 -> x0, starting transfers between devices: 21.2 us -> none  [the longest x1 4.63 us: body(): lax.all_to_all(flat_cpl, ('mode', 'rad'), split_axis=2, concat_axis=1, ti...]
    ppermute x4 -> x6, waiting for transfers between devices: 0.01 us -> 15.9 us  [the longest x2 15.9 us: fetch(): lax.ppermute(value, 'mode', [((i + s) % groups, i) for i in range(groups)])]
    pallas_call x0 -> x4, Pallas kernels: none -> 13.8 us  [call(): pl.pallas_call(kernel, grid_spec=pltpu.PrefetchScalarGridSpec(num_scalar_...]
    unnamed x34 -> x20, local copies, waits for them, and re-layouts: 11 us -> 2.35 us
    reshape x3 -> x0, local copies, waits for them, and re-layouts: 7.98 us -> none  [the longest x1 3.13 us: body(): flat_cpl = coupled.reshape(fields, modes_here, points)]
    mul x4 -> x0, other arithmetic: 7.04 us -> none  [the longest x1 2.73 us: body(): axial_diff = 0.5 * (padded[:, :, 2:, 1:-1] - padded[:, :, :-2, 1:-1])]
  transfers between devices with their start and end apart: 9 -> 6, of which waited for: 2 -> 1; matrix products, arithmetic and copies ran while one was open for 48% -> 7% of each run, Pallas kernels for 0% -> 29%
where the time goes in v1:
time: 47.6 us; the launch traced here: 47.3 us
  waiting for transfers between devices  15.9 us (33%)
  Pallas kernels  13.8 us (29%)
  starting transfers between devices  10.5 us (22%)
  local copies, waits for them, and re-layouts  5.57 us (12%)
  other arithmetic  0.82 us (2%)
  between operations  0.77 us (2%)
    ppermute x2, waiting for transfers between devices, fetch(): lax.ppermute(value, 'mode', [((i + s) % groups, i) for i in range(groups)])  15.9 us
    pallas_call x4, Pallas kernels, call(): pl.pallas_call(kernel, grid_spec=pltpu.PrefetchScalarGridSpec(num_scalar_...  13.8 us
    ppermute x2, starting transfers between devices, fetch(): lax.ppermute(value, 'mode', [((i + s) % groups, i) for i in range(groups)])  3.6 us
    ppermute x1, starting transfers between devices, body(): below = lax.ppermute(adjoint[:, :, cells_ax - 1, :], 'ax', up)  3.43 us
    slice x1, local copies, waits for them, and re-layouts, body(): above = lax.ppermute(adjoint[:, :, 0, :], 'ax', down)  3.22 us
    unnamed x20, local copies, waits for them, and re-layouts  2.35 us
    ppermute x1, starting transfers between devices, deliver(): lax.ppermute(value, 'mode', [(i, (i + s) % groups) for i in range(groups)])  2.12 us
    ppermute x1, starting transfers between devices, body(): above = lax.ppermute(adjoint[:, :, 0, :], 'ax', down)  1.29 us
  transfers between devices with their start and end apart: 6, of which 1 were waited for; matrix products, arithmetic and copies ran while one was open for 7% of the time, Pallas kernels for 29%

profile of v1, /device:TPU:0, one launch (start us, length us, event | category | flops | bytes accessed | tf_op | source)
XLA Modules:
  0.0 47.3 jit_solution(4201258705628745479)
XLA Ops:
  0.6 0.0 copy-start
  0.6 0.0 copy-start.7
  0.6 3.0 %collective-permute-start.1 = (f32[5,512,128]{2,1,0:T(8,128)}, f32[5,512,128]{2,1,0:T(8,128)}, u32[]{:S(2)}, u32[]{:S(2)}) collective-permute-start(f32[5,512,128]{2,1,0:T(8,128)} %bitcast.13), channel_id=1, source_target_pairs={{16,0},{0,16},{17,1},{1,17},{18,2},{2,18},{19,3},{3,19},{20,4},{4,... | collective-permute-start | bytes 3932168 | tf_op jit(solution)/shard_map/ppermute | solution.py:236
  3.7 0.0 collective-permute-start.4
  3.7 3.2 %fusion = (f32[5,128,1,128]{3,2,1,0:T(1,128)}, f32[5,128,1,128]{3,2,1,0:T(1,128)}) fusion(f32[5,128,4,128]{3,2,1,0:T(4,128)} %param.10), kind=kLoop, calls=%fused_computation.2 | loop fusion | bytes 1310720 | tf_op jit(solution)/shard_map/slice | solution.py:246
  6.9 3.4 %collective-permute-start.2 = (f32[5,128,128]{2,1,0:T(8,128)}, f32[5,128,128]{2,1,0:T(8,128)S(1)}, u32[]{:S(2)}, u32[]{:S(2)}) collective-permute-start(f32[5,128,128]{2,1,0:T(8,128)} %bitcast.5), channel_id=1, source_target_pairs={{0,2},{2,4},{4,6},{6,8},{8,10},{10,12},{12,14},{1,3},{3,5},{5,7},{... | collective-permute-start | bytes 983048 | tf_op jit(solution)/shard_map/ppermute | solution.py:245
  10.3 1.3 %collective-permute-start.3 = (f32[5,128,128]{2,1,0:T(8,128)}, f32[5,128,128]{2,1,0:T(8,128)S(1)}, u32[]{:S(2)}, u32[]{:S(2)}) collective-permute-start(f32[5,128,128]{2,1,0:T(8,128)} %bitcast.6), channel_id=1, source_target_pairs={{2,0},{4,2},{6,4},{8,6},{10,8},{12,10},{14,12},{3,1},{5,3},{7,5},{... | collective-permute-start | bytes 983048 | tf_op jit(solution)/shard_map/ppermute | solution.py:246
  11.6 0.6 %collective-permute-start = (f32[512,128]{1,0:T(8,128)}, f32[512,128]{1,0:T(8,128)S(1)}, u32[]{:S(2)}, u32[]{:S(2)}) collective-permute-start(f32[512,128]{1,0:T(8,128)} %bitcast.17), channel_id=1, source_target_pairs={{16,0},{0,16},{17,1},{1,17},{18,2},{2,18},{19,3},{3,19},{20,4},{4,... | collective-permute-start | bytes 786440 | tf_op jit(solution)/shard_map/ppermute | solution.py:236
  12.2 0.1 pad_add_fusion.where
  12.3 0.0 copy-done
  12.3 0.0 copy-done.7
  12.3 0.0 copy-start.8
  12.3 1.3 %copy-done.8 = f32[5,128,4,128]{3,2,1,0:T(4,128)S(1)} copy-done((f32[5,128,4,128]{3,2,1,0:T(4,128)S(1)}, f32[5,128,4,128]{3,2,1,0:T(4,128)}, u32[]{:S(2)}) %copy-start.8) | copy-done | bytes 1310744
  13.6 0.0 copy-start.9
  13.6 1.0 %copy-done.9 = bf16[2,256,384]{2,1,0:T(8,128)(2,1)S(1)} copy-done((bf16[2,256,384]{2,1,0:T(8,128)(2,1)S(1)}, bf16[2,256,384]{2,1,0:T(8,128)(2,1)}, u32[]{:S(2)}) %copy-start.9) | copy-done | bytes 393240
  14.6 0.0 copy-start.2
  14.6 3.1 %shard_map.113 = (f32[2,256,1280]{2,1,0:T(8,128)S(1)}, f32[2,256,1280]{2,1,0:T(8,128)S(1)}) custom-call(s32[2]{0:T(128)S(1)} %pad_add_fusion.where, f32[5,512,128]{2,1,0:T(8,128)S(1)} %bitcast.15, f32[5,512,128]{2,1,0:T(8,128)S(1)} %bitcast.19, f32[5,5]{1,0:T(8,128)S(1)} %copy-done.7, bf16[2,256,384]{2,1,0:T(8,128)(2,1)S(1)} %copy-done.9), custom_call_target="tpu_custom_call" | custom-call | flops 1006632960 | bytes 8257636 | tf_op jit(solution)/shard_map/pallas_call | solution.py:197
  17.7 15.9 %collective-permute-done.1.refs_0_ = f32[5,512,128]{2,1,0:T(8,128)} collective-permute-done((f32[5,512,128]{2,1,0:T(8,128)}, f32[5,512,128]{2,1,0:T(8,128)}, u32[]{:S(2)}, u32[]{:S(2)}) %collective-permute-start.1) | collective-permute-done | bytes 1310752 | tf_op jit(solution)/shard_map/ppermute | solution.py:236
  33.6 0.0 copy-done.2
  33.6 0.0 copy-start.4
  33.6 0.0 copy-start.5
  33.6 0.0 copy-start.6
  33.6 3.0 %shard_map.114 = (f32[2,256,1280]{2,1,0:T(8,128)S(1)}, f32[512,128]{1,0:T(8,128)S(1)}, f32[512,128]{1,0:T(8,128)S(1)}) custom-call(s32[2]{0:T(128)S(1)} %pad_add_fusion.where, f32[5,512,128]{2,1,0:T(8,128)} %collective-permute-done.1.refs_0_, f32[2,256,1280]{2,1,0:T(8,128)S(1)} %get-tuple-element.7.refs_1_, f32[2,256,1280]{2,1,0:T(8,128)S(1)} %get-tuple-element.8.refs_2_, ...), custom_call_target="tpu_custom_call" | custom-call | flops 503316480 | bytes 10092544 | tf_op jit(solution)/shard_map/pallas_call | solution.py:197
  36.6 0.0 copy-start.1
  36.6 0.0 copy-start.3
  36.6 2.1 %collective-permute-start.5 = (f32[512,128]{1,0:T(8,128)S(1)}, f32[512,128]{1,0:T(8,128)S(1)}, u32[]{:S(2)}, u32[]{:S(2)}) collective-permute-start(f32[512,128]{1,0:T(8,128)S(1)} %get-tuple-element.11), channel_id=1, source_target_pairs={{0,16},{16,0},{1,17},{17,1},{2,18},{18,2},{3,19},{19,3},{4,20},{20... | collective-permute-start | bytes 786440 | tf_op jit(solution)/shard_map/ppermute | solution.py:239
  38.8 0.0 collective-permute-done.2.below
  38.8 0.0 collective-permute-done.3.above
  38.8 0.0 collective-permute-done.4.inner.outer
  38.8 0.0 copy-done.4
  38.8 0.0 copy-done.5
  38.8 0.0 copy-done.6
  38.8 3.8 %shard_map.115.refs_3_ = f32[5,512,128]{2,1,0:T(8,128)S(1)} custom-call(s32[2]{0:T(128)S(1)} %pad_add_fusion.where, f32[5,512,128]{2,1,0:T(8,128)S(1)} %bitcast.16, f32[5,128,128]{2,1,0:T(8,128)S(1)} %collective-permute-done.2.below, f32[5,128,128]{2,1,0:T(8,128)S(1)} %collective-permute-done.3.above, f32[5,512,128]{2,1,0:T(8,128)S(1)} %collective-permute-done.4.inner.outer, ...), custom_call_target="tpu_custom_call" | custom-call | flops 52428800 | bytes 5898540 | tf_op jit(solution)/shard_map/pallas_call | solution.py:197
  42.7 0.0 collective-permute-done.refs_1_
  42.7 0.0 copy-done.1
  42.7 0.0 copy-done.3
  42.7 3.9 %shard_map.116 = f32[5,512,128]{2,1,0:T(8,128)} custom-call(s32[2]{0:T(128)S(1)} %pad_add_fusion.where, f32[512,128]{1,0:T(8,128)S(1)} %bitcast.18, f32[512,128]{1,0:T(8,128)S(1)} %collective-permute-done.refs_1_, f32[2,256,1280]{2,1,0:T(8,128)S(1)} %get-tuple-element.9.refs_2_, f32[5,512,128]{2,1,0:T(8,128)S(1)} %shard_map.115.refs_3_, ...), custom_call_target="tpu_custom_call" | custom-call | flops 503316480 | bytes 6160484 | tf_op jit(solution)/shard_map/pallas_call | solution.py:197
  46.5 0.0 collective-permute-done.5
  46.5 0.7 %add_negate_fusion = f32[512,128]{1,0:T(8,128)} fusion(f32[512,128]{1,0:T(8,128)S(1)} %get-tuple-element.10, f32[512,128]{1,0:T(8,128)S(1)} %collective-permute-done.5), kind=kLoop, calls=%fused_computation | loop fusion | flops 131072 | bytes 786432 | tf_op jit(solution)/shard_map/neg | solution.py:312
Async XLA Ops:
  0.6 11.7 %copy-start = (f32[5,128,4,128]{3,2,1,0:T(4,128)S(1)}, f32[5,128,4,128]{3,2,1,0:T(4,128)}, u32[]{:S(2)}) copy-start(f32[5,128,4,128]{3,2,1,0:T(4,128)} %param.10) | copy-start | bytes 3932164
  0.6 11.7 %copy-start.7 = (f32[5,5]{1,0:T(8,128)S(1)}, f32[5,5]{1,0:T(8,128)}, u32[]{:S(2)}) copy-start(f32[5,5]{1,0:T(8,128)} %refs_4_.1) | copy-start | bytes 304
  0.6 32.9 %collective-permute-start.1 = (f32[5,512,128]{2,1,0:T(8,128)}, f32[5,512,128]{2,1,0:T(8,128)}, u32[]{:S(2)}, u32[]{:S(2)}) collective-permute-start(f32[5,512,128]{2,1,0:T(8,128)} %bitcast.13), channel_id=1, source_target_pairs={{16,0},{0,16},{17,1},{1,17},{18,2},{2,18},{19,3},{3,19},{20,4},{4,... | collective-permute-start | bytes 3932168 | tf_op jit(solution)/shard_map/ppermute | solution.py:236
  3.7 35.1 %collective-permute-start.4 = (f32[5,512,128]{2,1,0:T(8,128)}, f32[5,512,128]{2,1,0:T(8,128)S(1)}, u32[]{:S(2)}, u32[]{:S(2)}) collective-permute-start(f32[5,512,128]{2,1,0:T(8,128)} %bitcast.14), channel_id=1, source_target_pairs={{0,1},{1,0},{2,3},{3,2},{4,5},{5,4},{6,7},{7,6},{8,9},{9,8},{10,11... | collective-permute-start | bytes 3932168 | tf_op jit(solution)/shard_map/ppermute | solution.py:248
  6.9 31.9 %collective-permute-start.2 = (f32[5,128,128]{2,1,0:T(8,128)}, f32[5,128,128]{2,1,0:T(8,128)S(1)}, u32[]{:S(2)}, u32[]{:S(2)}) collective-permute-start(f32[5,128,128]{2,1,0:T(8,128)} %bitcast.5), channel_id=1, source_target_pairs={{0,2},{2,4},{4,6},{6,8},{8,10},{10,12},{12,14},{1,3},{3,5},{5,7},{... | collective-permute-start | bytes 983048 | tf_op jit(solution)/shard_map/ppermute | solution.py:245
  10.3 28.5 %collective-permute-start.3 = (f32[5,128,128]{2,1,0:T(8,128)}, f32[5,128,128]{2,1,0:T(8,128)S(1)}, u32[]{:S(2)}, u32[]{:S(2)}) collective-permute-start(f32[5,128,128]{2,1,0:T(8,128)} %bitcast.6), channel_id=1, source_target_pairs={{2,0},{4,2},{6,4},{8,6},{10,8},{12,10},{14,12},{3,1},{5,3},{7,5},{... | collective-permute-start | bytes 983048 | tf_op jit(solution)/shard_map/ppermute | solution.py:246
  11.6 31.0 %collective-permute-start = (f32[512,128]{1,0:T(8,128)}, f32[512,128]{1,0:T(8,128)S(1)}, u32[]{:S(2)}, u32[]{:S(2)}) collective-permute-start(f32[512,128]{1,0:T(8,128)} %bitcast.17), channel_id=1, source_target_pairs={{16,0},{0,16},{17,1},{1,17},{18,2},{2,18},{19,3},{3,19},{20,4},{4,... | collective-permute-start | bytes 786440 | tf_op jit(solution)/shard_map/ppermute | solution.py:236
  12.3 1.3 %copy-start.8 = (f32[5,128,4,128]{3,2,1,0:T(4,128)S(1)}, f32[5,128,4,128]{3,2,1,0:T(4,128)}, u32[]{:S(2)}) copy-start(f32[5,128,4,128]{3,2,1,0:T(4,128)} %param.11) | copy-start | bytes 3932164
  13.6 1.0 %copy-start.9 = (bf16[2,256,384]{2,1,0:T(8,128)(2,1)S(1)}, bf16[2,256,384]{2,1,0:T(8,128)(2,1)}, u32[]{:S(2)}) copy-start(bf16[2,256,384]{2,1,0:T(8,128)(2,1)} %constant.14.clone.table) | copy-start | bytes 1179652
  14.6 19.0 %copy-start.2 = (bf16[2,1,256,384]{3,2,1,0:T(8,128)(2,1)S(1)}, bf16[2,1,256,384]{3,2,1,0:T(8,128)(2,1)}, u32[]{:S(2)}) copy-start(bf16[2,1,256,384]{3,2,1,0:T(8,128)(2,1)} %constant.15.clone.refs_3_) | copy-start | bytes 1179652
  33.6 5.2 %copy-start.4 = (f32[5,5]{1,0:T(8,128)S(1)}, f32[5,5]{1,0:T(8,128)}, u32[]{:S(2)}) copy-start(f32[5,5]{1,0:T(8,128)} %jac_axial.1) | copy-start | bytes 304
  33.6 5.2 %copy-start.5 = (f32[5,5]{1,0:T(8,128)S(1)}, f32[5,5]{1,0:T(8,128)}, u32[]{:S(2)}) copy-start(f32[5,5]{1,0:T(8,128)} %jac_radial.1) | copy-start | bytes 304
  33.6 5.2 %copy-start.6 = (f32[5,5]{1,0:T(8,128)S(1)}, f32[5,5]{1,0:T(8,128)}, u32[]{:S(2)}) copy-start(f32[5,5]{1,0:T(8,128)} %jac_swirl.1) | copy-start | bytes 304
  36.6 6.1 %copy-start.1 = (bf16[2,128,768]{2,1,0:T(8,128)(2,1)S(1)}, bf16[2,128,768]{2,1,0:T(8,128)(2,1)}, u32[]{:S(2)}) copy-start(bf16[2,128,768]{2,1,0:T(8,128)(2,1)} %constant.16.clone.refs_5_) | copy-start | bytes 1179652
  36.6 6.1 %copy-start.3 = (f32[128,4,128]{2,1,0:T(4,128)S(1)}, f32[128,4,128]{2,1,0:T(4,128)}, u32[]{:S(2)}) copy-start(f32[128,4,128]{2,1,0:T(4,128)} %param.12) | copy-start | bytes 786436
  36.6 9.9 %collective-permute-start.5 = (f32[512,128]{1,0:T(8,128)S(1)}, f32[512,128]{1,0:T(8,128)S(1)}, u32[]{:S(2)}, u32[]{:S(2)}) collective-permute-start(f32[512,128]{1,0:T(8,128)S(1)} %get-tuple-element.11), channel_id=1, source_target_pairs={{0,16},{16,0},{1,17},{17,1},{2,18},{18,2},{3,19},{19,3},{4,20},{20... | collective-permute-start | bytes 786440 | tf_op jit(solution)/shard_map/ppermute | solution.py:239

commit v2 on v1

--- a/solution.py
+++ b/solution.py
@@ -77,9 +77,9 @@
 def join_kernel(dims, groups, where, *refs):
     fields, modes, cells_ax, width, cols_of = dims
     recv = refs[: groups - 1]
-    a_own, c_own, table, a_out = refs[groups - 1 : groups + 3]
-    h_out = refs[groups + 3 : 2 * groups + 3]
-    terms = refs[2 * groups + 3]
+    a_own, c_own, table, _, a_out = refs[groups - 1 : groups + 4]
+    h_out = refs[groups + 4 : 2 * groups + 4]
+    terms = refs[2 * groups + 4]
     total = a_own[0]
     for s in range(groups - 1):
         for j in range(width):
@@ -190,6 +190,7 @@
 
 
 SMEM = pl.BlockSpec(memory_space=pltpu.SMEM)
+ANY = pl.BlockSpec(memory_space=pl.ANY)
 
 
 def call(kernel, steps, where, args, in_specs, outs, out_specs, scratch, flops):
@@ -283,9 +284,9 @@
 
     joined = call(
         functools.partial(join_kernel, dims, groups), steps, where,
-        (*adj_recv, a_own, c_own, other_table),
+        (*adj_recv, a_own, c_own, other_table, base),
         [whole(field_shape)] * (groups - 1)
-        + [stepped(angle_shape), stepped(angle_shape), chosen(other_table.shape)],
+        + [stepped(angle_shape), stepped(angle_shape), chosen(other_table.shape), ANY],
         [angle] + [plane] * groups,
         [stepped(angle_shape)] + [whole((rows, lanes))] * groups,
         [pltpu.VMEM((3 * modes, cols), jnp.bfloat16)],

time: 47.6 us -> 45.6 us (0.958)
  waiting for transfers between devices: 15.9 us -> 13.9 us
    ppermute x2, waiting for transfers between devices: 15.9 us -> 5.02 us  [fetch(): lax.ppermute(value, 'mode', [((i + s) % groups, i) for i in range(groups)])]
    ppermute x1, waiting for transfers between devices: 0.01 us -> 7.15 us  [body(): below = lax.ppermute(adjoint[:, :, cells_ax - 1, :], 'ax', up)]
    ppermute x1, waiting for transfers between devices: 0.01 us -> 1.77 us  [deliver(): lax.ppermute(value, 'mode', [(i, (i + s) % groups) for i in range(groups)])]
    ppermute x1, starting transfers between devices: 0.01 us -> 0.52 us  [body(): inner = outer = lax.ppermute(adj, 'rad', [(0, 1), (1, 0)])]
  transfers between devices with their start and end apart: 6 -> 6, of which waited for: 1 -> 4; matrix products, arithmetic and copies ran while one was open for 7% -> 7% of each run, Pallas kernels for 29% -> 31%
where the time goes in v2:
time: 45.6 us; the launch traced here: 45.3 us
  waiting for transfers between devices  13.9 us (30%)
  Pallas kernels  13.8 us (30%)
  starting transfers between devices  10.4 us (23%)
  local copies, waits for them, and re-layouts  5.56 us (12%)
  other arithmetic  0.81 us (2%)
  between operations  0.73 us (2%)
    pallas_call x4, Pallas kernels, call(): pl.pallas_call(kernel, grid_spec=pltpu.PrefetchScalarGridSpec(num_scalar_...  13.8 us
    ppermute x1, waiting for transfers between devices, body(): below = lax.ppermute(adjoint[:, :, cells_ax - 1, :], 'ax', up)  7.15 us
    ppermute x2, waiting for transfers between devices, fetch(): lax.ppermute(value, 'mode', [((i + s) % groups, i) for i in range(groups)])  5.02 us
    ppermute x1, starting transfers between devices, body(): below = lax.ppermute(adjoint[:, :, cells_ax - 1, :], 'ax', up)  3.43 us
    slice x1, local copies, waits for them, and re-layouts, body(): above = lax.ppermute(adjoint[:, :, 0, :], 'ax', down)  3.22 us
    ppermute x2, starting transfers between devices, fetch(): lax.ppermute(value, 'mode', [((i + s) % groups, i) for i in range(groups)])  3.16 us
    unnamed x20, local copies, waits for them, and re-layouts  2.35 us
    ppermute x1, starting transfers between devices, deliver(): lax.ppermute(value, 'mode', [(i, (i + s) % groups) for i in range(groups)])  2.02 us
  transfers between devices with their start and end apart: 6, of which 4 were waited for; matrix products, arithmetic and copies ran while one was open for 7% of the time, Pallas kernels for 31%

profile of v2, /device:TPU:0, one launch (start us, length us, event | category | flops | bytes accessed | tf_op | source)
XLA Modules:
  0.0 45.3 jit_solution(13602373592644476839)
XLA Ops:
  0.6 0.0 copy-start
  0.6 0.0 copy-start.7
  0.6 0.5 %collective-permute-start.4 = (f32[5,512,128]{2,1,0:T(8,128)}, f32[5,512,128]{2,1,0:T(8,128)S(1)}, u32[]{:S(2)}, u32[]{:S(2)}) collective-permute-start(f32[5,512,128]{2,1,0:T(8,128)} %bitcast.13), channel_id=1, source_target_pairs={{0,1},{1,0},{2,3},{3,2},{4,5},{5,4},{6,7},{7,6},{8,9},{9,8},{10,11... | collective-permute-start | bytes 3932168 | tf_op jit(solution)/shard_map/ppermute | solution.py:249
  1.2 2.6 %collective-permute-start.1 = (f32[5,512,128]{2,1,0:T(8,128)}, f32[5,512,128]{2,1,0:T(8,128)}, u32[]{:S(2)}, u32[]{:S(2)}) collective-permute-start(f32[5,512,128]{2,1,0:T(8,128)} %bitcast.14), channel_id=1, source_target_pairs={{16,0},{0,16},{17,1},{1,17},{18,2},{2,18},{19,3},{3,19},{20,4},{4,... | collective-permute-start | bytes 3932168 | tf_op jit(solution)/shard_map/ppermute | solution.py:237
  3.7 3.2 %fusion = (f32[5,128,1,128]{3,2,1,0:T(1,128)}, f32[5,128,1,128]{3,2,1,0:T(1,128)}) fusion(f32[5,128,4,128]{3,2,1,0:T(4,128)} %param.10), kind=kLoop, calls=%fused_computation.2 | loop fusion | bytes 1310720 | tf_op jit(solution)/shard_map/slice | solution.py:247
  6.9 3.4 %collective-permute-start.2 = (f32[5,128,128]{2,1,0:T(8,128)}, f32[5,128,128]{2,1,0:T(8,128)S(1)}, u32[]{:S(2)}, u32[]{:S(2)}) collective-permute-start(f32[5,128,128]{2,1,0:T(8,128)} %bitcast.5), channel_id=1, source_target_pairs={{0,2},{2,4},{4,6},{6,8},{8,10},{10,12},{12,14},{1,3},{3,5},{5,7},{... | collective-permute-start | bytes 983048 | tf_op jit(solution)/shard_map/ppermute | solution.py:246
  10.4 1.3 %collective-permute-start.3 = (f32[5,128,128]{2,1,0:T(8,128)}, f32[5,128,128]{2,1,0:T(8,128)S(1)}, u32[]{:S(2)}, u32[]{:S(2)}) collective-permute-start(f32[5,128,128]{2,1,0:T(8,128)} %bitcast.6), channel_id=1, source_target_pairs={{2,0},{4,2},{6,4},{8,6},{10,8},{12,10},{14,12},{3,1},{5,3},{7,5},{... | collective-permute-start | bytes 983048 | tf_op jit(solution)/shard_map/ppermute | solution.py:247
  11.7 0.6 %collective-permute-start = (f32[512,128]{1,0:T(8,128)}, f32[512,128]{1,0:T(8,128)S(1)}, u32[]{:S(2)}, u32[]{:S(2)}) collective-permute-start(f32[512,128]{1,0:T(8,128)} %bitcast.17), channel_id=1, source_target_pairs={{16,0},{0,16},{17,1},{1,17},{18,2},{2,18},{19,3},{3,19},{20,4},{4,... | collective-permute-start | bytes 786440 | tf_op jit(solution)/shard_map/ppermute | solution.py:237
  12.3 0.1 pad_add_fusion.where
  12.4 0.0 copy-done
  12.4 0.0 copy-done.7
  12.4 0.0 copy-start.8
  12.4 1.3 %copy-done.8 = f32[5,128,4,128]{3,2,1,0:T(4,128)S(1)} copy-done((f32[5,128,4,128]{3,2,1,0:T(4,128)S(1)}, f32[5,128,4,128]{3,2,1,0:T(4,128)}, u32[]{:S(2)}) %copy-start.8) | copy-done | bytes 1310744
  13.7 0.0 copy-start.9
  13.7 1.0 %copy-done.9 = bf16[2,256,384]{2,1,0:T(8,128)(2,1)S(1)} copy-done((bf16[2,256,384]{2,1,0:T(8,128)(2,1)S(1)}, bf16[2,256,384]{2,1,0:T(8,128)(2,1)}, u32[]{:S(2)}) %copy-start.9) | copy-done | bytes 393240
  14.7 0.0 copy-start.4
  14.7 0.0 copy-start.5
  14.7 0.0 copy-start.6
  14.7 3.1 %shard_map.113 = (f32[2,256,1280]{2,1,0:T(8,128)S(1)}, f32[2,256,1280]{2,1,0:T(8,128)S(1)}) custom-call(s32[2]{0:T(128)S(1)} %pad_add_fusion.where, f32[5,512,128]{2,1,0:T(8,128)S(1)} %bitcast.15, f32[5,512,128]{2,1,0:T(8,128)S(1)} %bitcast.19, f32[5,5]{1,0:T(8,128)S(1)} %copy-done.7, bf16[2,256,384]{2,1,0:T(8,128)(2,1)S(1)} %copy-done.9), custom_call_target="tpu_custom_call" | custom-call | flops 1006632960 | bytes 8257636 | tf_op jit(solution)/shard_map/pallas_call | solution.py:198
  17.8 0.0 copy-start.1
  17.8 7.2 %collective-permute-done.2.below = f32[5,128,128]{2,1,0:T(8,128)S(1)} collective-permute-done((f32[5,128,128]{2,1,0:T(8,128)}, f32[5,128,128]{2,1,0:T(8,128)S(1)}, u32[]{:S(2)}, u32[]{:S(2)}) %collective-permute-start.2) | collective-permute-done | bytes 327712 | tf_op jit(solution)/shard_map/ppermute | solution.py:246
  25.0 0.0 collective-permute-done.3.above
  25.0 0.0 collective-permute-done.4.inner.outer
  25.0 0.0 copy-done.4
  25.0 0.0 copy-done.5
  25.0 0.0 copy-done.6
  25.0 3.8 %shard_map.114.refs_4_.refs_3_ = f32[5,512,128]{2,1,0:T(8,128)S(1)} custom-call(s32[2]{0:T(128)S(1)} %pad_add_fusion.where, f32[5,512,128]{2,1,0:T(8,128)S(1)} %bitcast.16, f32[5,128,128]{2,1,0:T(8,128)S(1)} %collective-permute-done.2.below, f32[5,128,128]{2,1,0:T(8,128)S(1)} %collective-permute-done.3.above, ...), custom_call_target="tpu_custom_call" | custom-call | flops 52428800 | bytes 5898540 | tf_op jit(solution)/shard_map/pallas_call | solution.py:198
  28.9 4.8 %collective-permute-done.1.refs_0_ = f32[5,512,128]{2,1,0:T(8,128)} collective-permute-done((f32[5,512,128]{2,1,0:T(8,128)}, f32[5,512,128]{2,1,0:T(8,128)}, u32[]{:S(2)}, u32[]{:S(2)}) %collective-permute-start.1) | collective-permute-done | bytes 1310752 | tf_op jit(solution)/shard_map/ppermute | solution.py:237
  33.7 0.0 copy-done.1
  33.7 0.0 copy-start.2
  33.7 0.0 copy-start.3
  33.7 3.0 %shard_map.115 = (f32[2,256,1280]{2,1,0:T(8,128)S(1)}, f32[512,128]{1,0:T(8,128)S(1)}, f32[512,128]{1,0:T(8,128)S(1)}) custom-call(s32[2]{0:T(128)S(1)} %pad_add_fusion.where, f32[5,512,128]{2,1,0:T(8,128)} %collective-permute-done.1.refs_0_, f32[2,256,1280]{2,1,0:T(8,128)S(1)} %get-tuple-element.7.refs_1_, f32[2,256,1280]{2,1,0:T(8,128)S(1)} %get-tuple-element.8.refs_2_, ...), custom_call_target="tpu_custom_call" | custom-call | flops 503316480 | bytes 11403264 | tf_op jit(solution)/shard_map/pallas_call | solution.py:198
  36.7 2.0 %collective-permute-start.5 = (f32[512,128]{1,0:T(8,128)S(1)}, f32[512,128]{1,0:T(8,128)S(1)}, u32[]{:S(2)}, u32[]{:S(2)}) collective-permute-start(f32[512,128]{1,0:T(8,128)S(1)} %get-tuple-element.11), channel_id=1, source_target_pairs={{0,16},{16,0},{1,17},{17,1},{2,18},{18,2},{3,19},{19,3},{4,20},{20... | collective-permute-start | bytes 786440 | tf_op jit(solution)/shard_map/ppermute | solution.py:240
  38.7 0.2 collective-permute-done.refs_1_
  38.9 0.0 copy-done.2
  38.9 0.0 copy-done.3
  38.9 3.9 %shard_map.116 = f32[5,512,128]{2,1,0:T(8,128)} custom-call(s32[2]{0:T(128)S(1)} %pad_add_fusion.where, f32[512,128]{1,0:T(8,128)S(1)} %bitcast.18, f32[512,128]{1,0:T(8,128)S(1)} %collective-permute-done.refs_1_, f32[2,256,1280]{2,1,0:T(8,128)S(1)} %get-tuple-element.9.refs_2_, f32[5,512,128]{2,1,0:T(8,128)S(1)} %shard_map.114.refs_4_.refs_3_, ...), custom_call_target="tpu_custom_call" | custom-call | flops 503316480 | bytes 6160484 | tf_op jit(solution)/shard_map/pallas_call | solution.py:198
  42.8 1.8 %collective-permute-done.5 = f32[512,128]{1,0:T(8,128)S(1)} collective-permute-done((f32[512,128]{1,0:T(8,128)S(1)}, f32[512,128]{1,0:T(8,128)S(1)}, u32[]{:S(2)}, u32[]{:S(2)}) %collective-permute-start.5) | collective-permute-done | bytes 262176 | tf_op jit(solution)/shard_map/ppermute | solution.py:240
  44.6 0.7 %add_negate_fusion = f32[512,128]{1,0:T(8,128)} fusion(f32[512,128]{1,0:T(8,128)S(1)} %get-tuple-element.10, f32[512,128]{1,0:T(8,128)S(1)} %collective-permute-done.5), kind=kLoop, calls=%fused_computation | loop fusion | flops 131072 | bytes 786432 | tf_op jit(solution)/shard_map/neg | solution.py:313
Async XLA Ops:
  0.6 11.7 %copy-start = (f32[5,128,4,128]{3,2,1,0:T(4,128)S(1)}, f32[5,128,4,128]{3,2,1,0:T(4,128)}, u32[]{:S(2)}) copy-start(f32[5,128,4,128]{3,2,1,0:T(4,128)} %param.10) | copy-start | bytes 3932164
  0.6 11.7 %copy-start.7 = (f32[5,5]{1,0:T(8,128)S(1)}, f32[5,5]{1,0:T(8,128)}, u32[]{:S(2)}) copy-start(f32[5,5]{1,0:T(8,128)} %refs_4_.1) | copy-start | bytes 304
  0.6 24.3 %collective-permute-start.4 = (f32[5,512,128]{2,1,0:T(8,128)}, f32[5,512,128]{2,1,0:T(8,128)S(1)}, u32[]{:S(2)}, u32[]{:S(2)}) collective-permute-start(f32[5,512,128]{2,1,0:T(8,128)} %bitcast.13), channel_id=1, source_target_pairs={{0,1},{1,0},{2,3},{3,2},{4,5},{5,4},{6,7},{7,6},{8,9},{9,8},{10,11... | collective-permute-start | bytes 3932168 | tf_op jit(solution)/shard_map/ppermute | solution.py:249
  1.2 32.5 %collective-permute-start.1 = (f32[5,512,128]{2,1,0:T(8,128)}, f32[5,512,128]{2,1,0:T(8,128)}, u32[]{:S(2)}, u32[]{:S(2)}) collective-permute-start(f32[5,512,128]{2,1,0:T(8,128)} %bitcast.14), channel_id=1, source_target_pairs={{16,0},{0,16},{17,1},{1,17},{18,2},{2,18},{19,3},{3,19},{20,4},{4,... | collective-permute-start | bytes 3932168 | tf_op jit(solution)/shard_map/ppermute | solution.py:237
  6.9 18.0 %collective-permute-start.2 = (f32[5,128,128]{2,1,0:T(8,128)}, f32[5,128,128]{2,1,0:T(8,128)S(1)}, u32[]{:S(2)}, u32[]{:S(2)}) collective-permute-start(f32[5,128,128]{2,1,0:T(8,128)} %bitcast.5), channel_id=1, source_target_pairs={{0,2},{2,4},{4,6},{6,8},{8,10},{10,12},{12,14},{1,3},{3,5},{5,7},{... | collective-permute-start | bytes 983048 | tf_op jit(solution)/shard_map/ppermute | solution.py:246
  10.4 14.6 %collective-permute-start.3 = (f32[5,128,128]{2,1,0:T(8,128)}, f32[5,128,128]{2,1,0:T(8,128)S(1)}, u32[]{:S(2)}, u32[]{:S(2)}) collective-permute-start(f32[5,128,128]{2,1,0:T(8,128)} %bitcast.6), channel_id=1, source_target_pairs={{2,0},{4,2},{6,4},{8,6},{10,8},{12,10},{14,12},{3,1},{5,3},{7,5},{... | collective-permute-start | bytes 983048 | tf_op jit(solution)/shard_map/ppermute | solution.py:247
  11.7 27.2 %collective-permute-start = (f32[512,128]{1,0:T(8,128)}, f32[512,128]{1,0:T(8,128)S(1)}, u32[]{:S(2)}, u32[]{:S(2)}) collective-permute-start(f32[512,128]{1,0:T(8,128)} %bitcast.17), channel_id=1, source_target_pairs={{16,0},{0,16},{17,1},{1,17},{18,2},{2,18},{19,3},{3,19},{20,4},{4,... | collective-permute-start | bytes 786440 | tf_op jit(solution)/shard_map/ppermute | solution.py:237
  12.4 1.3 %copy-start.8 = (f32[5,128,4,128]{3,2,1,0:T(4,128)S(1)}, f32[5,128,4,128]{3,2,1,0:T(4,128)}, u32[]{:S(2)}) copy-start(f32[5,128,4,128]{3,2,1,0:T(4,128)} %param.11) | copy-start | bytes 3932164
  13.7 1.0 %copy-start.9 = (bf16[2,256,384]{2,1,0:T(8,128)(2,1)S(1)}, bf16[2,256,384]{2,1,0:T(8,128)(2,1)}, u32[]{:S(2)}) copy-start(bf16[2,256,384]{2,1,0:T(8,128)(2,1)} %constant.14.clone.table) | copy-start | bytes 1179652
  14.7 10.3 %copy-start.4 = (f32[5,5]{1,0:T(8,128)S(1)}, f32[5,5]{1,0:T(8,128)}, u32[]{:S(2)}) copy-start(f32[5,5]{1,0:T(8,128)} %jac_axial.1) | copy-start | bytes 304
  14.7 10.3 %copy-start.5 = (f32[5,5]{1,0:T(8,128)S(1)}, f32[5,5]{1,0:T(8,128)}, u32[]{:S(2)}) copy-start(f32[5,5]{1,0:T(8,128)} %jac_radial.1) | copy-start | bytes 304
  14.7 10.3 %copy-start.6 = (f32[5,5]{1,0:T(8,128)S(1)}, f32[5,5]{1,0:T(8,128)}, u32[]{:S(2)}) copy-start(f32[5,5]{1,0:T(8,128)} %jac_swirl.1) | copy-start | bytes 304
  17.8 15.9 %copy-start.1 = (bf16[2,1,256,384]{3,2,1,0:T(8,128)(2,1)S(1)}, bf16[2,1,256,384]{3,2,1,0:T(8,128)(2,1)}, u32[]{:S(2)}) copy-start(bf16[2,1,256,384]{3,2,1,0:T(8,128)(2,1)} %constant.15.clone.refs_3_) | copy-start | bytes 1179652
  33.7 5.3 %copy-start.2 = (bf16[2,128,768]{2,1,0:T(8,128)(2,1)S(1)}, bf16[2,128,768]{2,1,0:T(8,128)(2,1)}, u32[]{:S(2)}) copy-start(bf16[2,128,768]{2,1,0:T(8,128)(2,1)} %constant.16.clone.refs_5_) | copy-start | bytes 1179652
  33.7 5.3 %copy-start.3 = (f32[128,4,128]{2,1,0:T(4,128)S(1)}, f32[128,4,128]{2,1,0:T(4,128)}, u32[]{:S(2)}) copy-start(f32[128,4,128]{2,1,0:T(4,128)} %param.12) | copy-start | bytes 786436
  36.7 7.9 %collective-permute-start.5 = (f32[512,128]{1,0:T(8,128)S(1)}, f32[512,128]{1,0:T(8,128)S(1)}, u32[]{:S(2)}, u32[]{:S(2)}) collective-permute-start(f32[512,128]{1,0:T(8,128)S(1)} %get-tuple-element.11), channel_id=1, source_target_pairs={{0,16},{16,0},{1,17},{17,1},{2,18},{18,2},{3,19},{19,3},{4,20},{20... | collective-permute-start | bytes 786440 | tf_op jit(solution)/shard_map/ppermute | solution.py:240

commit v3 on v2

--- a/solution.py
+++ b/solution.py
@@ -53,6 +53,25 @@
     terms[pl.ds(row, rows), cols] = high
     terms[pl.ds(total + row, rows), cols] = high
     terms[pl.ds(2 * total + row, rows), cols] = low
+
+
+def pack_kernel(fields, modes, cells_ax, adj, first, last, edges):
+    lanes = adj.shape[2]
+    lane = lax.broadcasted_iota(jnp.int32, (modes, lanes), 1)
+    packed = jnp.zeros((modes, lanes), jnp.float32)
+    for f in range(fields):
+        for x in range(cells_ax):
+            block = adj[f, pl.ds(x, modes, stride=cells_ax), :]
+            if x == 0:
+                first[f] = block
+            if x == cells_ax - 1:
+                last[f] = block
+            j = f * cells_ax + x
+            packed = jnp.where(lane == j, pltpu.roll(block, j, 1), packed)
+            packed = jnp.where(
+                lane == lanes // 2 + j, pltpu.roll(block, (j + 1 + lanes // 2) % lanes, 1), packed
+            )
+    edges[...] = packed
 
 
 def own_kernel(dims, where, adj, state, coupling, table, a_out, c_out, terms_a, terms_c):
@@ -143,6 +162,7 @@
         rate = swirl * order
         for p in range(2):
             halo = pl.ds(2 * i * chunk + p, chunk, stride=2)
+            inner_edges, outer_edges = inner[halo, :], outer[halo, :]
             for x in range(cells_ax):
                 def at(e, parity, cell):
                     start = (2 * i * chunk + parity) * cells_ax + cell
@@ -155,8 +175,13 @@
                     low = below[e, halo, :] if x == 0 else at(e, p, x - 1)
                     high = above[e, halo, :] if x == cells_ax - 1 else at(e, p, x + 1)
                     axial = 0.5 * (high - low)
-                    from_inner = jnp.where(lane == lanes - 1, inner[e, here, :], centre)
-                    from_outer = jnp.where(lane == 0, outer[e, here, :], centre)
+                    j = e * cells_ax + x
+                    from_inner = jnp.where(
+                        lane == lanes - 1, pltpu.roll(inner_edges, lanes // 2 - 1 - j, 1), centre
+                    )
+                    from_outer = jnp.where(
+                        lane == 0, pltpu.roll(outer_edges, (lanes - j) % lanes, 1), centre
+                    )
                     radial = has_outer * pltpu.roll(from_outer, lanes - 1, 1) - has_inner * pltpu.roll(
                         from_inner, 1, 1
                     )
@@ -243,13 +268,19 @@
 
     up = [(i, i + 1) for i in range(ax_size - 1)]
     down = [(i + 1, i) for i in range(ax_size - 1)]
-    below = lax.ppermute(adjoint[:, :, cells_ax - 1, :], "ax", up)
-    above = lax.ppermute(adjoint[:, :, 0, :], "ax", down)
+    layer = jax.ShapeDtypeStruct((fields, modes, lanes), adjoint.dtype)
+    first, last, edges = pl.pallas_call(
+        functools.partial(pack_kernel, fields, modes, cells_ax),
+        out_shape=[layer, layer, jax.ShapeDtypeStruct((modes, lanes), adjoint.dtype)],
+        compiler_params=pltpu.CompilerParams(vmem_limit_bytes=VMEM_LIMIT),
+    )(adj)
+    below = lax.ppermute(last, "ax", up)
+    above = lax.ppermute(first, "ax", down)
     if rad_size == 2:
-        inner = outer = lax.ppermute(adj, "rad", [(0, 1), (1, 0)])
+        inner = outer = lax.ppermute(edges, "rad", [(0, 1), (1, 0)])
     else:
-        inner = lax.ppermute(adj, "rad", [(i, i + 1) for i in range(rad_size - 1)])
-        outer = lax.ppermute(adj, "rad", [(i + 1, i) for i in range(rad_size - 1)])
+        inner = lax.ppermute(edges, "rad", [(i, i + 1) for i in range(rad_size - 1)])
+        outer = lax.ppermute(edges, "rad", [(i + 1, i) for i in range(rad_size - 1)])
     wake_recv = [fetch(wk, s) for s in range(1, groups)]
 
     field_shape = (fields, rows, lanes)
@@ -277,7 +308,7 @@
         1, where,
         (adj, below, above, inner, outer, jac_axial, jac_radial, jac_swirl),
         [whole(field_shape), whole(below.shape), whole(above.shape)]
-        + [whole(field_shape)] * 2 + [SMEM] * 3,
+        + [whole(edges.shape)] * 2 + [SMEM] * 3,
         [field], [whole(field_shape)], [],
         32 * fields * fields * rows * lanes,
     )[0]

time: 45.6 us -> 44.9 us (0.985)
  Pallas kernels: 13.8 us -> 19.5 us
  waiting for transfers between devices: 13.9 us -> 9.37 us
  local copies, waits for them, and re-layouts: 5.56 us -> 3.69 us
    pallas_call x4, Pallas kernels: 13.8 us -> 18.1 us  [call(): pl.pallas_call(kernel, grid_spec=pltpu.PrefetchScalarGridSpec(num_scalar_...]
    slice x1 -> x0, local copies, waits for them, and re-layouts: 3.22 us -> none  [body(): above = lax.ppermute(adjoint[:, :, 0, :], 'ax', down)]
    ppermute x2, waiting for transfers between devices: 5.02 us -> 1.99 us  [fetch(): lax.ppermute(value, 'mode', [((i + s) % groups, i) for i in range(groups)])]
    pallas_call x0 -> x1, Pallas kernels: none -> 1.38 us  [body(): pl.pallas_call(functools.partial(pack_kernel, fields, modes, cells_ax), o...]
    unnamed x20 -> x22, local copies, waits for them, and re-layouts: 2.35 us -> 3.69 us
    ppermute x1, waiting for transfers between devices: 1.77 us -> 0.92 us  [deliver(): lax.ppermute(value, 'mode', [(i, (i + s) % groups) for i in range(groups)])]
    ppermute x3, waiting for transfers between devices: 7.16 us -> 6.46 us  [the longest x1 6.45 us: body(): below = lax.ppermute(last, 'ax', up)]
  transfers between devices with their start and end apart: 6 -> 6, of which waited for: 4 -> 4; matrix products, arithmetic and copies ran while one was open for 7% -> 0% of each run, Pallas kernels for 31% -> 44%
where the time goes in v3:
time: 44.9 us; the launch traced here: 44.6 us
  Pallas kernels  19.5 us (43%)
  starting transfers between devices  10.5 us (23%)
  waiting for transfers between devices  9.37 us (21%)
  local copies, waits for them, and re-layouts  3.69 us (8%)
  other arithmetic  0.81 us (2%)
  between operations  0.71 us (2%)
    pallas_call x4, Pallas kernels, call(): pl.pallas_call(kernel, grid_spec=pltpu.PrefetchScalarGridSpec(num_scalar_...  18.1 us
    ppermute x1, waiting for transfers between devices, body(): below = lax.ppermute(last, 'ax', up)  6.45 us
    unnamed x22, local copies, waits for them, and re-layouts  3.69 us
    ppermute x2, starting transfers between devices, fetch(): lax.ppermute(value, 'mode', [((i + s) % groups, i) for i in range(groups)])  3.6 us
    ppermute x1, starting transfers between devices, body(): below = lax.ppermute(last, 'ax', up)  3.43 us
    ppermute x1, starting transfers between devices, deliver(): lax.ppermute(value, 'mode', [(i, (i + s) % groups) for i in range(groups)])  2.12 us
    ppermute x2, waiting for transfers between devices, fetch(): lax.ppermute(value, 'mode', [((i + s) % groups, i) for i in range(groups)])  1.99 us
    pallas_call x1, Pallas kernels, body(): pl.pallas_call(functools.partial(pack_kernel, fields, modes, cells_ax), o...  1.38 us
  transfers between devices with their start and end apart: 6, of which 4 were waited for; matrix products, arithmetic and copies ran while one was open for 0% of the time, Pallas kernels for 44%

profile of v3, /device:TPU:0, one launch (start us, length us, event | category | flops | bytes accessed | tf_op | source)
XLA Modules:
  0.0 44.6 jit_solution(5285107703495695370)
XLA Ops:
  0.6 3.0 %collective-permute-start.1 = (f32[5,512,128]{2,1,0:T(8,128)}, f32[5,512,128]{2,1,0:T(8,128)S(1)}, u32[]{:S(2)}, u32[]{:S(2)}) collective-permute-start(f32[5,512,128]{2,1,0:T(8,128)} %bitcast.7), channel_id=1, source_target_pairs={{16,0},{0,16},{17,1},{1,17},{18,2},{2,18},{19,3},{3,19},{20,4},{4,... | collective-permute-start | bytes 3932168 | tf_op jit(solution)/shard_map/ppermute | solution.py:262
  3.6 0.0 copy-start
  3.6 1.3 %copy-done = f32[5,128,4,128]{3,2,1,0:T(4,128)S(1)} copy-done((f32[5,128,4,128]{3,2,1,0:T(4,128)S(1)}, f32[5,128,4,128]{3,2,1,0:T(4,128)}, u32[]{:S(2)}) %copy-start) | copy-done | bytes 1310744
  5.0 0.0 copy-start.1
  5.0 0.0 copy-start.8
  5.0 1.4 %shard_map.114 = (f32[5,128,128]{2,1,0:T(8,128)}, f32[5,128,128]{2,1,0:T(8,128)}, f32[128,128]{1,0:T(8,128)}) custom-call(f32[5,512,128]{2,1,0:T(8,128)S(1)} %bitcast.8), custom_call_target="tpu_custom_call" | custom-call | tf_op jit(solution)/shard_map/pallas_call | solution.py:272
  6.4 3.4 %collective-permute-start.2 = (f32[5,128,128]{2,1,0:T(8,128)}, f32[5,128,128]{2,1,0:T(8,128)S(1)}, u32[]{:S(2)}, u32[]{:S(2)}) collective-permute-start(f32[5,128,128]{2,1,0:T(8,128)} %get-tuple-element.12), channel_id=1, source_target_pairs={{0,2},{2,4},{4,6},{6,8},{8,10},{10,12},{12,14},{1,3},{3,5},{5,7},{... | collective-permute-start | bytes 983048 | tf_op jit(solution)/shard_map/ppermute | solution.py:277
  9.8 1.3 %collective-permute-start.3 = (f32[5,128,128]{2,1,0:T(8,128)}, f32[5,128,128]{2,1,0:T(8,128)S(1)}, u32[]{:S(2)}, u32[]{:S(2)}) collective-permute-start(f32[5,128,128]{2,1,0:T(8,128)} %get-tuple-element.13), channel_id=1, source_target_pairs={{2,0},{4,2},{6,4},{8,6},{10,8},{12,10},{14,12},{3,1},{5,3},{7,5},{... | collective-permute-start | bytes 983048 | tf_op jit(solution)/shard_map/ppermute | solution.py:278
  11.1 0.1 collective-permute-start.4
  11.2 0.6 %collective-permute-start = (f32[512,128]{1,0:T(8,128)}, f32[512,128]{1,0:T(8,128)S(1)}, u32[]{:S(2)}, u32[]{:S(2)}) collective-permute-start(f32[512,128]{1,0:T(8,128)} %bitcast.11), channel_id=1, source_target_pairs={{16,0},{0,16},{17,1},{1,17},{18,2},{2,18},{19,3},{3,19},{20,4},{4,... | collective-permute-start | bytes 786440 | tf_op jit(solution)/shard_map/ppermute | solution.py:262
  11.8 0.1 pad_add_fusion.where
  11.9 0.0 copy-done.1
  11.9 0.0 copy-done.8
  11.9 0.0 copy-start.9
  11.9 1.3 %copy-done.9 = f32[5,128,4,128]{3,2,1,0:T(4,128)S(1)} copy-done((f32[5,128,4,128]{3,2,1,0:T(4,128)S(1)}, f32[5,128,4,128]{3,2,1,0:T(4,128)}, u32[]{:S(2)}) %copy-start.9) | copy-done | bytes 1310744
  13.2 0.0 copy-start.10
  13.2 1.0 %copy-done.10 = bf16[2,256,384]{2,1,0:T(8,128)(2,1)S(1)} copy-done((bf16[2,256,384]{2,1,0:T(8,128)(2,1)S(1)}, bf16[2,256,384]{2,1,0:T(8,128)(2,1)}, u32[]{:S(2)}) %copy-start.10) | copy-done | bytes 393240
  14.2 0.0 copy-start.5
  14.2 0.0 copy-start.6
  14.2 0.0 copy-start.7
  14.2 3.1 %shard_map.113 = (f32[2,256,1280]{2,1,0:T(8,128)S(1)}, f32[2,256,1280]{2,1,0:T(8,128)S(1)}) custom-call(s32[2]{0:T(128)S(1)} %pad_add_fusion.where, f32[5,512,128]{2,1,0:T(8,128)S(1)} %bitcast.9, f32[5,512,128]{2,1,0:T(8,128)S(1)} %bitcast.13, f32[5,5]{1,0:T(8,128)S(1)} %copy-done.8, bf16[2,256,384]{2,1,0:T(8,128)(2,1)S(1)} %copy-done.10), custom_call_target="tpu_custom_call" | custom-call | flops 1006632960 | bytes 8257636 | tf_op jit(solution)/shard_map/pallas_call | solution.py:223
  17.3 0.0 copy-start.2
  17.3 0.0 collective-permute-done.4.inner.outer
  17.3 6.5 %collective-permute-done.2.below = f32[5,128,128]{2,1,0:T(8,128)S(1)} collective-permute-done((f32[5,128,128]{2,1,0:T(8,128)}, f32[5,128,128]{2,1,0:T(8,128)S(1)}, u32[]{:S(2)}, u32[]{:S(2)}) %collective-permute-start.2) | collective-permute-done | bytes 327712 | tf_op jit(solution)/shard_map/ppermute | solution.py:277
  23.8 0.0 collective-permute-done.3.above
  23.8 0.0 copy-done.5
  23.8 0.0 copy-done.6
  23.8 0.0 copy-done.7
  23.8 9.4 %shard_map.115.refs_4_.refs_3_ = f32[5,512,128]{2,1,0:T(8,128)S(1)} custom-call(s32[2]{0:T(128)S(1)} %pad_add_fusion.where, f32[5,512,128]{2,1,0:T(8,128)S(1)} %bitcast.10, f32[5,128,128]{2,1,0:T(8,128)S(1)} %collective-permute-done.2.below, f32[5,128,128]{2,1,0:T(8,128)S(1)} %collective-permute-done.3.above, f32[128,128]{1,0:T(8,128)} %collective-permute-done.4.inner.outer, ...), custom_call_target="tpu_custom_call" | custom-call | flops 52428800 | bytes 3408172 | tf_op jit(solution)/shard_map/pallas_call | solution.py:223
  33.2 0.2 collective-permute-done.1.refs_0_
  33.4 0.0 copy-done.2
  33.5 0.0 copy-start.3
  33.5 0.0 copy-start.4
  33.5 1.7 %shard_map.116 = (f32[2,256,1280]{2,1,0:T(8,128)S(1)}, f32[512,128]{1,0:T(8,128)S(1)}, f32[512,128]{1,0:T(8,128)S(1)}) custom-call(s32[2]{0:T(128)S(1)} %pad_add_fusion.where, f32[5,512,128]{2,1,0:T(8,128)S(1)} %collective-permute-done.1.refs_0_, f32[2,256,1280]{2,1,0:T(8,128)S(1)} %get-tuple-element.10.refs_1_, ...), custom_call_target="tpu_custom_call" | custom-call | flops 503316480 | bytes 11403264 | tf_op jit(solution)/shard_map/pallas_call | solution.py:223
  35.2 2.1 %collective-permute-start.5 = (f32[512,128]{1,0:T(8,128)S(1)}, f32[512,128]{1,0:T(8,128)S(1)}, u32[]{:S(2)}, u32[]{:S(2)}) collective-permute-start(f32[512,128]{1,0:T(8,128)S(1)} %get-tuple-element.17), channel_id=1, source_target_pairs={{0,16},{16,0},{1,17},{17,1},{2,18},{18,2},{3,19},{19,3},{4,20},{20... | collective-permute-start | bytes 786440 | tf_op jit(solution)/shard_map/ppermute | solution.py:265
  37.3 1.8 %collective-permute-done.refs_1_ = f32[512,128]{1,0:T(8,128)S(1)} collective-permute-done((f32[512,128]{1,0:T(8,128)}, f32[512,128]{1,0:T(8,128)S(1)}, u32[]{:S(2)}, u32[]{:S(2)}) %collective-permute-start) | collective-permute-done | bytes 262176 | tf_op jit(solution)/shard_map/ppermute | solution.py:262
  39.1 0.0 copy-done.3
  39.1 0.0 copy-done.4
  39.1 3.9 %shard_map.117 = f32[5,512,128]{2,1,0:T(8,128)} custom-call(s32[2]{0:T(128)S(1)} %pad_add_fusion.where, f32[512,128]{1,0:T(8,128)S(1)} %bitcast.12, f32[512,128]{1,0:T(8,128)S(1)} %collective-permute-done.refs_1_, f32[2,256,1280]{2,1,0:T(8,128)S(1)} %get-tuple-element.15.refs_2_, f32[5,512,128]{2,1,0:T(8,128)S(1)} %shard_map.115.refs_4_.refs_3_, ...), custom_call_target="tpu_custom_call" | custom-call | flops 503316480 | bytes 6160484 | tf_op jit(solution)/shard_map/pallas_call | solution.py:223
  42.9 0.9 %collective-permute-done.5 = f32[512,128]{1,0:T(8,128)S(1)} collective-permute-done((f32[512,128]{1,0:T(8,128)S(1)}, f32[512,128]{1,0:T(8,128)S(1)}, u32[]{:S(2)}, u32[]{:S(2)}) %collective-permute-start.5) | collective-permute-done | bytes 262176 | tf_op jit(solution)/shard_map/ppermute | solution.py:265
  43.9 0.7 %add_negate_fusion = f32[512,128]{1,0:T(8,128)} fusion(f32[512,128]{1,0:T(8,128)S(1)} %get-tuple-element.16, f32[512,128]{1,0:T(8,128)S(1)} %collective-permute-done.5), kind=kLoop, calls=%fused_computation | loop fusion | flops 131072 | bytes 786432 | tf_op jit(solution)/shard_map/neg | solution.py:344
Async XLA Ops:
  0.6 32.8 %collective-permute-start.1 = (f32[5,512,128]{2,1,0:T(8,128)}, f32[5,512,128]{2,1,0:T(8,128)S(1)}, u32[]{:S(2)}, u32[]{:S(2)}) collective-permute-start(f32[5,512,128]{2,1,0:T(8,128)} %bitcast.7), channel_id=1, source_target_pairs={{16,0},{0,16},{17,1},{1,17},{18,2},{2,18},{19,3},{3,19},{20,4},{4,... | collective-permute-start | bytes 3932168 | tf_op jit(solution)/shard_map/ppermute | solution.py:262
  3.6 1.4 %copy-start = (f32[5,128,4,128]{3,2,1,0:T(4,128)S(1)}, f32[5,128,4,128]{3,2,1,0:T(4,128)}, u32[]{:S(2)}) copy-start(f32[5,128,4,128]{3,2,1,0:T(4,128)} %param.10) | copy-start | bytes 3932164
  5.0 6.9 %copy-start.1 = (f32[5,128,4,128]{3,2,1,0:T(4,128)S(1)}, f32[5,128,4,128]{3,2,1,0:T(4,128)}, u32[]{:S(2)}) copy-start(f32[5,128,4,128]{3,2,1,0:T(4,128)} %param.10) | copy-start | bytes 3932164
  5.0 6.9 %copy-start.8 = (f32[5,5]{1,0:T(8,128)S(1)}, f32[5,5]{1,0:T(8,128)}, u32[]{:S(2)}) copy-start(f32[5,5]{1,0:T(8,128)} %refs_4_.1) | copy-start | bytes 304
  6.4 17.4 %collective-permute-start.2 = (f32[5,128,128]{2,1,0:T(8,128)}, f32[5,128,128]{2,1,0:T(8,128)S(1)}, u32[]{:S(2)}, u32[]{:S(2)}) collective-permute-start(f32[5,128,128]{2,1,0:T(8,128)} %get-tuple-element.12), channel_id=1, source_target_pairs={{0,2},{2,4},{4,6},{6,8},{8,10},{10,12},{12,14},{1,3},{3,5},{5,7},{... | collective-permute-start | bytes 983048 | tf_op jit(solution)/shard_map/ppermute | solution.py:277
  9.8 14.0 %collective-permute-start.3 = (f32[5,128,128]{2,1,0:T(8,128)}, f32[5,128,128]{2,1,0:T(8,128)S(1)}, u32[]{:S(2)}, u32[]{:S(2)}) collective-permute-start(f32[5,128,128]{2,1,0:T(8,128)} %get-tuple-element.13), channel_id=1, source_target_pairs={{2,0},{4,2},{6,4},{8,6},{10,8},{12,10},{14,12},{3,1},{5,3},{7,5},{... | collective-permute-start | bytes 983048 | tf_op jit(solution)/shard_map/ppermute | solution.py:278
  11.1 6.2 %collective-permute-start.4 = (f32[128,128]{1,0:T(8,128)}, f32[128,128]{1,0:T(8,128)}, u32[]{:S(2)}, u32[]{:S(2)}) collective-permute-start(f32[128,128]{1,0:T(8,128)} %get-tuple-element.14), channel_id=1, source_target_pairs={{0,1},{1,0},{2,3},{3,2},{4,5},{5,4},{6,7},{7,6},{8,9},{9,8},{10,11... | collective-permute-start | bytes 196616 | tf_op jit(solution)/shard_map/ppermute | solution.py:280
  11.2 27.9 %collective-permute-start = (f32[512,128]{1,0:T(8,128)}, f32[512,128]{1,0:T(8,128)S(1)}, u32[]{:S(2)}, u32[]{:S(2)}) collective-permute-start(f32[512,128]{1,0:T(8,128)} %bitcast.11), channel_id=1, source_target_pairs={{16,0},{0,16},{17,1},{1,17},{18,2},{2,18},{19,3},{3,19},{20,4},{4,... | collective-permute-start | bytes 786440 | tf_op jit(solution)/shard_map/ppermute | solution.py:262
  11.9 1.3 %copy-start.9 = (f32[5,128,4,128]{3,2,1,0:T(4,128)S(1)}, f32[5,128,4,128]{3,2,1,0:T(4,128)}, u32[]{:S(2)}) copy-start(f32[5,128,4,128]{3,2,1,0:T(4,128)} %param.11) | copy-start | bytes 3932164
  13.2 1.0 %copy-start.10 = (bf16[2,256,384]{2,1,0:T(8,128)(2,1)S(1)}, bf16[2,256,384]{2,1,0:T(8,128)(2,1)}, u32[]{:S(2)}) copy-start(bf16[2,256,384]{2,1,0:T(8,128)(2,1)} %constant.14.clone.table) | copy-start | bytes 1179652
  14.2 9.6 %copy-start.5 = (f32[5,5]{1,0:T(8,128)S(1)}, f32[5,5]{1,0:T(8,128)}, u32[]{:S(2)}) copy-start(f32[5,5]{1,0:T(8,128)} %jac_axial.1) | copy-start | bytes 304
  14.2 9.6 %copy-start.6 = (f32[5,5]{1,0:T(8,128)S(1)}, f32[5,5]{1,0:T(8,128)}, u32[]{:S(2)}) copy-start(f32[5,5]{1,0:T(8,128)} %jac_radial.1) | copy-start | bytes 304
  14.2 9.6 %copy-start.7 = (f32[5,5]{1,0:T(8,128)S(1)}, f32[5,5]{1,0:T(8,128)}, u32[]{:S(2)}) copy-start(f32[5,5]{1,0:T(8,128)} %jac_swirl.1) | copy-start | bytes 304
  17.3 16.1 %copy-start.2 = (bf16[2,1,256,384]{3,2,1,0:T(8,128)(2,1)S(1)}, bf16[2,1,256,384]{3,2,1,0:T(8,128)(2,1)}, u32[]{:S(2)}) copy-start(bf16[2,1,256,384]{3,2,1,0:T(8,128)(2,1)} %constant.15.clone.refs_3_) | copy-start | bytes 1179652
  33.5 5.6 %copy-start.3 = (bf16[2,128,768]{2,1,0:T(8,128)(2,1)S(1)}, bf16[2,128,768]{2,1,0:T(8,128)(2,1)}, u32[]{:S(2)}) copy-start(bf16[2,128,768]{2,1,0:T(8,128)(2,1)} %constant.16.clone.refs_5_) | copy-start | bytes 1179652
  33.5 5.6 %copy-start.4 = (f32[128,4,128]{2,1,0:T(4,128)S(1)}, f32[128,4,128]{2,1,0:T(4,128)}, u32[]{:S(2)}) copy-start(f32[128,4,128]{2,1,0:T(4,128)} %param.12) | copy-start | bytes 786436
  35.2 8.7 %collective-permute-start.5 = (f32[512,128]{1,0:T(8,128)S(1)}, f32[512,128]{1,0:T(8,128)S(1)}, u32[]{:S(2)}, u32[]{:S(2)}) collective-permute-start(f32[512,128]{1,0:T(8,128)S(1)} %get-tuple-element.17), channel_id=1, source_target_pairs={{0,16},{16,0},{1,17},{17,1},{2,18},{18,2},{3,19},{19,3},{4,20},{20... | collective-permute-start | bytes 786440 | tf_op jit(solution)/shard_map/ppermute | solution.py:265

commit v4 on v3

--- a/solution.py
+++ b/solution.py
@@ -93,12 +93,13 @@
     c_out[0] = jnp.dot(table[0], terms_c[...], preferred_element_type=jnp.float32)
 
 
-def join_kernel(dims, groups, where, *refs):
+def join_kernel(dims, groups, cuts, where, *refs):
     fields, modes, cells_ax, width, cols_of = dims
+    pieces = len(cuts) - 1
     recv = refs[: groups - 1]
     a_own, c_own, table, _, a_out = refs[groups - 1 : groups + 4]
-    h_out = refs[groups + 4 : 2 * groups + 4]
-    terms = refs[2 * groups + 4]
+    h_out = refs[groups + 4 : -1]
+    terms = refs[-1]
     total = a_own[0]
     for s in range(groups - 1):
         for j in range(width):
@@ -110,13 +111,20 @@
     a_out[0] = total
     for j in range(width):
         x = pl.program_id(0) * width + j
-        rows = pl.ds(x, modes, stride=cells_ax)
-        for s in range(groups):
-            here = pl.ds(s * modes, modes)
+        for s, k in ((s, k) for s in range(groups) for k in range(pieces)):
+            here = pl.ds(s * modes + cuts[k], cuts[k + 1] - cuts[k])
+            rows = pl.ds(x, cuts[k + 1] - cuts[k], stride=cells_ax)
             part = a_out[0, here, cols_of(j, 0)] * c_own[0, here, cols_of(j, 0)]
             for f in range(1, fields):
                 part = part + a_out[0, here, cols_of(j, f)] * c_own[0, here, cols_of(j, f)]
-            h_out[s][rows, :] = part
+            h_out[s * pieces + k][rows, :] = part
+
+
+def total_kernel(terms, *refs):
+    total = refs[0][...]
+    for ref in refs[1:terms]:
+        total = total + ref[...]
+    refs[-1][...] = -total
 
 
 def back_kernel(dims, groups, where, *refs):
@@ -313,18 +321,22 @@
         32 * fields * fields * rows * lanes,
     )[0]
 
+    cuts = (0, max(modes * 3 // 4 // 8 * 8, modes // 2), modes)
+    pieces = len(cuts) - 1
+    piece_rows = [(cuts[k + 1] - cuts[k]) * cells_ax for k in range(pieces)]
     joined = call(
-        functools.partial(join_kernel, dims, groups), steps, where,
+        functools.partial(join_kernel, dims, groups, cuts), steps, where,
         (*adj_recv, a_own, c_own, other_table, base),
         [whole(field_shape)] * (groups - 1)
         + [stepped(angle_shape), stepped(angle_shape), chosen(other_table.shape), ANY],
-        [angle] + [plane] * groups,
-        [stepped(angle_shape)] + [whole((rows, lanes))] * groups,
+        [angle] + [jax.ShapeDtypeStruct((n, lanes), f32) for n in piece_rows] * groups,
+        [stepped(angle_shape)] + [whole((n, lanes)) for n in piece_rows] * groups,
         [pltpu.VMEM((3 * modes, cols), jnp.bfloat16)],
         (groups - 1) * own_flops // 2,
     )
-    a_all, parts = joined[0], joined[1:]
-    part_recv = [deliver(parts[s], s) for s in range(1, groups)]
+    a_all = joined[0]
+    parts = [joined[1 + k :: pieces] for k in range(pieces)]
+    arrived = [[deliver(part[s], s) for s in range(1, groups)] for part in parts]
 
     adjoint_in = call(
         functools.partial(back_kernel, dims, groups), steps, where,
@@ -336,12 +348,22 @@
         own_flops // 2,
     )[0]
 
-    total = parts[0]
-    for part in part_recv:
-        total = total + part
+    wake_grad = None
+    for k in range(pieces):
+        size, place = piece_rows[k], cuts[k] * cells_ax
+        wake_grad = pl.pallas_call(
+            functools.partial(total_kernel, groups),
+            grid=(1,),
+            out_shape=plane,
+            in_specs=[pl.BlockSpec((size, lanes), lambda i: (0, 0))] * groups
+            + ([] if wake_grad is None else [ANY]),
+            out_specs=pl.BlockSpec((size, lanes), lambda i, at=place // size: (at, 0)),
+            input_output_aliases={} if wake_grad is None else {groups: 0},
+            compiler_params=pltpu.CompilerParams(vmem_limit_bytes=VMEM_LIMIT),
+        )(parts[k][0], *arrived[k], *([] if wake_grad is None else [wake_grad]))
     return (
         adjoint_in.reshape(adjoint.shape),
-        (-total).reshape(wake.shape),
+        wake_grad.reshape(wake.shape),
     )
 
 

time: 44.9 us -> 44.8 us (level)
  Pallas kernels: 19.5 us -> 20.8 us
  waiting for transfers between devices: 9.37 us -> 8.59 us
  other arithmetic: 0.81 us -> 0.07 us
    pallas_call x0 -> x2, Pallas kernels: none -> 1.34 us  [body(): pl.pallas_call(functools.partial(total_kernel, groups), grid=(1,), out_sh...]
    neg x1 -> x0, other arithmetic: 0.73 us -> none  [body(): return (adjoint_in.reshape(adjoint.shape), (-total).reshape(wake.shape))]
    ppermute x1 -> x2, waiting for transfers between devices: 0.92 us -> 0.22 us  [deliver(): lax.ppermute(value, 'mode', [(i, (i + s) % groups) for i in range(groups)])]
    ppermute x1 -> x2, starting transfers between devices: 2.12 us -> 2.2 us  [deliver(): lax.ppermute(value, 'mode', [(i, (i + s) % groups) for i in range(groups)])]
  transfers between devices with their start and end apart: 6 -> 7, of which waited for: 4 -> 4; matrix products, arithmetic and copies ran while one was open for 0% -> 0% of each run, Pallas kernels for 44% -> 45%
where the time goes in v4:
time: 44.8 us; the launch traced here: 44.5 us
  Pallas kernels  20.8 us (46%)
  starting transfers between devices  10.6 us (24%)
  waiting for transfers between devices  8.59 us (19%)
  local copies, waits for them, and re-layouts  3.69 us (8%)
  between operations  0.71 us (2%)
    pallas_call x4, Pallas kernels, call(): pl.pallas_call(kernel, grid_spec=pltpu.PrefetchScalarGridSpec(num_scalar_...  18.1 us
    ppermute x1, waiting for transfers between devices, body(): below = lax.ppermute(last, 'ax', up)  6.45 us
    unnamed x22, local copies, waits for them, and re-layouts  3.69 us
    ppermute x2, starting transfers between devices, fetch(): lax.ppermute(value, 'mode', [((i + s) % groups, i) for i in range(groups)])  3.6 us
    ppermute x1, starting transfers between devices, body(): below = lax.ppermute(last, 'ax', up)  3.43 us
    ppermute x2, starting transfers between devices, deliver(): lax.ppermute(value, 'mode', [(i, (i + s) % groups) for i in range(groups)])  2.2 us
    ppermute x2, waiting for transfers between devices, fetch(): lax.ppermute(value, 'mode', [((i + s) % groups, i) for i in range(groups)])  1.91 us
    pallas_call x1, Pallas kernels, body(): pl.pallas_call(functools.partial(pack_kernel, fields, modes, cells_ax), o...  1.38 us
  transfers between devices with their start and end apart: 7, of which 4 were waited for; matrix products, arithmetic and copies ran while one was open for 0% of the time, Pallas kernels for 45%

profile of v4, /device:TPU:0, one launch (start us, length us, event | category | flops | bytes accessed | tf_op | source)
XLA Modules:
  0.0 44.5 jit_solution(10308121287983591346)
XLA Ops:
  0.6 3.0 %collective-permute-start.1 = (f32[5,512,128]{2,1,0:T(8,128)}, f32[5,512,128]{2,1,0:T(8,128)S(1)}, u32[]{:S(2)}, u32[]{:S(2)}) collective-permute-start(f32[5,512,128]{2,1,0:T(8,128)} %bitcast.7), channel_id=1, source_target_pairs={{16,0},{0,16},{17,1},{1,17},{18,2},{2,18},{19,3},{3,19},{20,4},{4,... | collective-permute-start | bytes 3932168 | tf_op jit(solution)/shard_map/ppermute | solution.py:270
  3.6 0.0 copy-start
  3.6 1.3 %copy-done = f32[5,128,4,128]{3,2,1,0:T(4,128)S(1)} copy-done((f32[5,128,4,128]{3,2,1,0:T(4,128)S(1)}, f32[5,128,4,128]{3,2,1,0:T(4,128)}, u32[]{:S(2)}) %copy-start) | copy-done | bytes 1310744
  5.0 0.0 copy-start.1
  5.0 0.0 copy-start.8
  5.0 1.4 %shard_map.114 = (f32[5,128,128]{2,1,0:T(8,128)}, f32[5,128,128]{2,1,0:T(8,128)}, f32[128,128]{1,0:T(8,128)}) custom-call(f32[5,512,128]{2,1,0:T(8,128)S(1)} %bitcast.8), custom_call_target="tpu_custom_call" | custom-call | tf_op jit(solution)/shard_map/pallas_call | solution.py:280
  6.4 3.4 %collective-permute-start.2 = (f32[5,128,128]{2,1,0:T(8,128)}, f32[5,128,128]{2,1,0:T(8,128)S(1)}, u32[]{:S(2)}, u32[]{:S(2)}) collective-permute-start(f32[5,128,128]{2,1,0:T(8,128)} %get-tuple-element.14), channel_id=1, source_target_pairs={{0,2},{2,4},{4,6},{6,8},{8,10},{10,12},{12,14},{1,3},{3,5},{5,7},{... | collective-permute-start | bytes 983048 | tf_op jit(solution)/shard_map/ppermute | solution.py:285
  9.8 1.3 %collective-permute-start.3 = (f32[5,128,128]{2,1,0:T(8,128)}, f32[5,128,128]{2,1,0:T(8,128)S(1)}, u32[]{:S(2)}, u32[]{:S(2)}) collective-permute-start(f32[5,128,128]{2,1,0:T(8,128)} %get-tuple-element.15), channel_id=1, source_target_pairs={{2,0},{4,2},{6,4},{8,6},{10,8},{12,10},{14,12},{3,1},{5,3},{7,5},{... | collective-permute-start | bytes 983048 | tf_op jit(solution)/shard_map/ppermute | solution.py:286
  11.1 0.1 collective-permute-start.4
  11.2 0.6 %collective-permute-start = (f32[512,128]{1,0:T(8,128)}, f32[512,128]{1,0:T(8,128)S(1)}, u32[]{:S(2)}, u32[]{:S(2)}) collective-permute-start(f32[512,128]{1,0:T(8,128)} %bitcast.11), channel_id=1, source_target_pairs={{16,0},{0,16},{17,1},{1,17},{18,2},{2,18},{19,3},{3,19},{20,4},{4,... | collective-permute-start | bytes 786440 | tf_op jit(solution)/shard_map/ppermute | solution.py:270
  11.8 0.1 pad_add_fusion.where
  11.9 0.0 copy-done.1
  11.9 0.0 copy-done.8
  11.9 0.0 copy-start.9
  11.9 1.3 %copy-done.9 = f32[5,128,4,128]{3,2,1,0:T(4,128)S(1)} copy-done((f32[5,128,4,128]{3,2,1,0:T(4,128)S(1)}, f32[5,128,4,128]{3,2,1,0:T(4,128)}, u32[]{:S(2)}) %copy-start.9) | copy-done | bytes 1310744
  13.2 0.0 copy-start.10
  13.2 1.0 %copy-done.10 = bf16[2,256,384]{2,1,0:T(8,128)(2,1)S(1)} copy-done((bf16[2,256,384]{2,1,0:T(8,128)(2,1)S(1)}, bf16[2,256,384]{2,1,0:T(8,128)(2,1)}, u32[]{:S(2)}) %copy-start.10) | copy-done | bytes 393240
  14.2 0.0 copy-start.5
  14.2 0.0 copy-start.6
  14.2 0.0 copy-start.7
  14.2 3.1 %shard_map.113 = (f32[2,256,1280]{2,1,0:T(8,128)S(1)}, f32[2,256,1280]{2,1,0:T(8,128)S(1)}) custom-call(s32[2]{0:T(128)S(1)} %pad_add_fusion.where, f32[5,512,128]{2,1,0:T(8,128)S(1)} %bitcast.9, f32[5,512,128]{2,1,0:T(8,128)S(1)} %bitcast.13, f32[5,5]{1,0:T(8,128)S(1)} %copy-done.8, bf16[2,256,384]{2,1,0:T(8,128)(2,1)S(1)} %copy-done.10), custom_call_target="tpu_custom_call" | custom-call | flops 1006632960 | bytes 8257636 | tf_op jit(solution)/shard_map/pallas_call | solution.py:231
  17.3 0.0 copy-start.2
  17.3 0.0 collective-permute-done.4.inner.outer
  17.3 6.5 %collective-permute-done.2.below = f32[5,128,128]{2,1,0:T(8,128)S(1)} collective-permute-done((f32[5,128,128]{2,1,0:T(8,128)}, f32[5,128,128]{2,1,0:T(8,128)S(1)}, u32[]{:S(2)}, u32[]{:S(2)}) %collective-permute-start.2) | collective-permute-done | bytes 327712 | tf_op jit(solution)/shard_map/ppermute | solution.py:285
  23.8 0.0 collective-permute-done.3.above
  23.8 0.0 copy-done.5
  23.8 0.0 copy-done.6
  23.8 0.0 copy-done.7
  23.8 9.4 %shard_map.115.refs_4_.refs_3_ = f32[5,512,128]{2,1,0:T(8,128)S(1)} custom-call(s32[2]{0:T(128)S(1)} %pad_add_fusion.where, f32[5,512,128]{2,1,0:T(8,128)S(1)} %bitcast.10, f32[5,128,128]{2,1,0:T(8,128)S(1)} %collective-permute-done.2.below, f32[5,128,128]{2,1,0:T(8,128)S(1)} %collective-permute-done.3.above, f32[128,128]{1,0:T(8,128)} %collective-permute-done.4.inner.outer, ...), custom_call_target="tpu_custom_call" | custom-call | flops 52428800 | bytes 3408172 | tf_op jit(solution)/shard_map/pallas_call | solution.py:231
  33.2 0.2 collective-permute-done.1.refs_0_
  33.4 0.0 copy-done.2
  33.5 0.0 copy-start.3
  33.5 0.0 copy-start.4
  33.5 1.7 %shard_map.116 = (f32[2,256,1280]{2,1,0:T(8,128)S(1)}, f32[384,128]{1,0:T(8,128)S(1)}, f32[128,128]{1,0:T(8,128)S(1)}, f32[384,128]{1,0:T(8,128)S(1)}, f32[128,128]{1,0:T(8,128)S(1)}) custom-call(s32[2]{0:T(128)S(1)} %pad_add_fusion.where, f32[5,512,128]{2,1,0:T(8,128)S(1)} %collective-permute-done.1.refs_0_, f32[2,256,1280]{2,1,0:T(8,128)S(1)} %get-tuple-element.12.refs_1_, ...), custom_call_target="tpu_custom_call" | custom-call | flops 503316480 | bytes 11403264 | tf_op jit(solution)/shard_map/pallas_call | solution.py:231
  35.2 2.1 %collective-permute-start.6 = (f32[384,128]{1,0:T(8,128)S(1)}, f32[384,128]{1,0:T(8,128)S(1)}, u32[]{:S(2)}, u32[]{:S(2)}) collective-permute-start(f32[384,128]{1,0:T(8,128)S(1)} %get-tuple-element.21), channel_id=1, source_target_pairs={{0,16},{16,0},{1,17},{17,1},{2,18},{18,2},{3,19},{19,3},{4,20},{20... | collective-permute-start | bytes 589832 | tf_op jit(solution)/shard_map/ppermute | solution.py:273
  37.3 0.1 collective-permute-start.5
  37.4 1.7 %collective-permute-done.refs_1_ = f32[512,128]{1,0:T(8,128)S(1)} collective-permute-done((f32[512,128]{1,0:T(8,128)}, f32[512,128]{1,0:T(8,128)S(1)}, u32[]{:S(2)}, u32[]{:S(2)}) %collective-permute-start) | collective-permute-done | bytes 262176 | tf_op jit(solution)/shard_map/ppermute | solution.py:270
  39.1 0.0 copy-done.3
  39.1 0.0 copy-done.4
  39.1 3.9 %shard_map.117 = f32[5,512,128]{2,1,0:T(8,128)} custom-call(s32[2]{0:T(128)S(1)} %pad_add_fusion.where, f32[512,128]{1,0:T(8,128)S(1)} %bitcast.12, f32[512,128]{1,0:T(8,128)S(1)} %collective-permute-done.refs_1_, f32[2,256,1280]{2,1,0:T(8,128)S(1)} %get-tuple-element.17.refs_2_, f32[5,512,128]{2,1,0:T(8,128)S(1)} %shard_map.115.refs_4_.refs_3_, ...), custom_call_target="tpu_custom_call" | custom-call | flops 503316480 | bytes 6160484 | tf_op jit(solution)/shard_map/pallas_call | solution.py:231
  42.9 0.2 collective-permute-done.6.refs_1_
  43.2 0.7 %shard_map.118.refs_2_ = f32[512,128]{1,0:T(8,128)} custom-call(f32[384,128]{1,0:T(8,128)S(1)} %get-tuple-element.20.refs_0_, f32[384,128]{1,0:T(8,128)S(1)} %collective-permute-done.6.refs_1_), custom_call_target="tpu_custom_call" | custom-call | tf_op jit(solution)/shard_map/pallas_call | solution.py:354
  43.9 0.0 collective-permute-done.5.refs_1_
  43.9 0.6 %shard_map.119 = f32[512,128]{1,0:T(8,128)} custom-call(f32[128,128]{1,0:T(8,128)S(1)} %get-tuple-element.18.refs_0_, f32[128,128]{1,0:T(8,128)S(1)} %collective-permute-done.5.refs_1_, f32[512,128]{1,0:T(8,128)} %shard_map.118.refs_2_), custom_call_target="tpu_custom_call", output_to_operand_aliasing={{}: (2, {})} | custom-call | tf_op jit(solution)/shard_map/pallas_call | solution.py:354
Async XLA Ops:
  0.6 32.8 %collective-permute-start.1 = (f32[5,512,128]{2,1,0:T(8,128)}, f32[5,512,128]{2,1,0:T(8,128)S(1)}, u32[]{:S(2)}, u32[]{:S(2)}) collective-permute-start(f32[5,512,128]{2,1,0:T(8,128)} %bitcast.7), channel_id=1, source_target_pairs={{16,0},{0,16},{17,1},{1,17},{18,2},{2,18},{19,3},{3,19},{20,4},{4,... | collective-permute-start | bytes 3932168 | tf_op jit(solution)/shard_map/ppermute | solution.py:270
  3.6 1.4 %copy-start = (f32[5,128,4,128]{3,2,1,0:T(4,128)S(1)}, f32[5,128,4,128]{3,2,1,0:T(4,128)}, u32[]{:S(2)}) copy-start(f32[5,128,4,128]{3,2,1,0:T(4,128)} %param.10) | copy-start | bytes 3932164
  5.0 6.9 %copy-start.1 = (f32[5,128,4,128]{3,2,1,0:T(4,128)S(1)}, f32[5,128,4,128]{3,2,1,0:T(4,128)}, u32[]{:S(2)}) copy-start(f32[5,128,4,128]{3,2,1,0:T(4,128)} %param.10) | copy-start | bytes 3932164
  5.0 6.9 %copy-start.8 = (f32[5,5]{1,0:T(8,128)S(1)}, f32[5,5]{1,0:T(8,128)}, u32[]{:S(2)}) copy-start(f32[5,5]{1,0:T(8,128)} %refs_4_.1) | copy-start | bytes 304
  6.4 17.4 %collective-permute-start.2 = (f32[5,128,128]{2,1,0:T(8,128)}, f32[5,128,128]{2,1,0:T(8,128)S(1)}, u32[]{:S(2)}, u32[]{:S(2)}) collective-permute-start(f32[5,128,128]{2,1,0:T(8,128)} %get-tuple-element.14), channel_id=1, source_target_pairs={{0,2},{2,4},{4,6},{6,8},{8,10},{10,12},{12,14},{1,3},{3,5},{5,7},{... | collective-permute-start | bytes 983048 | tf_op jit(solution)/shard_map/ppermute | solution.py:285
  9.8 14.0 %collective-permute-start.3 = (f32[5,128,128]{2,1,0:T(8,128)}, f32[5,128,128]{2,1,0:T(8,128)S(1)}, u32[]{:S(2)}, u32[]{:S(2)}) collective-permute-start(f32[5,128,128]{2,1,0:T(8,128)} %get-tuple-element.15), channel_id=1, source_target_pairs={{2,0},{4,2},{6,4},{8,6},{10,8},{12,10},{14,12},{3,1},{5,3},{7,5},{... | collective-permute-start | bytes 983048 | tf_op jit(solution)/shard_map/ppermute | solution.py:286
  11.1 6.2 %collective-permute-start.4 = (f32[128,128]{1,0:T(8,128)}, f32[128,128]{1,0:T(8,128)}, u32[]{:S(2)}, u32[]{:S(2)}) collective-permute-start(f32[128,128]{1,0:T(8,128)} %get-tuple-element.16), channel_id=1, source_target_pairs={{0,1},{1,0},{2,3},{3,2},{4,5},{5,4},{6,7},{7,6},{8,9},{9,8},{10,11... | collective-permute-start | bytes 196616 | tf_op jit(solution)/shard_map/ppermute | solution.py:288
  11.2 27.9 %collective-permute-start = (f32[512,128]{1,0:T(8,128)}, f32[512,128]{1,0:T(8,128)S(1)}, u32[]{:S(2)}, u32[]{:S(2)}) collective-permute-start(f32[512,128]{1,0:T(8,128)} %bitcast.11), channel_id=1, source_target_pairs={{16,0},{0,16},{17,1},{1,17},{18,2},{2,18},{19,3},{3,19},{20,4},{4,... | collective-permute-start | bytes 786440 | tf_op jit(solution)/shard_map/ppermute | solution.py:270
  11.9 1.3 %copy-start.9 = (f32[5,128,4,128]{3,2,1,0:T(4,128)S(1)}, f32[5,128,4,128]{3,2,1,0:T(4,128)}, u32[]{:S(2)}) copy-start(f32[5,128,4,128]{3,2,1,0:T(4,128)} %param.11) | copy-start | bytes 3932164
  13.2 1.0 %copy-start.10 = (bf16[2,256,384]{2,1,0:T(8,128)(2,1)S(1)}, bf16[2,256,384]{2,1,0:T(8,128)(2,1)}, u32[]{:S(2)}) copy-start(bf16[2,256,384]{2,1,0:T(8,128)(2,1)} %constant.14.clone.table) | copy-start | bytes 1179652
  14.2 9.6 %copy-start.5 = (f32[5,5]{1,0:T(8,128)S(1)}, f32[5,5]{1,0:T(8,128)}, u32[]{:S(2)}) copy-start(f32[5,5]{1,0:T(8,128)} %jac_axial.1) | copy-start | bytes 304
  14.2 9.6 %copy-start.6 = (f32[5,5]{1,0:T(8,128)S(1)}, f32[5,5]{1,0:T(8,128)}, u32[]{:S(2)}) copy-start(f32[5,5]{1,0:T(8,128)} %jac_radial.1) | copy-start | bytes 304
  14.2 9.6 %copy-start.7 = (f32[5,5]{1,0:T(8,128)S(1)}, f32[5,5]{1,0:T(8,128)}, u32[]{:S(2)}) copy-start(f32[5,5]{1,0:T(8,128)} %jac_swirl.1) | copy-start | bytes 304
  17.3 16.1 %copy-start.2 = (bf16[2,1,256,384]{3,2,1,0:T(8,128)(2,1)S(1)}, bf16[2,1,256,384]{3,2,1,0:T(8,128)(2,1)}, u32[]{:S(2)}) copy-start(bf16[2,1,256,384]{3,2,1,0:T(8,128)(2,1)} %constant.15.clone.refs_3_) | copy-start | bytes 1179652
  33.5 5.6 %copy-start.3 = (bf16[2,128,768]{2,1,0:T(8,128)(2,1)S(1)}, bf16[2,128,768]{2,1,0:T(8,128)(2,1)}, u32[]{:S(2)}) copy-start(bf16[2,128,768]{2,1,0:T(8,128)(2,1)} %constant.16.clone.refs_5_) | copy-start | bytes 1179652
  33.5 5.6 %copy-start.4 = (f32[128,4,128]{2,1,0:T(4,128)S(1)}, f32[128,4,128]{2,1,0:T(4,128)}, u32[]{:S(2)}) copy-start(f32[128,4,128]{2,1,0:T(4,128)} %param.12) | copy-start | bytes 786436
  35.2 8.0 %collective-permute-start.6 = (f32[384,128]{1,0:T(8,128)S(1)}, f32[384,128]{1,0:T(8,128)S(1)}, u32[]{:S(2)}, u32[]{:S(2)}) collective-permute-start(f32[384,128]{1,0:T(8,128)S(1)} %get-tuple-element.21), channel_id=1, source_target_pairs={{0,16},{16,0},{1,17},{17,1},{2,18},{18,2},{3,19},{19,3},{4,20},{20... | collective-permute-start | bytes 589832 | tf_op jit(solution)/shard_map/ppermute | solution.py:273
  37.3 6.6 %collective-permute-start.5 = (f32[128,128]{1,0:T(8,128)S(1)}, f32[128,128]{1,0:T(8,128)S(1)}, u32[]{:S(2)}, u32[]{:S(2)}) collective-permute-start(f32[128,128]{1,0:T(8,128)S(1)} %get-tuple-element.19), channel_id=1, source_target_pairs={{0,16},{16,0},{1,17},{17,1},{2,18},{18,2},{3,19},{19,3},{4,20},{20... | collective-permute-start | bytes 196616 | tf_op jit(solution)/shard_map/ppermute | solution.py:273

commit v5 on v3

--- a/solution.py
+++ b/solution.py
@@ -57,7 +57,7 @@
 
 def pack_kernel(fields, modes, cells_ax, adj, first, last, edges):
     lanes = adj.shape[2]
-    lane = lax.broadcasted_iota(jnp.int32, (modes, lanes), 1)
+    pair = lax.broadcasted_iota(jnp.int32, (modes, lanes), 1) // 2
     packed = jnp.zeros((modes, lanes), jnp.float32)
     for f in range(fields):
         for x in range(cells_ax):
@@ -67,10 +67,7 @@
             if x == cells_ax - 1:
                 last[f] = block
             j = f * cells_ax + x
-            packed = jnp.where(lane == j, pltpu.roll(block, j, 1), packed)
-            packed = jnp.where(
-                lane == lanes // 2 + j, pltpu.roll(block, (j + 1 + lanes // 2) % lanes, 1), packed
-            )
+            packed = jnp.where(pair == j, pltpu.roll(block, 2 * j + 1, 1), packed)
     edges[...] = packed
 
 
@@ -162,7 +159,7 @@
         rate = swirl * order
         for p in range(2):
             halo = pl.ds(2 * i * chunk + p, chunk, stride=2)
-            inner_edges, outer_edges = inner[halo, :], outer[halo, :]
+            edges = jnp.where(lane % 2 == 0, pltpu.roll(inner[halo, :], 2, 1), outer[halo, :])
             for x in range(cells_ax):
                 def at(e, parity, cell):
                     start = (2 * i * chunk + parity) * cells_ax + cell
@@ -175,16 +172,10 @@
                     low = below[e, halo, :] if x == 0 else at(e, p, x - 1)
                     high = above[e, halo, :] if x == cells_ax - 1 else at(e, p, x + 1)
                     axial = 0.5 * (high - low)
-                    j = e * cells_ax + x
-                    from_inner = jnp.where(
-                        lane == lanes - 1, pltpu.roll(inner_edges, lanes // 2 - 1 - j, 1), centre
-                    )
-                    from_outer = jnp.where(
-                        lane == 0, pltpu.roll(outer_edges, (lanes - j) % lanes, 1), centre
-                    )
-                    radial = has_outer * pltpu.roll(from_outer, lanes - 1, 1) - has_inner * pltpu.roll(
-                        from_inner, 1, 1
-                    )
+                    edge = pltpu.roll(edges, lanes - 2 * (e * cells_ax + x) - 2, 1)
+                    inward = jnp.where(lane == 0, edge, pltpu.roll(centre, 1, 1))
+                    outward = jnp.where(lane == lanes - 1, edge, pltpu.roll(centre, lanes - 1, 1))
+                    radial = has_outer * outward - has_inner * inward
                     turned = (rate if p == 0 else -rate) * at(e, 1 - p, x)
                     for f in range(fields):
                         term = (

time: 44.9 us -> 44.9 us (level)
  waiting for transfers between devices: 9.37 us -> 14.9 us
  Pallas kernels: 19.5 us -> 14 us
    ppermute x2, waiting for transfers between devices: 1.99 us -> 7.52 us  [fetch(): lax.ppermute(value, 'mode', [((i + s) % groups, i) for i in range(groups)])]
    pallas_call x4, Pallas kernels: 18.1 us -> 12.9 us  [call(): pl.pallas_call(kernel, grid_spec=pltpu.PrefetchScalarGridSpec(num_scalar_...]
  transfers between devices with their start and end apart: 6 -> 6, of which waited for: 4 -> 4; matrix products, arithmetic and copies ran while one was open for 0% -> 0% of each run, Pallas kernels for 44% -> 31%
where the time goes in v5:
time: 44.9 us; the launch traced here: 44.6 us
  waiting for transfers between devices  14.9 us (33%)
  Pallas kernels  14 us (31%)
  starting transfers between devices  10.5 us (23%)
  local copies, waits for them, and re-layouts  3.69 us (8%)
  other arithmetic  0.81 us (2%)
  between operations  0.71 us (2%)
    pallas_call x4, Pallas kernels, call(): pl.pallas_call(kernel, grid_spec=pltpu.PrefetchScalarGridSpec(num_scalar_...  12.9 us
    ppermute x2, waiting for transfers between devices, fetch(): lax.ppermute(value, 'mode', [((i + s) % groups, i) for i in range(groups)])  7.52 us
    ppermute x1, waiting for transfers between devices, body(): below = lax.ppermute(last, 'ax', up)  6.45 us
    unnamed x22, local copies, waits for them, and re-layouts  3.69 us
    ppermute x2, starting transfers between devices, fetch(): lax.ppermute(value, 'mode', [((i + s) % groups, i) for i in range(groups)])  3.6 us
    ppermute x1, starting transfers between devices, body(): below = lax.ppermute(last, 'ax', up)  3.43 us
    ppermute x1, starting transfers between devices, deliver(): lax.ppermute(value, 'mode', [(i, (i + s) % groups) for i in range(groups)])  2.12 us
    ppermute x1, starting transfers between devices, body(): above = lax.ppermute(first, 'ax', down)  1.29 us
  transfers between devices with their start and end apart: 6, of which 4 were waited for; matrix products, arithmetic and copies ran while one was open for 0% of the time, Pallas kernels for 31%

profile of v5, /device:TPU:0, one launch (start us, length us, event | category | flops | bytes accessed | tf_op | source)
XLA Modules:
  0.0 44.6 jit_solution(5305810878965869057)
XLA Ops:
  0.6 3.0 %collective-permute-start.1 = (f32[5,512,128]{2,1,0:T(8,128)}, f32[5,512,128]{2,1,0:T(8,128)S(1)}, u32[]{:S(2)}, u32[]{:S(2)}) collective-permute-start(f32[5,512,128]{2,1,0:T(8,128)} %bitcast.7), channel_id=1, source_target_pairs={{16,0},{0,16},{17,1},{1,17},{18,2},{2,18},{19,3},{3,19},{20,4},{4,... | collective-permute-start | bytes 3932168 | tf_op jit(solution)/shard_map/ppermute | solution.py:253
  3.6 0.0 copy-start
  3.6 1.3 %copy-done = f32[5,128,4,128]{3,2,1,0:T(4,128)S(1)} copy-done((f32[5,128,4,128]{3,2,1,0:T(4,128)S(1)}, f32[5,128,4,128]{3,2,1,0:T(4,128)}, u32[]{:S(2)}) %copy-start) | copy-done | bytes 1310744
  5.0 0.0 copy-start.1
  5.0 0.0 copy-start.8
  5.0 1.1 %shard_map.114 = (f32[5,128,128]{2,1,0:T(8,128)}, f32[5,128,128]{2,1,0:T(8,128)}, f32[128,128]{1,0:T(8,128)}) custom-call(f32[5,512,128]{2,1,0:T(8,128)S(1)} %bitcast.8), custom_call_target="tpu_custom_call" | custom-call | tf_op jit(solution)/shard_map/pallas_call | solution.py:263
  6.1 3.4 %collective-permute-start.2 = (f32[5,128,128]{2,1,0:T(8,128)}, f32[5,128,128]{2,1,0:T(8,128)S(1)}, u32[]{:S(2)}, u32[]{:S(2)}) collective-permute-start(f32[5,128,128]{2,1,0:T(8,128)} %get-tuple-element.12), channel_id=1, source_target_pairs={{0,2},{2,4},{4,6},{6,8},{8,10},{10,12},{12,14},{1,3},{3,5},{5,7},{... | collective-permute-start | bytes 983048 | tf_op jit(solution)/shard_map/ppermute | solution.py:268
  9.5 1.3 %collective-permute-start.3 = (f32[5,128,128]{2,1,0:T(8,128)}, f32[5,128,128]{2,1,0:T(8,128)S(1)}, u32[]{:S(2)}, u32[]{:S(2)}) collective-permute-start(f32[5,128,128]{2,1,0:T(8,128)} %get-tuple-element.13), channel_id=1, source_target_pairs={{2,0},{4,2},{6,4},{8,6},{10,8},{12,10},{14,12},{3,1},{5,3},{7,5},{... | collective-permute-start | bytes 983048 | tf_op jit(solution)/shard_map/ppermute | solution.py:269
  10.8 0.1 collective-permute-start.4
  10.9 0.6 %collective-permute-start = (f32[512,128]{1,0:T(8,128)}, f32[512,128]{1,0:T(8,128)S(1)}, u32[]{:S(2)}, u32[]{:S(2)}) collective-permute-start(f32[512,128]{1,0:T(8,128)} %bitcast.11), channel_id=1, source_target_pairs={{16,0},{0,16},{17,1},{1,17},{18,2},{2,18},{19,3},{3,19},{20,4},{4,... | collective-permute-start | bytes 786440 | tf_op jit(solution)/shard_map/ppermute | solution.py:253
  11.5 0.1 pad_add_fusion.where
  11.5 0.0 copy-done.1
  11.6 0.0 copy-done.8
  11.6 0.0 copy-start.9
  11.6 1.3 %copy-done.9 = f32[5,128,4,128]{3,2,1,0:T(4,128)S(1)} copy-done((f32[5,128,4,128]{3,2,1,0:T(4,128)S(1)}, f32[5,128,4,128]{3,2,1,0:T(4,128)}, u32[]{:S(2)}) %copy-start.9) | copy-done | bytes 1310744
  12.9 0.0 copy-start.10
  12.9 1.0 %copy-done.10 = bf16[2,256,384]{2,1,0:T(8,128)(2,1)S(1)} copy-done((bf16[2,256,384]{2,1,0:T(8,128)(2,1)S(1)}, bf16[2,256,384]{2,1,0:T(8,128)(2,1)}, u32[]{:S(2)}) %copy-start.10) | copy-done | bytes 393240
  13.9 0.0 copy-start.5
  13.9 0.0 copy-start.6
  13.9 0.0 copy-start.7
  13.9 3.1 %shard_map.113 = (f32[2,256,1280]{2,1,0:T(8,128)S(1)}, f32[2,256,1280]{2,1,0:T(8,128)S(1)}) custom-call(s32[2]{0:T(128)S(1)} %pad_add_fusion.where, f32[5,512,128]{2,1,0:T(8,128)S(1)} %bitcast.9, f32[5,512,128]{2,1,0:T(8,128)S(1)} %bitcast.13, f32[5,5]{1,0:T(8,128)S(1)} %copy-done.8, bf16[2,256,384]{2,1,0:T(8,128)(2,1)S(1)} %copy-done.10), custom_call_target="tpu_custom_call" | custom-call | flops 1006632960 | bytes 8257636 | tf_op jit(solution)/shard_map/pallas_call | solution.py:214
  17.0 0.0 copy-start.2
  17.0 0.0 collective-permute-done.4.inner.outer
  17.0 6.5 %collective-permute-done.2.below = f32[5,128,128]{2,1,0:T(8,128)S(1)} collective-permute-done((f32[5,128,128]{2,1,0:T(8,128)}, f32[5,128,128]{2,1,0:T(8,128)S(1)}, u32[]{:S(2)}, u32[]{:S(2)}) %collective-permute-start.2) | collective-permute-done | bytes 327712 | tf_op jit(solution)/shard_map/ppermute | solution.py:268
  23.5 0.0 collective-permute-done.3.above
  23.5 0.0 copy-done.5
  23.5 0.0 copy-done.6
  23.5 0.0 copy-done.7
  23.5 4.2 %shard_map.115.refs_4_.refs_3_ = f32[5,512,128]{2,1,0:T(8,128)S(1)} custom-call(s32[2]{0:T(128)S(1)} %pad_add_fusion.where, f32[5,512,128]{2,1,0:T(8,128)S(1)} %bitcast.10, f32[5,128,128]{2,1,0:T(8,128)S(1)} %collective-permute-done.2.below, f32[5,128,128]{2,1,0:T(8,128)S(1)} %collective-permute-done.3.above, f32[128,128]{1,0:T(8,128)} %collective-permute-done.4.inner.outer, ...), custom_call_target="tpu_custom_call" | custom-call | flops 52428800 | bytes 3408172 | tf_op jit(solution)/shard_map/pallas_call | solution.py:214
  27.7 5.7 %collective-permute-done.1.refs_0_ = f32[5,512,128]{2,1,0:T(8,128)S(1)} collective-permute-done((f32[5,512,128]{2,1,0:T(8,128)}, f32[5,512,128]{2,1,0:T(8,128)S(1)}, u32[]{:S(2)}, u32[]{:S(2)}) %collective-permute-start.1) | collective-permute-done | bytes 1310752 | tf_op jit(solution)/shard_map/ppermute | solution.py:253
  33.4 0.0 copy-done.2
  33.5 0.0 copy-start.3
  33.5 0.0 copy-start.4
  33.5 1.7 %shard_map.116 = (f32[2,256,1280]{2,1,0:T(8,128)S(1)}, f32[512,128]{1,0:T(8,128)S(1)}, f32[512,128]{1,0:T(8,128)S(1)}) custom-call(s32[2]{0:T(128)S(1)} %pad_add_fusion.where, f32[5,512,128]{2,1,0:T(8,128)S(1)} %collective-permute-done.1.refs_0_, f32[2,256,1280]{2,1,0:T(8,128)S(1)} %get-tuple-element.10.refs_1_, ...), custom_call_target="tpu_custom_call" | custom-call | flops 503316480 | bytes 11403264 | tf_op jit(solution)/shard_map/pallas_call | solution.py:214
  35.2 2.1 %collective-permute-start.5 = (f32[512,128]{1,0:T(8,128)S(1)}, f32[512,128]{1,0:T(8,128)S(1)}, u32[]{:S(2)}, u32[]{:S(2)}) collective-permute-start(f32[512,128]{1,0:T(8,128)S(1)} %get-tuple-element.17), channel_id=1, source_target_pairs={{0,16},{16,0},{1,17},{17,1},{2,18},{18,2},{3,19},{19,3},{4,20},{20... | collective-permute-start | bytes 786440 | tf_op jit(solution)/shard_map/ppermute | solution.py:256
  37.3 1.8 %collective-permute-done.refs_1_ = f32[512,128]{1,0:T(8,128)S(1)} collective-permute-done((f32[512,128]{1,0:T(8,128)}, f32[512,128]{1,0:T(8,128)S(1)}, u32[]{:S(2)}, u32[]{:S(2)}) %collective-permute-start) | collective-permute-done | bytes 262176 | tf_op jit(solution)/shard_map/ppermute | solution.py:253
  39.1 0.0 copy-done.3
  39.1 0.0 copy-done.4
  39.1 3.9 %shard_map.117 = f32[5,512,128]{2,1,0:T(8,128)} custom-call(s32[2]{0:T(128)S(1)} %pad_add_fusion.where, f32[512,128]{1,0:T(8,128)S(1)} %bitcast.12, f32[512,128]{1,0:T(8,128)S(1)} %collective-permute-done.refs_1_, f32[2,256,1280]{2,1,0:T(8,128)S(1)} %get-tuple-element.15.refs_2_, f32[5,512,128]{2,1,0:T(8,128)S(1)} %shard_map.115.refs_4_.refs_3_, ...), custom_call_target="tpu_custom_call" | custom-call | flops 503316480 | bytes 6160484 | tf_op jit(solution)/shard_map/pallas_call | solution.py:214
  42.9 0.9 %collective-permute-done.5 = f32[512,128]{1,0:T(8,128)S(1)} collective-permute-done((f32[512,128]{1,0:T(8,128)S(1)}, f32[512,128]{1,0:T(8,128)S(1)}, u32[]{:S(2)}, u32[]{:S(2)}) %collective-permute-start.5) | collective-permute-done | bytes 262176 | tf_op jit(solution)/shard_map/ppermute | solution.py:256
  43.9 0.7 %add_negate_fusion = f32[512,128]{1,0:T(8,128)} fusion(f32[512,128]{1,0:T(8,128)S(1)} %get-tuple-element.16, f32[512,128]{1,0:T(8,128)S(1)} %collective-permute-done.5), kind=kLoop, calls=%fused_computation | loop fusion | flops 131072 | bytes 786432 | tf_op jit(solution)/shard_map/neg | solution.py:335
Async XLA Ops:
  0.6 32.8 %collective-permute-start.1 = (f32[5,512,128]{2,1,0:T(8,128)}, f32[5,512,128]{2,1,0:T(8,128)S(1)}, u32[]{:S(2)}, u32[]{:S(2)}) collective-permute-start(f32[5,512,128]{2,1,0:T(8,128)} %bitcast.7), channel_id=1, source_target_pairs={{16,0},{0,16},{17,1},{1,17},{18,2},{2,18},{19,3},{3,19},{20,4},{4,... | collective-permute-start | bytes 3932168 | tf_op jit(solution)/shard_map/ppermute | solution.py:253
  3.6 1.4 %copy-start = (f32[5,128,4,128]{3,2,1,0:T(4,128)S(1)}, f32[5,128,4,128]{3,2,1,0:T(4,128)}, u32[]{:S(2)}) copy-start(f32[5,128,4,128]{3,2,1,0:T(4,128)} %param.10) | copy-start | bytes 3932164
  5.0 6.6 %copy-start.1 = (f32[5,128,4,128]{3,2,1,0:T(4,128)S(1)}, f32[5,128,4,128]{3,2,1,0:T(4,128)}, u32[]{:S(2)}) copy-start(f32[5,128,4,128]{3,2,1,0:T(4,128)} %param.10) | copy-start | bytes 3932164
  5.0 6.6 %copy-start.8 = (f32[5,5]{1,0:T(8,128)S(1)}, f32[5,5]{1,0:T(8,128)}, u32[]{:S(2)}) copy-start(f32[5,5]{1,0:T(8,128)} %refs_4_.1) | copy-start | bytes 304
  6.1 17.4 %collective-permute-start.2 = (f32[5,128,128]{2,1,0:T(8,128)}, f32[5,128,128]{2,1,0:T(8,128)S(1)}, u32[]{:S(2)}, u32[]{:S(2)}) collective-permute-start(f32[5,128,128]{2,1,0:T(8,128)} %get-tuple-element.12), channel_id=1, source_target_pairs={{0,2},{2,4},{4,6},{6,8},{8,10},{10,12},{12,14},{1,3},{3,5},{5,7},{... | collective-permute-start | bytes 983048 | tf_op jit(solution)/shard_map/ppermute | solution.py:268
  9.5 14.0 %collective-permute-start.3 = (f32[5,128,128]{2,1,0:T(8,128)}, f32[5,128,128]{2,1,0:T(8,128)S(1)}, u32[]{:S(2)}, u32[]{:S(2)}) collective-permute-start(f32[5,128,128]{2,1,0:T(8,128)} %get-tuple-element.13), channel_id=1, source_target_pairs={{2,0},{4,2},{6,4},{8,6},{10,8},{12,10},{14,12},{3,1},{5,3},{7,5},{... | collective-permute-start | bytes 983048 | tf_op jit(solution)/shard_map/ppermute | solution.py:269
  10.8 6.2 %collective-permute-start.4 = (f32[128,128]{1,0:T(8,128)}, f32[128,128]{1,0:T(8,128)}, u32[]{:S(2)}, u32[]{:S(2)}) collective-permute-start(f32[128,128]{1,0:T(8,128)} %get-tuple-element.14), channel_id=1, source_target_pairs={{0,1},{1,0},{2,3},{3,2},{4,5},{5,4},{6,7},{7,6},{8,9},{9,8},{10,11... | collective-permute-start | bytes 196616 | tf_op jit(solution)/shard_map/ppermute | solution.py:271
  10.9 28.2 %collective-permute-start = (f32[512,128]{1,0:T(8,128)}, f32[512,128]{1,0:T(8,128)S(1)}, u32[]{:S(2)}, u32[]{:S(2)}) collective-permute-start(f32[512,128]{1,0:T(8,128)} %bitcast.11), channel_id=1, source_target_pairs={{16,0},{0,16},{17,1},{1,17},{18,2},{2,18},{19,3},{3,19},{20,4},{4,... | collective-permute-start | bytes 786440 | tf_op jit(solution)/shard_map/ppermute | solution.py:253
  11.6 1.3 %copy-start.9 = (f32[5,128,4,128]{3,2,1,0:T(4,128)S(1)}, f32[5,128,4,128]{3,2,1,0:T(4,128)}, u32[]{:S(2)}) copy-start(f32[5,128,4,128]{3,2,1,0:T(4,128)} %param.11) | copy-start | bytes 3932164
  12.9 1.0 %copy-start.10 = (bf16[2,256,384]{2,1,0:T(8,128)(2,1)S(1)}, bf16[2,256,384]{2,1,0:T(8,128)(2,1)}, u32[]{:S(2)}) copy-start(bf16[2,256,384]{2,1,0:T(8,128)(2,1)} %constant.14.clone.table) | copy-start | bytes 1179652
  13.9 9.6 %copy-start.5 = (f32[5,5]{1,0:T(8,128)S(1)}, f32[5,5]{1,0:T(8,128)}, u32[]{:S(2)}) copy-start(f32[5,5]{1,0:T(8,128)} %jac_axial.1) | copy-start | bytes 304
  13.9 9.6 %copy-start.6 = (f32[5,5]{1,0:T(8,128)S(1)}, f32[5,5]{1,0:T(8,128)}, u32[]{:S(2)}) copy-start(f32[5,5]{1,0:T(8,128)} %jac_radial.1) | copy-start | bytes 304
  13.9 9.6 %copy-start.7 = (f32[5,5]{1,0:T(8,128)S(1)}, f32[5,5]{1,0:T(8,128)}, u32[]{:S(2)}) copy-start(f32[5,5]{1,0:T(8,128)} %jac_swirl.1) | copy-start | bytes 304
  17.0 16.4 %copy-start.2 = (bf16[2,1,256,384]{3,2,1,0:T(8,128)(2,1)S(1)}, bf16[2,1,256,384]{3,2,1,0:T(8,128)(2,1)}, u32[]{:S(2)}) copy-start(bf16[2,1,256,384]{3,2,1,0:T(8,128)(2,1)} %constant.15.clone.refs_3_) | copy-start | bytes 1179652
  33.5 5.6 %copy-start.3 = (bf16[2,128,768]{2,1,0:T(8,128)(2,1)S(1)}, bf16[2,128,768]{2,1,0:T(8,128)(2,1)}, u32[]{:S(2)}) copy-start(bf16[2,128,768]{2,1,0:T(8,128)(2,1)} %constant.16.clone.refs_5_) | copy-start | bytes 1179652
  33.5 5.6 %copy-start.4 = (f32[128,4,128]{2,1,0:T(4,128)S(1)}, f32[128,4,128]{2,1,0:T(4,128)}, u32[]{:S(2)}) copy-start(f32[128,4,128]{2,1,0:T(4,128)} %param.12) | copy-start | bytes 786436
  35.2 8.7 %collective-permute-start.5 = (f32[512,128]{1,0:T(8,128)S(1)}, f32[512,128]{1,0:T(8,128)S(1)}, u32[]{:S(2)}, u32[]{:S(2)}) collective-permute-start(f32[512,128]{1,0:T(8,128)S(1)} %get-tuple-element.17), channel_id=1, source_target_pairs={{0,16},{16,0},{1,17},{17,1},{2,18},{18,2},{3,19},{19,3},{4,20},{20... | collective-permute-start | bytes 786440 | tf_op jit(solution)/shard_map/ppermute | solution.py:256

commit v6 on v4

--- a/solution.py
+++ b/solution.py
@@ -57,7 +57,7 @@
 
 def pack_kernel(fields, modes, cells_ax, adj, first, last, edges):
     lanes = adj.shape[2]
-    lane = lax.broadcasted_iota(jnp.int32, (modes, lanes), 1)
+    pair = lax.broadcasted_iota(jnp.int32, (modes, lanes), 1) // 2
     packed = jnp.zeros((modes, lanes), jnp.float32)
     for f in range(fields):
         for x in range(cells_ax):
@@ -67,10 +67,7 @@
             if x == cells_ax - 1:
                 last[f] = block
             j = f * cells_ax + x
-            packed = jnp.where(lane == j, pltpu.roll(block, j, 1), packed)
-            packed = jnp.where(
-                lane == lanes // 2 + j, pltpu.roll(block, (j + 1 + lanes // 2) % lanes, 1), packed
-            )
+            packed = jnp.where(pair == j, pltpu.roll(block, 2 * j + 1, 1), packed)
     edges[...] = packed
 
 
@@ -170,7 +167,7 @@
         rate = swirl * order
         for p in range(2):
             halo = pl.ds(2 * i * chunk + p, chunk, stride=2)
-            inner_edges, outer_edges = inner[halo, :], outer[halo, :]
+            edges = jnp.where(lane % 2 == 0, pltpu.roll(inner[halo, :], 2, 1), outer[halo, :])
             for x in range(cells_ax):
                 def at(e, parity, cell):
                     start = (2 * i * chunk + parity) * cells_ax + cell
@@ -183,16 +180,10 @@
                     low = below[e, halo, :] if x == 0 else at(e, p, x - 1)
                     high = above[e, halo, :] if x == cells_ax - 1 else at(e, p, x + 1)
                     axial = 0.5 * (high - low)
-                    j = e * cells_ax + x
-                    from_inner = jnp.where(
-                        lane == lanes - 1, pltpu.roll(inner_edges, lanes // 2 - 1 - j, 1), centre
-                    )
-                    from_outer = jnp.where(
-                        lane == 0, pltpu.roll(outer_edges, (lanes - j) % lanes, 1), centre
-                    )
-                    radial = has_outer * pltpu.roll(from_outer, lanes - 1, 1) - has_inner * pltpu.roll(
-                        from_inner, 1, 1
-                    )
+                    edge = pltpu.roll(edges, lanes - 2 * (e * cells_ax + x) - 2, 1)
+                    inward = jnp.where(lane == 0, edge, pltpu.roll(centre, 1, 1))
+                    outward = jnp.where(lane == lanes - 1, edge, pltpu.roll(centre, lanes - 1, 1))
+                    radial = has_outer * outward - has_inner * inward
                     turned = (rate if p == 0 else -rate) * at(e, 1 - p, x)
                     for f in range(fields):
                         term = (
@@ -321,7 +312,7 @@
         32 * fields * fields * rows * lanes,
     )[0]
 
-    cuts = (0, max(modes * 3 // 4 // 8 * 8, modes // 2), modes)
+    cuts = (0, modes // 2, modes)
     pieces = len(cuts) - 1
     piece_rows = [(cuts[k + 1] - cuts[k]) * cells_ax for k in range(pieces)]
     joined = call(

time: 44.8 us -> 44.8 us (level)
  waiting for transfers between devices: 8.59 us -> 14.1 us
  Pallas kernels: 20.8 us -> 15.3 us
    ppermute x2, waiting for transfers between devices: 1.91 us -> 7.44 us  [fetch(): lax.ppermute(value, 'mode', [((i + s) % groups, i) for i in range(groups)])]
    pallas_call x4, Pallas kernels: 18.1 us -> 12.9 us  [call(): pl.pallas_call(kernel, grid_spec=pltpu.PrefetchScalarGridSpec(num_scalar_...]
  transfers between devices with their start and end apart: 7 -> 7, of which waited for: 4 -> 4; matrix products, arithmetic and copies ran while one was open for 0% -> 0% of each run, Pallas kernels for 45% -> 33%
where the time goes in v6:
time: 44.8 us; the launch traced here: 44.5 us
  Pallas kernels  15.3 us (34%)
  waiting for transfers between devices  14.1 us (31%)
  starting transfers between devices  10.6 us (24%)
  local copies, waits for them, and re-layouts  3.69 us (8%)
  between operations  0.71 us (2%)
    pallas_call x4, Pallas kernels, call(): pl.pallas_call(kernel, grid_spec=pltpu.PrefetchScalarGridSpec(num_scalar_...  12.9 us
    ppermute x2, waiting for transfers between devices, fetch(): lax.ppermute(value, 'mode', [((i + s) % groups, i) for i in range(groups)])  7.44 us
    ppermute x1, waiting for transfers between devices, body(): below = lax.ppermute(last, 'ax', up)  6.45 us
    unnamed x22, local copies, waits for them, and re-layouts  3.69 us
    ppermute x2, starting transfers between devices, fetch(): lax.ppermute(value, 'mode', [((i + s) % groups, i) for i in range(groups)])  3.6 us
    ppermute x1, starting transfers between devices, body(): below = lax.ppermute(last, 'ax', up)  3.43 us
    ppermute x2, starting transfers between devices, deliver(): lax.ppermute(value, 'mode', [(i, (i + s) % groups) for i in range(groups)])  2.2 us
    pallas_call x2, Pallas kernels, body(): pl.pallas_call(functools.partial(total_kernel, groups), grid=(1,), out_sh...  1.34 us
  transfers between devices with their start and end apart: 7, of which 4 were waited for; matrix products, arithmetic and copies ran while one was open for 0% of the time, Pallas kernels for 33%

profile of v6, /device:TPU:0, one launch (start us, length us, event | category | flops | bytes accessed | tf_op | source)
XLA Modules:
  0.0 44.5 jit_solution(6078526328262695480)
XLA Ops:
  0.6 3.0 %collective-permute-start.1 = (f32[5,512,128]{2,1,0:T(8,128)}, f32[5,512,128]{2,1,0:T(8,128)S(1)}, u32[]{:S(2)}, u32[]{:S(2)}) collective-permute-start(f32[5,512,128]{2,1,0:T(8,128)} %bitcast.7), channel_id=1, source_target_pairs={{16,0},{0,16},{17,1},{1,17},{18,2},{2,18},{19,3},{3,19},{20,4},{4,... | collective-permute-start | bytes 3932168 | tf_op jit(solution)/shard_map/ppermute | solution.py:261
  3.6 0.0 copy-start
  3.6 1.3 %copy-done = f32[5,128,4,128]{3,2,1,0:T(4,128)S(1)} copy-done((f32[5,128,4,128]{3,2,1,0:T(4,128)S(1)}, f32[5,128,4,128]{3,2,1,0:T(4,128)}, u32[]{:S(2)}) %copy-start) | copy-done | bytes 1310744
  5.0 0.0 copy-start.1
  5.0 0.0 copy-start.8
  5.0 1.1 %shard_map.114 = (f32[5,128,128]{2,1,0:T(8,128)}, f32[5,128,128]{2,1,0:T(8,128)}, f32[128,128]{1,0:T(8,128)}) custom-call(f32[5,512,128]{2,1,0:T(8,128)S(1)} %bitcast.8), custom_call_target="tpu_custom_call" | custom-call | tf_op jit(solution)/shard_map/pallas_call | solution.py:271
  6.1 3.4 %collective-permute-start.2 = (f32[5,128,128]{2,1,0:T(8,128)}, f32[5,128,128]{2,1,0:T(8,128)S(1)}, u32[]{:S(2)}, u32[]{:S(2)}) collective-permute-start(f32[5,128,128]{2,1,0:T(8,128)} %get-tuple-element.14), channel_id=1, source_target_pairs={{0,2},{2,4},{4,6},{6,8},{8,10},{10,12},{12,14},{1,3},{3,5},{5,7},{... | collective-permute-start | bytes 983048 | tf_op jit(solution)/shard_map/ppermute | solution.py:276
  9.5 1.3 %collective-permute-start.3 = (f32[5,128,128]{2,1,0:T(8,128)}, f32[5,128,128]{2,1,0:T(8,128)S(1)}, u32[]{:S(2)}, u32[]{:S(2)}) collective-permute-start(f32[5,128,128]{2,1,0:T(8,128)} %get-tuple-element.15), channel_id=1, source_target_pairs={{2,0},{4,2},{6,4},{8,6},{10,8},{12,10},{14,12},{3,1},{5,3},{7,5},{... | collective-permute-start | bytes 983048 | tf_op jit(solution)/shard_map/ppermute | solution.py:277
  10.8 0.1 collective-permute-start.4
  10.9 0.6 %collective-permute-start = (f32[512,128]{1,0:T(8,128)}, f32[512,128]{1,0:T(8,128)S(1)}, u32[]{:S(2)}, u32[]{:S(2)}) collective-permute-start(f32[512,128]{1,0:T(8,128)} %bitcast.11), channel_id=1, source_target_pairs={{16,0},{0,16},{17,1},{1,17},{18,2},{2,18},{19,3},{3,19},{20,4},{4,... | collective-permute-start | bytes 786440 | tf_op jit(solution)/shard_map/ppermute | solution.py:261
  11.5 0.1 pad_add_fusion.where
  11.5 0.0 copy-done.1
  11.6 0.0 copy-done.8
  11.6 0.0 copy-start.9
  11.6 1.3 %copy-done.9 = f32[5,128,4,128]{3,2,1,0:T(4,128)S(1)} copy-done((f32[5,128,4,128]{3,2,1,0:T(4,128)S(1)}, f32[5,128,4,128]{3,2,1,0:T(4,128)}, u32[]{:S(2)}) %copy-start.9) | copy-done | bytes 1310744
  12.9 0.0 copy-start.10
  12.9 1.0 %copy-done.10 = bf16[2,256,384]{2,1,0:T(8,128)(2,1)S(1)} copy-done((bf16[2,256,384]{2,1,0:T(8,128)(2,1)S(1)}, bf16[2,256,384]{2,1,0:T(8,128)(2,1)}, u32[]{:S(2)}) %copy-start.10) | copy-done | bytes 393240
  13.9 0.0 copy-start.5
  13.9 0.0 copy-start.6
  13.9 0.0 copy-start.7
  13.9 3.1 %shard_map.113 = (f32[2,256,1280]{2,1,0:T(8,128)S(1)}, f32[2,256,1280]{2,1,0:T(8,128)S(1)}) custom-call(s32[2]{0:T(128)S(1)} %pad_add_fusion.where, f32[5,512,128]{2,1,0:T(8,128)S(1)} %bitcast.9, f32[5,512,128]{2,1,0:T(8,128)S(1)} %bitcast.13, f32[5,5]{1,0:T(8,128)S(1)} %copy-done.8, bf16[2,256,384]{2,1,0:T(8,128)(2,1)S(1)} %copy-done.10), custom_call_target="tpu_custom_call" | custom-call | flops 1006632960 | bytes 8257636 | tf_op jit(solution)/shard_map/pallas_call | solution.py:222
  17.0 0.0 copy-start.2
  17.0 0.0 collective-permute-done.4.inner.outer
  17.0 6.5 %collective-permute-done.2.below = f32[5,128,128]{2,1,0:T(8,128)S(1)} collective-permute-done((f32[5,128,128]{2,1,0:T(8,128)}, f32[5,128,128]{2,1,0:T(8,128)S(1)}, u32[]{:S(2)}, u32[]{:S(2)}) %collective-permute-start.2) | collective-permute-done | bytes 327712 | tf_op jit(solution)/shard_map/ppermute | solution.py:276
  23.5 0.0 collective-permute-done.3.above
  23.5 0.0 copy-done.5
  23.5 0.0 copy-done.6
  23.5 0.0 copy-done.7
  23.5 4.2 %shard_map.115.refs_4_.refs_3_ = f32[5,512,128]{2,1,0:T(8,128)S(1)} custom-call(s32[2]{0:T(128)S(1)} %pad_add_fusion.where, f32[5,512,128]{2,1,0:T(8,128)S(1)} %bitcast.10, f32[5,128,128]{2,1,0:T(8,128)S(1)} %collective-permute-done.2.below, f32[5,128,128]{2,1,0:T(8,128)S(1)} %collective-permute-done.3.above, f32[128,128]{1,0:T(8,128)} %collective-permute-done.4.inner.outer, ...), custom_call_target="tpu_custom_call" | custom-call | flops 52428800 | bytes 3408172 | tf_op jit(solution)/shard_map/pallas_call | solution.py:222
  27.7 5.7 %collective-permute-done.1.refs_0_ = f32[5,512,128]{2,1,0:T(8,128)S(1)} collective-permute-done((f32[5,512,128]{2,1,0:T(8,128)}, f32[5,512,128]{2,1,0:T(8,128)S(1)}, u32[]{:S(2)}, u32[]{:S(2)}) %collective-permute-start.1) | collective-permute-done | bytes 1310752 | tf_op jit(solution)/shard_map/ppermute | solution.py:261
  33.4 0.0 copy-done.2
  33.5 0.0 copy-start.3
  33.5 0.0 copy-start.4
  33.5 1.7 %shard_map.116 = (f32[2,256,1280]{2,1,0:T(8,128)S(1)}, f32[256,128]{1,0:T(8,128)S(1)}, f32[256,128]{1,0:T(8,128)S(1)}, f32[256,128]{1,0:T(8,128)S(1)}, f32[256,128]{1,0:T(8,128)S(1)}) custom-call(s32[2]{0:T(128)S(1)} %pad_add_fusion.where, f32[5,512,128]{2,1,0:T(8,128)S(1)} %collective-permute-done.1.refs_0_, f32[2,256,1280]{2,1,0:T(8,128)S(1)} %get-tuple-element.12.refs_1_, ...), custom_call_target="tpu_custom_call" | custom-call | flops 503316480 | bytes 11403264 | tf_op jit(solution)/shard_map/pallas_call | solution.py:222
  35.2 2.1 %collective-permute-start.6 = (f32[256,128]{1,0:T(8,128)S(1)}, f32[256,128]{1,0:T(8,128)S(1)}, u32[]{:S(2)}, u32[]{:S(2)}) collective-permute-start(f32[256,128]{1,0:T(8,128)S(1)} %get-tuple-element.21), channel_id=1, source_target_pairs={{0,16},{16,0},{1,17},{17,1},{2,18},{18,2},{3,19},{19,3},{4,20},{20... | collective-permute-start | bytes 393224 | tf_op jit(solution)/shard_map/ppermute | solution.py:264
  37.3 0.1 collective-permute-start.5
  37.4 1.7 %collective-permute-done.refs_1_ = f32[512,128]{1,0:T(8,128)S(1)} collective-permute-done((f32[512,128]{1,0:T(8,128)}, f32[512,128]{1,0:T(8,128)S(1)}, u32[]{:S(2)}, u32[]{:S(2)}) %collective-permute-start) | collective-permute-done | bytes 262176 | tf_op jit(solution)/shard_map/ppermute | solution.py:261
  39.1 0.0 copy-done.3
  39.1 0.0 copy-done.4
  39.1 3.9 %shard_map.117 = f32[5,512,128]{2,1,0:T(8,128)} custom-call(s32[2]{0:T(128)S(1)} %pad_add_fusion.where, f32[512,128]{1,0:T(8,128)S(1)} %bitcast.12, f32[512,128]{1,0:T(8,128)S(1)} %collective-permute-done.refs_1_, f32[2,256,1280]{2,1,0:T(8,128)S(1)} %get-tuple-element.17.refs_2_, f32[5,512,128]{2,1,0:T(8,128)S(1)} %shard_map.115.refs_4_.refs_3_, ...), custom_call_target="tpu_custom_call" | custom-call | flops 503316480 | bytes 6160484 | tf_op jit(solution)/shard_map/pallas_call | solution.py:222
  42.9 0.0 collective-permute-done.6.refs_1_
  42.9 0.7 %shard_map.118.refs_2_ = f32[512,128]{1,0:T(8,128)} custom-call(f32[256,128]{1,0:T(8,128)S(1)} %get-tuple-element.20.refs_0_, f32[256,128]{1,0:T(8,128)S(1)} %collective-permute-done.6.refs_1_), custom_call_target="tpu_custom_call" | custom-call | tf_op jit(solution)/shard_map/pallas_call | solution.py:345
  43.6 0.2 collective-permute-done.5.refs_1_
  43.9 0.7 %shard_map.119 = f32[512,128]{1,0:T(8,128)} custom-call(f32[256,128]{1,0:T(8,128)S(1)} %get-tuple-element.18.refs_0_, f32[256,128]{1,0:T(8,128)S(1)} %collective-permute-done.5.refs_1_, f32[512,128]{1,0:T(8,128)} %shard_map.118.refs_2_), custom_call_target="tpu_custom_call", output_to_operand_aliasing={{}: (2, {})} | custom-call | tf_op jit(solution)/shard_map/pallas_call | solution.py:345
Async XLA Ops:
  0.6 32.8 %collective-permute-start.1 = (f32[5,512,128]{2,1,0:T(8,128)}, f32[5,512,128]{2,1,0:T(8,128)S(1)}, u32[]{:S(2)}, u32[]{:S(2)}) collective-permute-start(f32[5,512,128]{2,1,0:T(8,128)} %bitcast.7), channel_id=1, source_target_pairs={{16,0},{0,16},{17,1},{1,17},{18,2},{2,18},{19,3},{3,19},{20,4},{4,... | collective-permute-start | bytes 3932168 | tf_op jit(solution)/shard_map/ppermute | solution.py:261
  3.6 1.4 %copy-start = (f32[5,128,4,128]{3,2,1,0:T(4,128)S(1)}, f32[5,128,4,128]{3,2,1,0:T(4,128)}, u32[]{:S(2)}) copy-start(f32[5,128,4,128]{3,2,1,0:T(4,128)} %param.10) | copy-start | bytes 3932164
  5.0 6.6 %copy-start.1 = (f32[5,128,4,128]{3,2,1,0:T(4,128)S(1)}, f32[5,128,4,128]{3,2,1,0:T(4,128)}, u32[]{:S(2)}) copy-start(f32[5,128,4,128]{3,2,1,0:T(4,128)} %param.10) | copy-start | bytes 3932164
  5.0 6.6 %copy-start.8 = (f32[5,5]{1,0:T(8,128)S(1)}, f32[5,5]{1,0:T(8,128)}, u32[]{:S(2)}) copy-start(f32[5,5]{1,0:T(8,128)} %refs_4_.1) | copy-start | bytes 304
  6.1 17.4 %collective-permute-start.2 = (f32[5,128,128]{2,1,0:T(8,128)}, f32[5,128,128]{2,1,0:T(8,128)S(1)}, u32[]{:S(2)}, u32[]{:S(2)}) collective-permute-start(f32[5,128,128]{2,1,0:T(8,128)} %get-tuple-element.14), channel_id=1, source_target_pairs={{0,2},{2,4},{4,6},{6,8},{8,10},{10,12},{12,14},{1,3},{3,5},{5,7},{... | collective-permute-start | bytes 983048 | tf_op jit(solution)/shard_map/ppermute | solution.py:276
  9.5 14.0 %collective-permute-start.3 = (f32[5,128,128]{2,1,0:T(8,128)}, f32[5,128,128]{2,1,0:T(8,128)S(1)}, u32[]{:S(2)}, u32[]{:S(2)}) collective-permute-start(f32[5,128,128]{2,1,0:T(8,128)} %get-tuple-element.15), channel_id=1, source_target_pairs={{2,0},{4,2},{6,4},{8,6},{10,8},{12,10},{14,12},{3,1},{5,3},{7,5},{... | collective-permute-start | bytes 983048 | tf_op jit(solution)/shard_map/ppermute | solution.py:277
  10.8 6.2 %collective-permute-start.4 = (f32[128,128]{1,0:T(8,128)}, f32[128,128]{1,0:T(8,128)}, u32[]{:S(2)}, u32[]{:S(2)}) collective-permute-start(f32[128,128]{1,0:T(8,128)} %get-tuple-element.16), channel_id=1, source_target_pairs={{0,1},{1,0},{2,3},{3,2},{4,5},{5,4},{6,7},{7,6},{8,9},{9,8},{10,11... | collective-permute-start | bytes 196616 | tf_op jit(solution)/shard_map/ppermute | solution.py:279
  10.9 28.2 %collective-permute-start = (f32[512,128]{1,0:T(8,128)}, f32[512,128]{1,0:T(8,128)S(1)}, u32[]{:S(2)}, u32[]{:S(2)}) collective-permute-start(f32[512,128]{1,0:T(8,128)} %bitcast.11), channel_id=1, source_target_pairs={{16,0},{0,16},{17,1},{1,17},{18,2},{2,18},{19,3},{3,19},{20,4},{4,... | collective-permute-start | bytes 786440 | tf_op jit(solution)/shard_map/ppermute | solution.py:261
  11.6 1.3 %copy-start.9 = (f32[5,128,4,128]{3,2,1,0:T(4,128)S(1)}, f32[5,128,4,128]{3,2,1,0:T(4,128)}, u32[]{:S(2)}) copy-start(f32[5,128,4,128]{3,2,1,0:T(4,128)} %param.11) | copy-start | bytes 3932164
  12.9 1.0 %copy-start.10 = (bf16[2,256,384]{2,1,0:T(8,128)(2,1)S(1)}, bf16[2,256,384]{2,1,0:T(8,128)(2,1)}, u32[]{:S(2)}) copy-start(bf16[2,256,384]{2,1,0:T(8,128)(2,1)} %constant.14.clone.table) | copy-start | bytes 1179652
  13.9 9.6 %copy-start.5 = (f32[5,5]{1,0:T(8,128)S(1)}, f32[5,5]{1,0:T(8,128)}, u32[]{:S(2)}) copy-start(f32[5,5]{1,0:T(8,128)} %jac_axial.1) | copy-start | bytes 304
  13.9 9.6 %copy-start.6 = (f32[5,5]{1,0:T(8,128)S(1)}, f32[5,5]{1,0:T(8,128)}, u32[]{:S(2)}) copy-start(f32[5,5]{1,0:T(8,128)} %jac_radial.1) | copy-start | bytes 304
  13.9 9.6 %copy-start.7 = (f32[5,5]{1,0:T(8,128)S(1)}, f32[5,5]{1,0:T(8,128)}, u32[]{:S(2)}) copy-start(f32[5,5]{1,0:T(8,128)} %jac_swirl.1) | copy-start | bytes 304
  17.0 16.4 %copy-start.2 = (bf16[2,1,256,384]{3,2,1,0:T(8,128)(2,1)S(1)}, bf16[2,1,256,384]{3,2,1,0:T(8,128)(2,1)}, u32[]{:S(2)}) copy-start(bf16[2,1,256,384]{3,2,1,0:T(8,128)(2,1)} %constant.15.clone.refs_3_) | copy-start | bytes 1179652
  33.5 5.6 %copy-start.3 = (bf16[2,128,768]{2,1,0:T(8,128)(2,1)S(1)}, bf16[2,128,768]{2,1,0:T(8,128)(2,1)}, u32[]{:S(2)}) copy-start(bf16[2,128,768]{2,1,0:T(8,128)(2,1)} %constant.16.clone.refs_5_) | copy-start | bytes 1179652
  33.5 5.6 %copy-start.4 = (f32[128,4,128]{2,1,0:T(4,128)S(1)}, f32[128,4,128]{2,1,0:T(4,128)}, u32[]{:S(2)}) copy-start(f32[128,4,128]{2,1,0:T(4,128)} %param.12) | copy-start | bytes 786436
  35.2 7.8 %collective-permute-start.6 = (f32[256,128]{1,0:T(8,128)S(1)}, f32[256,128]{1,0:T(8,128)S(1)}, u32[]{:S(2)}, u32[]{:S(2)}) collective-permute-start(f32[256,128]{1,0:T(8,128)S(1)} %get-tuple-element.21), channel_id=1, source_target_pairs={{0,16},{16,0},{1,17},{17,1},{2,18},{18,2},{3,19},{19,3},{4,20},{20... | collective-permute-start | bytes 393224 | tf_op jit(solution)/shard_map/ppermute | solution.py:264
  37.3 6.6 %collective-permute-start.5 = (f32[256,128]{1,0:T(8,128)S(1)}, f32[256,128]{1,0:T(8,128)S(1)}, u32[]{:S(2)}, u32[]{:S(2)}) collective-permute-start(f32[256,128]{1,0:T(8,128)S(1)} %get-tuple-element.19), channel_id=1, source_target_pairs={{0,16},{16,0},{1,17},{17,1},{2,18},{18,2},{3,19},{19,3},{4,20},{20... | collective-permute-start | bytes 393224 | tf_op jit(solution)/shard_map/ppermute | solution.py:264

commit v7 on v6

--- a/solution.py
+++ b/solution.py
@@ -117,11 +117,20 @@
             h_out[s * pieces + k][rows, :] = part
 
 
-def total_kernel(terms, *refs):
+def sum_kernel(*refs):
     total = refs[0][...]
-    for ref in refs[1:terms]:
+    for ref in refs[1:-1]:
         total = total + ref[...]
-    refs[-1][...] = -total
+    refs[-1][...] = total
+
+
+def total_kernel(cut, *refs):
+    out = refs[-1]
+    out[pl.ds(0, cut), :] = -refs[0][...]
+    total = refs[1][...]
+    for ref in refs[2:-1]:
+        total = total + ref[...]
+    out[pl.ds(cut, out.shape[0] - cut), :] = -total
 
 
 def back_kernel(dims, groups, where, *refs):
@@ -312,7 +321,7 @@
         32 * fields * fields * rows * lanes,
     )[0]
 
-    cuts = (0, modes // 2, modes)
+    cuts = (0, modes * 3 // 4 // 8 * 8, modes)
     pieces = len(cuts) - 1
     piece_rows = [(cuts[k + 1] - cuts[k]) * cells_ax for k in range(pieces)]
     joined = call(
@@ -327,7 +336,12 @@
     )
     a_all = joined[0]
     parts = [joined[1 + k :: pieces] for k in range(pieces)]
-    arrived = [[deliver(part[s], s) for s in range(1, groups)] for part in parts]
+    arrived = [[deliver(part[s], s) for s in range(1, groups)] for part in parts[:1]]
+    if groups == 2 and rad_size == 2:
+        sibling = lax.ppermute(parts[1][1], "rad", [(0, 1), (1, 0)])
+        arrived.append([lax.ppermute(sibling, ("mode", "rad"), [(i, 3 - i) for i in range(4)])])
+    else:
+        arrived.append([deliver(parts[1][s], s) for s in range(1, groups)])
 
     adjoint_in = call(
         functools.partial(back_kernel, dims, groups), steps, where,
@@ -339,19 +353,16 @@
         own_flops // 2,
     )[0]
 
-    wake_grad = None
-    for k in range(pieces):
-        size, place = piece_rows[k], cuts[k] * cells_ax
-        wake_grad = pl.pallas_call(
-            functools.partial(total_kernel, groups),
-            grid=(1,),
-            out_shape=plane,
-            in_specs=[pl.BlockSpec((size, lanes), lambda i: (0, 0))] * groups
-            + ([] if wake_grad is None else [ANY]),
-            out_specs=pl.BlockSpec((size, lanes), lambda i, at=place // size: (at, 0)),
-            input_output_aliases={} if wake_grad is None else {groups: 0},
-            compiler_params=pltpu.CompilerParams(vmem_limit_bytes=VMEM_LIMIT),
-        )(parts[k][0], *arrived[k], *([] if wake_grad is None else [wake_grad]))
+    early = pl.pallas_call(
+        sum_kernel,
+        out_shape=jax.ShapeDtypeStruct(parts[0][0].shape, f32),
+        compiler_params=pltpu.CompilerParams(vmem_limit_bytes=VMEM_LIMIT),
+    )(parts[0][0], *arrived[0])
+    wake_grad = pl.pallas_call(
+        functools.partial(total_kernel, piece_rows[0]),
+        out_shape=plane,
+        compiler_params=pltpu.CompilerParams(vmem_limit_bytes=VMEM_LIMIT),
+    )(early, parts[1][0], *arrived[1])
     return (
         adjoint_in.reshape(adjoint.shape),
         wake_grad.reshape(wake.shape),

time: 44.8 us -> 44.3 us (0.989)
  Pallas kernels: 15.3 us -> 14.7 us
    ppermute x0 -> x2, waiting for transfers between devices: none -> 1.25 us  [the longest x1 1.25 us: body(): sibling = lax.ppermute(parts[1][1], 'rad', [(0, 1), (1, 0)])]
    ppermute x2, waiting for transfers between devices: 7.44 us -> 6.26 us  [fetch(): lax.ppermute(value, 'mode', [((i + s) % groups, i) for i in range(groups)])]
    pallas_call x2, Pallas kernels: 1.34 us -> 0.75 us  [the longest x1 0.73 us: body(): pl.pallas_call(functools.partial(total_kernel, piece_rows[0]), out_shape=...]
    ppermute x2 -> x1, starting transfers between devices: 2.2 us -> 2.12 us  [deliver(): lax.ppermute(value, 'mode', [(i, (i + s) % groups) for i in range(groups)])]
  transfers between devices with their start and end apart: 7 -> 8, of which waited for: 4 -> 5; matrix products, arithmetic and copies ran while one was open for 0% -> 0% of each run, Pallas kernels for 33% -> 32%
where the time goes in v7:
time: 44.3 us; the launch traced here: 43.9 us
  Pallas kernels  14.7 us (33%)
  waiting for transfers between devices  14.2 us (32%)
  starting transfers between devices  10.5 us (24%)
  local copies, waits for them, and re-layouts  3.69 us (8%)
  between operations  0.73 us (2%)
    pallas_call x4, Pallas kernels, call(): pl.pallas_call(kernel, grid_spec=pltpu.PrefetchScalarGridSpec(num_scalar_...  12.9 us
    ppermute x1, waiting for transfers between devices, body(): below = lax.ppermute(last, 'ax', up)  6.45 us
    ppermute x2, waiting for transfers between devices, fetch(): lax.ppermute(value, 'mode', [((i + s) % groups, i) for i in range(groups)])  6.26 us
    unnamed x22, local copies, waits for them, and re-layouts  3.69 us
    ppermute x2, starting transfers between devices, fetch(): lax.ppermute(value, 'mode', [((i + s) % groups, i) for i in range(groups)])  3.6 us
    ppermute x1, starting transfers between devices, body(): below = lax.ppermute(last, 'ax', up)  3.43 us
    ppermute x1, starting transfers between devices, deliver(): lax.ppermute(value, 'mode', [(i, (i + s) % groups) for i in range(groups)])  2.12 us
    ppermute x1, starting transfers between devices, body(): above = lax.ppermute(first, 'ax', down)  1.29 us
  transfers between devices with their start and end apart: 8, of which 5 were waited for; matrix products, arithmetic and copies ran while one was open for 0% of the time, Pallas kernels for 32%

profile of v7, /device:TPU:0, one launch (start us, length us, event | category | flops | bytes accessed | tf_op | source)
XLA Modules:
  0.0 43.9 jit_solution(13474254303019511473)
XLA Ops:
  0.6 3.0 %collective-permute-start.1 = (f32[5,512,128]{2,1,0:T(8,128)}, f32[5,512,128]{2,1,0:T(8,128)S(1)}, u32[]{:S(2)}, u32[]{:S(2)}) collective-permute-start(f32[5,512,128]{2,1,0:T(8,128)} %bitcast.7), channel_id=1, source_target_pairs={{16,0},{0,16},{17,1},{1,17},{18,2},{2,18},{19,3},{3,19},{20,4},{4,... | collective-permute-start | bytes 3932168 | tf_op jit(solution)/shard_map/ppermute | solution.py:270
  3.6 0.0 copy-start
  3.6 1.3 %copy-done = f32[5,128,4,128]{3,2,1,0:T(4,128)S(1)} copy-done((f32[5,128,4,128]{3,2,1,0:T(4,128)S(1)}, f32[5,128,4,128]{3,2,1,0:T(4,128)}, u32[]{:S(2)}) %copy-start) | copy-done | bytes 1310744
  5.0 0.0 copy-start.1
  5.0 0.0 copy-start.8
  5.0 1.1 %shard_map.114 = (f32[5,128,128]{2,1,0:T(8,128)}, f32[5,128,128]{2,1,0:T(8,128)}, f32[128,128]{1,0:T(8,128)}) custom-call(f32[5,512,128]{2,1,0:T(8,128)S(1)} %bitcast.8), custom_call_target="tpu_custom_call" | custom-call | tf_op jit(solution)/shard_map/pallas_call | solution.py:280
  6.1 3.4 %collective-permute-start.2 = (f32[5,128,128]{2,1,0:T(8,128)}, f32[5,128,128]{2,1,0:T(8,128)S(1)}, u32[]{:S(2)}, u32[]{:S(2)}) collective-permute-start(f32[5,128,128]{2,1,0:T(8,128)} %get-tuple-element.14), channel_id=1, source_target_pairs={{0,2},{2,4},{4,6},{6,8},{8,10},{10,12},{12,14},{1,3},{3,5},{5,7},{... | collective-permute-start | bytes 983048 | tf_op jit(solution)/shard_map/ppermute | solution.py:285
  9.5 1.3 %collective-permute-start.3 = (f32[5,128,128]{2,1,0:T(8,128)}, f32[5,128,128]{2,1,0:T(8,128)S(1)}, u32[]{:S(2)}, u32[]{:S(2)}) collective-permute-start(f32[5,128,128]{2,1,0:T(8,128)} %get-tuple-element.15), channel_id=1, source_target_pairs={{2,0},{4,2},{6,4},{8,6},{10,8},{12,10},{14,12},{3,1},{5,3},{7,5},{... | collective-permute-start | bytes 983048 | tf_op jit(solution)/shard_map/ppermute | solution.py:286
  10.8 0.1 collective-permute-start.4
  10.9 0.6 %collective-permute-start = (f32[512,128]{1,0:T(8,128)}, f32[512,128]{1,0:T(8,128)S(1)}, u32[]{:S(2)}, u32[]{:S(2)}) collective-permute-start(f32[512,128]{1,0:T(8,128)} %bitcast.11), channel_id=1, source_target_pairs={{16,0},{0,16},{17,1},{1,17},{18,2},{2,18},{19,3},{3,19},{20,4},{4,... | collective-permute-start | bytes 786440 | tf_op jit(solution)/shard_map/ppermute | solution.py:270
  11.5 0.1 pad_add_fusion.where
  11.5 0.0 copy-done.1
  11.6 0.0 copy-done.8
  11.6 0.0 copy-start.9
  11.6 1.3 %copy-done.9 = f32[5,128,4,128]{3,2,1,0:T(4,128)S(1)} copy-done((f32[5,128,4,128]{3,2,1,0:T(4,128)S(1)}, f32[5,128,4,128]{3,2,1,0:T(4,128)}, u32[]{:S(2)}) %copy-start.9) | copy-done | bytes 1310744
  12.9 0.0 copy-start.10
  12.9 1.0 %copy-done.10 = bf16[2,256,384]{2,1,0:T(8,128)(2,1)S(1)} copy-done((bf16[2,256,384]{2,1,0:T(8,128)(2,1)S(1)}, bf16[2,256,384]{2,1,0:T(8,128)(2,1)}, u32[]{:S(2)}) %copy-start.10) | copy-done | bytes 393240
  13.9 0.0 copy-start.5
  13.9 0.0 copy-start.6
  13.9 0.0 copy-start.7
  13.9 3.1 %shard_map.113 = (f32[2,256,1280]{2,1,0:T(8,128)S(1)}, f32[2,256,1280]{2,1,0:T(8,128)S(1)}) custom-call(s32[2]{0:T(128)S(1)} %pad_add_fusion.where, f32[5,512,128]{2,1,0:T(8,128)S(1)} %bitcast.9, f32[5,512,128]{2,1,0:T(8,128)S(1)} %bitcast.13, f32[5,5]{1,0:T(8,128)S(1)} %copy-done.8, bf16[2,256,384]{2,1,0:T(8,128)(2,1)S(1)} %copy-done.10), custom_call_target="tpu_custom_call" | custom-call | flops 1006632960 | bytes 8257636 | tf_op jit(solution)/shard_map/pallas_call | solution.py:231
  17.0 0.0 copy-start.2
  17.0 0.0 collective-permute-done.4.inner.outer
  17.0 6.5 %collective-permute-done.2.below = f32[5,128,128]{2,1,0:T(8,128)S(1)} collective-permute-done((f32[5,128,128]{2,1,0:T(8,128)}, f32[5,128,128]{2,1,0:T(8,128)S(1)}, u32[]{:S(2)}, u32[]{:S(2)}) %collective-permute-start.2) | collective-permute-done | bytes 327712 | tf_op jit(solution)/shard_map/ppermute | solution.py:285
  23.5 0.0 collective-permute-done.3.above
  23.5 0.0 copy-done.5
  23.5 0.0 copy-done.6
  23.5 0.0 copy-done.7
  23.5 4.2 %shard_map.115.refs_4_.refs_3_ = f32[5,512,128]{2,1,0:T(8,128)S(1)} custom-call(s32[2]{0:T(128)S(1)} %pad_add_fusion.where, f32[5,512,128]{2,1,0:T(8,128)S(1)} %bitcast.10, f32[5,128,128]{2,1,0:T(8,128)S(1)} %collective-permute-done.2.below, f32[5,128,128]{2,1,0:T(8,128)S(1)} %collective-permute-done.3.above, f32[128,128]{1,0:T(8,128)} %collective-permute-done.4.inner.outer, ...), custom_call_target="tpu_custom_call" | custom-call | flops 52428800 | bytes 3408172 | tf_op jit(solution)/shard_map/pallas_call | solution.py:231
  27.7 5.7 %collective-permute-done.1.refs_0_ = f32[5,512,128]{2,1,0:T(8,128)S(1)} collective-permute-done((f32[5,512,128]{2,1,0:T(8,128)}, f32[5,512,128]{2,1,0:T(8,128)S(1)}, u32[]{:S(2)}, u32[]{:S(2)}) %collective-permute-start.1) | collective-permute-done | bytes 1310752 | tf_op jit(solution)/shard_map/ppermute | solution.py:270
  33.4 0.0 copy-done.2
  33.5 0.0 copy-start.3
  33.5 0.0 copy-start.4
  33.5 1.7 %shard_map.116 = (f32[2,256,1280]{2,1,0:T(8,128)S(1)}, f32[384,128]{1,0:T(8,128)S(1)}, f32[128,128]{1,0:T(8,128)S(1)}, f32[384,128]{1,0:T(8,128)S(1)}, f32[128,128]{1,0:T(8,128)S(1)}) custom-call(s32[2]{0:T(128)S(1)} %pad_add_fusion.where, f32[5,512,128]{2,1,0:T(8,128)S(1)} %collective-permute-done.1.refs_0_, f32[2,256,1280]{2,1,0:T(8,128)S(1)} %get-tuple-element.12.refs_1_, ...), custom_call_target="tpu_custom_call" | custom-call | flops 503316480 | bytes 11403264 | tf_op jit(solution)/shard_map/pallas_call | solution.py:231
  35.2 2.1 %collective-permute-start.5 = (f32[384,128]{1,0:T(8,128)S(1)}, f32[384,128]{1,0:T(8,128)S(1)}, u32[]{:S(2)}, u32[]{:S(2)}) collective-permute-start(f32[384,128]{1,0:T(8,128)S(1)} %get-tuple-element.19), channel_id=1, source_target_pairs={{0,16},{16,0},{1,17},{17,1},{2,18},{18,2},{3,19},{19,3},{4,20},{20... | collective-permute-start | bytes 589832 | tf_op jit(solution)/shard_map/ppermute | solution.py:273
  37.3 0.0 collective-permute-start.6
  37.3 1.3 %collective-permute-done.6 = f32[128,128]{1,0:T(8,128)S(1)} collective-permute-done((f32[128,128]{1,0:T(8,128)S(1)}, f32[128,128]{1,0:T(8,128)S(1)}, u32[]{:S(2)}, u32[]{:S(2)}) %collective-permute-start.6) | collective-permute-done | bytes 65568 | tf_op jit(solution)/shard_map/ppermute | solution.py:341
  38.5 0.0 collective-permute-start.7
  38.5 0.5 %collective-permute-done.refs_1_ = f32[512,128]{1,0:T(8,128)S(1)} collective-permute-done((f32[512,128]{1,0:T(8,128)}, f32[512,128]{1,0:T(8,128)S(1)}, u32[]{:S(2)}, u32[]{:S(2)}) %collective-permute-start) | collective-permute-done | bytes 262176 | tf_op jit(solution)/shard_map/ppermute | solution.py:270
  39.1 0.0 copy-done.3
  39.1 0.0 copy-done.4
  39.1 3.9 %shard_map.117 = f32[5,512,128]{2,1,0:T(8,128)} custom-call(s32[2]{0:T(128)S(1)} %pad_add_fusion.where, f32[512,128]{1,0:T(8,128)S(1)} %bitcast.12, f32[512,128]{1,0:T(8,128)S(1)} %collective-permute-done.refs_1_, f32[2,256,1280]{2,1,0:T(8,128)S(1)} %get-tuple-element.17.refs_2_, f32[5,512,128]{2,1,0:T(8,128)S(1)} %shard_map.115.refs_4_.refs_3_, ...), custom_call_target="tpu_custom_call" | custom-call | flops 503316480 | bytes 6160484 | tf_op jit(solution)/shard_map/pallas_call | solution.py:231
  42.9 0.2 collective-permute-done.5.refs_1_
  43.2 0.0 collective-permute-done.7.refs_2_
  43.2 0.7 %shard_map.119 = f32[512,128]{1,0:T(8,128)} custom-call(f32[384,128]{1,0:T(8,128)S(1)} %shard_map.118.refs_0_, f32[128,128]{1,0:T(8,128)S(1)} %get-tuple-element.20.refs_1_, f32[128,128]{1,0:T(8,128)S(1)} %collective-permute-done.7.refs_2_), custom_call_target="tpu_custom_call" | custom-call | tf_op jit(solution)/shard_map/pallas_call | solution.py:361
  (1 shorter events, 0.0 us)
Async XLA Ops:
  0.6 32.8 %collective-permute-start.1 = (f32[5,512,128]{2,1,0:T(8,128)}, f32[5,512,128]{2,1,0:T(8,128)S(1)}, u32[]{:S(2)}, u32[]{:S(2)}) collective-permute-start(f32[5,512,128]{2,1,0:T(8,128)} %bitcast.7), channel_id=1, source_target_pairs={{16,0},{0,16},{17,1},{1,17},{18,2},{2,18},{19,3},{3,19},{20,4},{4,... | collective-permute-start | bytes 3932168 | tf_op jit(solution)/shard_map/ppermute | solution.py:270
  3.6 1.4 %copy-start = (f32[5,128,4,128]{3,2,1,0:T(4,128)S(1)}, f32[5,128,4,128]{3,2,1,0:T(4,128)}, u32[]{:S(2)}) copy-start(f32[5,128,4,128]{3,2,1,0:T(4,128)} %param.10) | copy-start | bytes 3932164
  5.0 6.6 %copy-start.1 = (f32[5,128,4,128]{3,2,1,0:T(4,128)S(1)}, f32[5,128,4,128]{3,2,1,0:T(4,128)}, u32[]{:S(2)}) copy-start(f32[5,128,4,128]{3,2,1,0:T(4,128)} %param.10) | copy-start | bytes 3932164
  5.0 6.6 %copy-start.8 = (f32[5,5]{1,0:T(8,128)S(1)}, f32[5,5]{1,0:T(8,128)}, u32[]{:S(2)}) copy-start(f32[5,5]{1,0:T(8,128)} %refs_4_.1) | copy-start | bytes 304
  6.1 17.4 %collective-permute-start.2 = (f32[5,128,128]{2,1,0:T(8,128)}, f32[5,128,128]{2,1,0:T(8,128)S(1)}, u32[]{:S(2)}, u32[]{:S(2)}) collective-permute-start(f32[5,128,128]{2,1,0:T(8,128)} %get-tuple-element.14), channel_id=1, source_target_pairs={{0,2},{2,4},{4,6},{6,8},{8,10},{10,12},{12,14},{1,3},{3,5},{5,7},{... | collective-permute-start | bytes 983048 | tf_op jit(solution)/shard_map/ppermute | solution.py:285
  9.5 14.0 %collective-permute-start.3 = (f32[5,128,128]{2,1,0:T(8,128)}, f32[5,128,128]{2,1,0:T(8,128)S(1)}, u32[]{:S(2)}, u32[]{:S(2)}) collective-permute-start(f32[5,128,128]{2,1,0:T(8,128)} %get-tuple-element.15), channel_id=1, source_target_pairs={{2,0},{4,2},{6,4},{8,6},{10,8},{12,10},{14,12},{3,1},{5,3},{7,5},{... | collective-permute-start | bytes 983048 | tf_op jit(solution)/shard_map/ppermute | solution.py:286
  10.8 6.2 %collective-permute-start.4 = (f32[128,128]{1,0:T(8,128)}, f32[128,128]{1,0:T(8,128)}, u32[]{:S(2)}, u32[]{:S(2)}) collective-permute-start(f32[128,128]{1,0:T(8,128)} %get-tuple-element.16), channel_id=1, source_target_pairs={{0,1},{1,0},{2,3},{3,2},{4,5},{5,4},{6,7},{7,6},{8,9},{9,8},{10,11... | collective-permute-start | bytes 196616 | tf_op jit(solution)/shard_map/ppermute | solution.py:288
  10.9 28.2 %collective-permute-start = (f32[512,128]{1,0:T(8,128)}, f32[512,128]{1,0:T(8,128)S(1)}, u32[]{:S(2)}, u32[]{:S(2)}) collective-permute-start(f32[512,128]{1,0:T(8,128)} %bitcast.11), channel_id=1, source_target_pairs={{16,0},{0,16},{17,1},{1,17},{18,2},{2,18},{19,3},{3,19},{20,4},{4,... | collective-permute-start | bytes 786440 | tf_op jit(solution)/shard_map/ppermute | solution.py:270
  11.6 1.3 %copy-start.9 = (f32[5,128,4,128]{3,2,1,0:T(4,128)S(1)}, f32[5,128,4,128]{3,2,1,0:T(4,128)}, u32[]{:S(2)}) copy-start(f32[5,128,4,128]{3,2,1,0:T(4,128)} %param.11) | copy-start | bytes 3932164
  12.9 1.0 %copy-start.10 = (bf16[2,256,384]{2,1,0:T(8,128)(2,1)S(1)}, bf16[2,256,384]{2,1,0:T(8,128)(2,1)}, u32[]{:S(2)}) copy-start(bf16[2,256,384]{2,1,0:T(8,128)(2,1)} %constant.14.clone.table) | copy-start | bytes 1179652
  13.9 9.6 %copy-start.5 = (f32[5,5]{1,0:T(8,128)S(1)}, f32[5,5]{1,0:T(8,128)}, u32[]{:S(2)}) copy-start(f32[5,5]{1,0:T(8,128)} %jac_axial.1) | copy-start | bytes 304
  13.9 9.6 %copy-start.6 = (f32[5,5]{1,0:T(8,128)S(1)}, f32[5,5]{1,0:T(8,128)}, u32[]{:S(2)}) copy-start(f32[5,5]{1,0:T(8,128)} %jac_radial.1) | copy-start | bytes 304
  13.9 9.6 %copy-start.7 = (f32[5,5]{1,0:T(8,128)S(1)}, f32[5,5]{1,0:T(8,128)}, u32[]{:S(2)}) copy-start(f32[5,5]{1,0:T(8,128)} %jac_swirl.1) | copy-start | bytes 304
  17.0 16.4 %copy-start.2 = (bf16[2,1,256,384]{3,2,1,0:T(8,128)(2,1)S(1)}, bf16[2,1,256,384]{3,2,1,0:T(8,128)(2,1)}, u32[]{:S(2)}) copy-start(bf16[2,1,256,384]{3,2,1,0:T(8,128)(2,1)} %constant.15.clone.refs_3_) | copy-start | bytes 1179652
  33.5 5.6 %copy-start.3 = (bf16[2,128,768]{2,1,0:T(8,128)(2,1)S(1)}, bf16[2,128,768]{2,1,0:T(8,128)(2,1)}, u32[]{:S(2)}) copy-start(bf16[2,128,768]{2,1,0:T(8,128)(2,1)} %constant.16.clone.refs_5_) | copy-start | bytes 1179652
  33.5 5.6 %copy-start.4 = (f32[128,4,128]{2,1,0:T(4,128)S(1)}, f32[128,4,128]{2,1,0:T(4,128)}, u32[]{:S(2)}) copy-start(f32[128,4,128]{2,1,0:T(4,128)} %param.12) | copy-start | bytes 786436
  35.2 8.0 %collective-permute-start.5 = (f32[384,128]{1,0:T(8,128)S(1)}, f32[384,128]{1,0:T(8,128)S(1)}, u32[]{:S(2)}, u32[]{:S(2)}) collective-permute-start(f32[384,128]{1,0:T(8,128)S(1)} %get-tuple-element.19), channel_id=1, source_target_pairs={{0,16},{16,0},{1,17},{17,1},{2,18},{18,2},{3,19},{19,3},{4,20},{20... | collective-permute-start | bytes 589832 | tf_op jit(solution)/shard_map/ppermute | solution.py:273
  37.3 1.3 %collective-permute-start.6 = (f32[128,128]{1,0:T(8,128)S(1)}, f32[128,128]{1,0:T(8,128)S(1)}, u32[]{:S(2)}, u32[]{:S(2)}) collective-permute-start(f32[128,128]{1,0:T(8,128)S(1)} %get-tuple-element.21), channel_id=1, source_target_pairs={{0,1},{1,0},{2,3},{3,2},{4,5},{5,4},{6,7},{7,6},{8,9},{9,8},{10,11... | collective-permute-start | bytes 196616 | tf_op jit(solution)/shard_map/ppermute | solution.py:341
  38.5 4.6 %collective-permute-start.7 = (f32[128,128]{1,0:T(8,128)S(1)}, f32[128,128]{1,0:T(8,128)S(1)}, u32[]{:S(2)}, u32[]{:S(2)}) collective-permute-start(f32[128,128]{1,0:T(8,128)S(1)} %collective-permute-done.6), channel_id=1, source_target_pairs={{0,17},{1,16},{16,1},{17,0},{2,19},{3,18},{18,3},{19,2},{4,21},{5,... | collective-permute-start | bytes 196616 | tf_op jit(solution)/shard_map/ppermute | solution.py:342

commit v8 on v7

--- a/solution.py
+++ b/solution.py
@@ -27,6 +27,12 @@
     high = table.astype(ml_dtypes.bfloat16)
     low = (table - high.astype(np.float32)).astype(ml_dtypes.bfloat16)
     return np.concatenate([high, low, high], axis=-1)
+
+
+def two_terms(table):
+    high = table.astype(ml_dtypes.bfloat16)
+    low = (table - high.astype(np.float32)).astype(ml_dtypes.bfloat16)
+    return np.concatenate([high, low], axis=0)
 
 
 def tables(groups, modes_here):
@@ -38,7 +44,7 @@
         blocks = [rolled[:, s * modes_here : (s + 1) * modes_here] for s in range(groups)]
         own.append(three_terms(blocks[0]))
         other.append(np.stack([three_terms(block) for block in blocks[1:]]))
-        back.append(three_terms(np.ascontiguousarray(blocks[0].T)))
+        back.append(two_terms(np.ascontiguousarray(blocks[0].T)))
     return np.stack(own), np.stack(other), np.stack(back)
 
 
@@ -117,22 +123,6 @@
             h_out[s * pieces + k][rows, :] = part
 
 
-def sum_kernel(*refs):
-    total = refs[0][...]
-    for ref in refs[1:-1]:
-        total = total + ref[...]
-    refs[-1][...] = total
-
-
-def total_kernel(cut, *refs):
-    out = refs[-1]
-    out[pl.ds(0, cut), :] = -refs[0][...]
-    total = refs[1][...]
-    for ref in refs[2:-1]:
-        total = total + ref[...]
-    out[pl.ds(cut, out.shape[0] - cut), :] = -total
-
-
 def back_kernel(dims, groups, where, *refs):
     fields, modes, cells_ax, width, cols_of = dims
     wakes = refs[:groups]
@@ -145,8 +135,14 @@
             wake = wakes[s][rows, :]
             for f in range(fields):
                 scaled = wake * angle[0, pl.ds(s * modes, modes), cols_of(j, f)]
-                put_split(terms, s * modes, modes, count, cols_of(j, f), scaled)
-    returned = jnp.dot(table[0], terms[...], preferred_element_type=jnp.float32)
+                high, low = split(scaled)
+                terms[pl.ds(s * modes, modes), cols_of(j, f)] = high
+                terms[pl.ds(count + s * modes, modes), cols_of(j, f)] = low
+    both = jnp.dot(table[0], terms[pl.ds(0, count), :], preferred_element_type=jnp.float32)
+    rest = jnp.dot(
+        table[0, pl.ds(0, modes), :], terms[pl.ds(count, count), :], preferred_element_type=jnp.float32
+    )
+    returned = both[:modes] + (both[modes:] + rest)
     for j in range(width):
         x = pl.program_id(0) * width + j
         rows = pl.ds(x, modes, stride=cells_ax)
@@ -274,8 +270,8 @@
 
     adj_recv = [fetch(adj, s) for s in range(1, groups)]
 
-    up = [(i, i + 1) for i in range(ax_size - 1)]
-    down = [(i + 1, i) for i in range(ax_size - 1)]
+    up = [(i, (i + 1) % ax_size) for i in range(ax_size)]
+    down = [(i, (i - 1) % ax_size) for i in range(ax_size)]
     layer = jax.ShapeDtypeStruct((fields, modes, lanes), adjoint.dtype)
     first, last, edges = pl.pallas_call(
         functools.partial(pack_kernel, fields, modes, cells_ax),
@@ -284,6 +280,8 @@
     )(adj)
     below = lax.ppermute(last, "ax", up)
     above = lax.ppermute(first, "ax", down)
+    below = jnp.where(lax.axis_index("ax") == 0, 0.0, below)
+    above = jnp.where(lax.axis_index("ax") == ax_size - 1, 0.0, above)
     if rad_size == 2:
         inner = outer = lax.ppermute(edges, "rad", [(0, 1), (1, 0)])
     else:
@@ -349,20 +347,12 @@
         [whole((rows, lanes))] * groups
         + [stepped(angle_shape), whole(field_shape), SMEM, chosen(back_table.shape)],
         [field], [whole(field_shape)],
-        [pltpu.VMEM((3 * count, cols), jnp.bfloat16)],
+        [pltpu.VMEM((2 * count, cols), jnp.bfloat16)],
         own_flops // 2,
     )[0]
 
-    early = pl.pallas_call(
-        sum_kernel,
-        out_shape=jax.ShapeDtypeStruct(parts[0][0].shape, f32),
-        compiler_params=pltpu.CompilerParams(vmem_limit_bytes=VMEM_LIMIT),
-    )(parts[0][0], *arrived[0])
-    wake_grad = pl.pallas_call(
-        functools.partial(total_kernel, piece_rows[0]),
-        out_shape=plane,
-        compiler_params=pltpu.CompilerParams(vmem_limit_bytes=VMEM_LIMIT),
-    )(early, parts[1][0], *arrived[1])
+    early, late = (functools.reduce(jnp.add, arrived[k], parts[k][0]) for k in range(pieces))
+    wake_grad = -jnp.concatenate([early, late], axis=0)
     return (
         adjoint_in.reshape(adjoint.shape),
         wake_grad.reshape(wake.shape),

time: 44.3 us -> 44.3 us (level)
  other arithmetic: 0.07 us -> 1.87 us
  Pallas kernels: 14.7 us -> 13.6 us
  waiting for transfers between devices: 14.2 us -> 13.7 us
    ppermute x1, waiting for transfers between devices: 6.45 us -> 0.01 us  [body(): below = lax.ppermute(last, 'ax', up)]
    ppermute x1, waiting for transfers between devices: 0.01 us -> 5.85 us  [body(): above = lax.ppermute(first, 'ax', down)]
    ppermute x1, starting transfers between devices: 3.43 us -> 0.01 us  [body(): below = lax.ppermute(last, 'ax', up)]
    ppermute x1, starting transfers between devices: 1.29 us -> 4.56 us  [body(): above = lax.ppermute(first, 'ax', down)]
    select_n x0 -> x2, other arithmetic: none -> 1.03 us  [the longest x1 1 us: body(): above = jnp.where(lax.axis_index('ax') == ax_size - 1, 0.0, above)]
    pallas_call x2 -> x0, Pallas kernels: 0.75 us -> none  [the longest x1 0.73 us: body(): pl.pallas_call(functools.partial(total_kernel, piece_rows[0]), out_shape=...]
    neg x0 -> x1, other arithmetic: none -> 0.72 us  [body(): wake_grad = -jnp.concatenate([early, late], axis=0)]
  transfers between devices with their start and end apart: 8 -> 8, of which waited for: 5 -> 5; matrix products, arithmetic and copies ran while one was open for 0% -> 3% of each run, Pallas kernels for 32% -> 31%
where the time goes in v8:
time: 44.3 us; the launch traced here: 43.9 us
  waiting for transfers between devices  13.7 us (31%)
  Pallas kernels  13.6 us (31%)
  starting transfers between devices  10.2 us (23%)
  local copies, waits for them, and re-layouts  3.7 us (8%)
  other arithmetic  1.87 us (4%)
  between operations  0.76 us (2%)
    pallas_call x4, Pallas kernels, call(): pl.pallas_call(kernel, grid_spec=pltpu.PrefetchScalarGridSpec(num_scalar_...  12.6 us
    ppermute x2, waiting for transfers between devices, fetch(): lax.ppermute(value, 'mode', [((i + s) % groups, i) for i in range(groups)])  6.3 us
    ppermute x1, waiting for transfers between devices, body(): above = lax.ppermute(first, 'ax', down)  5.85 us
    ppermute x1, starting transfers between devices, body(): above = lax.ppermute(first, 'ax', down)  4.56 us
    unnamed x22, local copies, waits for them, and re-layouts  3.7 us
    ppermute x2, starting transfers between devices, fetch(): lax.ppermute(value, 'mode', [((i + s) % groups, i) for i in range(groups)])  3.54 us
    ppermute x1, starting transfers between devices, deliver(): lax.ppermute(value, 'mode', [(i, (i + s) % groups) for i in range(groups)])  2.12 us
    ppermute x1, waiting for transfers between devices, body(): sibling = lax.ppermute(parts[1][1], 'rad', [(0, 1), (1, 0)])  1.25 us
  transfers between devices with their start and end apart: 8, of which 5 were waited for; matrix products, arithmetic and copies ran while one was open for 3% of the time, Pallas kernels for 31%

profile of v8, /device:TPU:0, one launch (start us, length us, event | category | flops | bytes accessed | tf_op | source)
XLA Modules:
  0.0 43.9 jit_solution(17565229082168588762)
XLA Ops:
  0.6 3.0 %collective-permute-start.1 = (f32[5,512,128]{2,1,0:T(8,128)}, f32[5,512,128]{2,1,0:T(8,128)S(1)}, u32[]{:S(2)}, u32[]{:S(2)}) collective-permute-start(f32[5,512,128]{2,1,0:T(8,128)} %bitcast.7), channel_id=1, source_target_pairs={{16,0},{0,16},{17,1},{1,17},{18,2},{2,18},{19,3},{3,19},{20,4},{4,... | collective-permute-start | bytes 3932168 | tf_op jit(solution)/shard_map/ppermute | solution.py:266
  3.6 0.0 copy-start
  3.6 1.3 %copy-done = f32[5,128,4,128]{3,2,1,0:T(4,128)S(1)} copy-done((f32[5,128,4,128]{3,2,1,0:T(4,128)S(1)}, f32[5,128,4,128]{3,2,1,0:T(4,128)}, u32[]{:S(2)}) %copy-start) | copy-done | bytes 1310744
  5.0 0.0 copy-start.1
  5.0 0.0 copy-start.8
  5.0 1.1 %shard_map.114 = (f32[5,128,128]{2,1,0:T(8,128)}, f32[5,128,128]{2,1,0:T(8,128)S(1)}, f32[128,128]{1,0:T(8,128)S(1)}) custom-call(f32[5,512,128]{2,1,0:T(8,128)S(1)} %bitcast.8), custom_call_target="tpu_custom_call" | custom-call | tf_op jit(solution)/shard_map/pallas_call | solution.py:276
  6.0 4.6 %collective-permute-start.3 = (f32[5,128,128]{2,1,0:T(8,128)}, f32[5,128,128]{2,1,0:T(8,128)}, u32[]{:S(2)}, u32[]{:S(2)}) collective-permute-start(f32[5,128,128]{2,1,0:T(8,128)} %get-tuple-element.15), channel_id=1, source_target_pairs={{0,14},{2,0},{4,2},{6,4},{8,6},{10,8},{12,10},{14,12},{1,15},{3,1}... | collective-permute-start | bytes 983048 | tf_op jit(solution)/shard_map/ppermute | solution.py:282
  10.6 0.0 collective-permute-start.2
  10.6 0.0 collective-permute-start.4
  10.6 0.5 %collective-permute-start = (f32[512,128]{1,0:T(8,128)}, f32[512,128]{1,0:T(8,128)S(1)}, u32[]{:S(2)}, u32[]{:S(2)}) collective-permute-start(f32[512,128]{1,0:T(8,128)} %bitcast.11), channel_id=1, source_target_pairs={{16,0},{0,16},{17,1},{1,17},{18,2},{2,18},{19,3},{3,19},{20,4},{4,... | collective-permute-start | bytes 786440 | tf_op jit(solution)/shard_map/ppermute | solution.py:266
  11.1 0.1 pad_add_fusion.where
  11.2 0.0 copy-done.1
  11.2 0.0 copy-done.8
  11.2 0.0 copy-start.9
  11.2 1.3 %copy-done.9 = f32[5,128,4,128]{3,2,1,0:T(4,128)S(1)} copy-done((f32[5,128,4,128]{3,2,1,0:T(4,128)S(1)}, f32[5,128,4,128]{3,2,1,0:T(4,128)}, u32[]{:S(2)}) %copy-start.9) | copy-done | bytes 1310744
  12.5 0.0 copy-start.10
  12.5 1.0 %copy-done.10 = bf16[2,256,384]{2,1,0:T(8,128)(2,1)S(1)} copy-done((bf16[2,256,384]{2,1,0:T(8,128)(2,1)S(1)}, bf16[2,256,384]{2,1,0:T(8,128)(2,1)}, u32[]{:S(2)}) %copy-start.10) | copy-done | bytes 393240
  13.5 3.1 %shard_map.113 = (f32[2,256,1280]{2,1,0:T(8,128)S(1)}, f32[2,256,1280]{2,1,0:T(8,128)S(1)}) custom-call(s32[2]{0:T(128)S(1)} %pad_add_fusion.where, f32[5,512,128]{2,1,0:T(8,128)S(1)} %bitcast.9, f32[5,512,128]{2,1,0:T(8,128)S(1)} %bitcast.13, f32[5,5]{1,0:T(8,128)S(1)} %copy-done.8, bf16[2,256,384]{2,1,0:T(8,128)(2,1)S(1)} %copy-done.10), custom_call_target="tpu_custom_call" | custom-call | flops 1006632960 | bytes 8257636 | tf_op jit(solution)/shard_map/pallas_call | solution.py:227
  16.7 0.0 copy-start.5
  16.7 0.0 copy-start.6
  16.7 0.0 copy-start.7
  16.7 5.8 %collective-permute-done.3 = f32[5,128,128]{2,1,0:T(8,128)} collective-permute-done((f32[5,128,128]{2,1,0:T(8,128)}, f32[5,128,128]{2,1,0:T(8,128)}, u32[]{:S(2)}, u32[]{:S(2)}) %collective-permute-start.3) | collective-permute-done | bytes 327712 | tf_op jit(solution)/shard_map/ppermute | solution.py:282
  22.5 1.0 %broadcast_select_fusion.above = f32[5,128,128]{2,1,0:T(8,128)S(1)} fusion(f32[5,128,128]{2,1,0:T(8,128)} %collective-permute-done.3, pred[]{:T(512)S(6)} %eq.7), kind=kLoop, calls=%fused_computation.1 | loop fusion | flops 81920 | bytes 655361 | tf_op jit(solution)/shard_map/jit(_where)/select_n | solution.py:284
  23.5 0.0 collective-permute-done.2
  23.6 0.0 copy-start.2
  23.6 0.0 collective-permute-done.4.inner.outer
  23.6 0.0 copy-done.5
  23.6 0.0 copy-done.6
  23.6 0.0 copy-done.7
  23.7 4.0 %shard_map.115.refs_4_.refs_3_ = f32[5,512,128]{2,1,0:T(8,128)S(1)} custom-call(s32[2]{0:T(128)S(1)} %pad_add_fusion.where, f32[5,512,128]{2,1,0:T(8,128)S(1)} %bitcast.10, f32[5,128,128]{2,1,0:T(8,128)S(1)} %broadcast_select_fusion.1.below, f32[5,128,128]{2,1,0:T(8,128)S(1)} %broadcast_select_fusion.above, ...), custom_call_target="tpu_custom_call" | custom-call | flops 52428800 | bytes 3408172 | tf_op jit(solution)/shard_map/pallas_call | solution.py:227
  27.7 5.8 %collective-permute-done.1.refs_0_ = f32[5,512,128]{2,1,0:T(8,128)S(1)} collective-permute-done((f32[5,512,128]{2,1,0:T(8,128)}, f32[5,512,128]{2,1,0:T(8,128)S(1)}, u32[]{:S(2)}, u32[]{:S(2)}) %collective-permute-start.1) | collective-permute-done | bytes 1310752 | tf_op jit(solution)/shard_map/ppermute | solution.py:266
  33.4 0.0 copy-done.2
  33.5 0.0 copy-start.3
  33.5 0.0 copy-start.4
  33.5 1.7 %shard_map.116 = (f32[2,256,1280]{2,1,0:T(8,128)S(1)}, f32[384,128]{1,0:T(8,128)S(1)}, f32[128,128]{1,0:T(8,128)S(1)}, f32[384,128]{1,0:T(8,128)S(1)}, f32[128,128]{1,0:T(8,128)S(1)}) custom-call(s32[2]{0:T(128)S(1)} %pad_add_fusion.where, f32[5,512,128]{2,1,0:T(8,128)S(1)} %collective-permute-done.1.refs_0_, f32[2,256,1280]{2,1,0:T(8,128)S(1)} %get-tuple-element.12.refs_1_, ...), custom_call_target="tpu_custom_call" | custom-call | flops 503316480 | bytes 11403264 | tf_op jit(solution)/shard_map/pallas_call | solution.py:227
  35.2 2.1 %collective-permute-start.5 = (f32[384,128]{1,0:T(8,128)S(1)}, f32[384,128]{1,0:T(8,128)S(1)}, u32[]{:S(2)}, u32[]{:S(2)}) collective-permute-start(f32[384,128]{1,0:T(8,128)S(1)} %get-tuple-element.19), channel_id=1, source_target_pairs={{0,16},{16,0},{1,17},{17,1},{2,18},{18,2},{3,19},{19,3},{4,20},{20... | collective-permute-start | bytes 589832 | tf_op jit(solution)/shard_map/ppermute | solution.py:269
  37.3 0.0 collective-permute-start.6
  37.3 1.3 %collective-permute-done.6 = f32[128,128]{1,0:T(8,128)S(1)} collective-permute-done((f32[128,128]{1,0:T(8,128)S(1)}, f32[128,128]{1,0:T(8,128)S(1)}, u32[]{:S(2)}, u32[]{:S(2)}) %collective-permute-start.6) | collective-permute-done | bytes 65568 | tf_op jit(solution)/shard_map/ppermute | solution.py:339
  38.5 0.0 collective-permute-start.7
  38.5 0.5 %collective-permute-done.refs_1_ = f32[512,128]{1,0:T(8,128)S(1)} collective-permute-done((f32[512,128]{1,0:T(8,128)}, f32[512,128]{1,0:T(8,128)S(1)}, u32[]{:S(2)}, u32[]{:S(2)}) %collective-permute-start) | collective-permute-done | bytes 262176 | tf_op jit(solution)/shard_map/ppermute | solution.py:266
  39.1 0.0 copy-done.3
  39.1 0.0 copy-done.4
  39.1 3.7 %shard_map.117 = f32[5,512,128]{2,1,0:T(8,128)} custom-call(s32[2]{0:T(128)S(1)} %pad_add_fusion.where, f32[512,128]{1,0:T(8,128)S(1)} %bitcast.12, f32[512,128]{1,0:T(8,128)S(1)} %collective-permute-done.refs_1_, f32[2,256,1280]{2,1,0:T(8,128)S(1)} %get-tuple-element.17.refs_2_, f32[5,512,128]{2,1,0:T(8,128)S(1)} %shard_map.115.refs_4_.refs_3_, ...), custom_call_target="tpu_custom_call" | custom-call | flops 503316480 | bytes 6029412 | tf_op jit(solution)/shard_map/pallas_call | solution.py:227
  42.8 0.3 collective-permute-done.7
  43.1 0.0 collective-permute-done.5
  43.2 0.7 %maximum_negate_fusion = f32[512,128]{1,0:T(8,128)} fusion(f32[128,128]{1,0:T(8,128)S(1)} %add.7, f32[384,128]{1,0:T(8,128)S(1)} %add.6), kind=kLoop, calls=%fused_computation | loop fusion | flops 131072 | bytes 524288 | tf_op jit(solution)/shard_map/neg | solution.py:355
  (3 shorter events, 0.1 us)
Async XLA Ops:
  0.6 32.8 %collective-permute-start.1 = (f32[5,512,128]{2,1,0:T(8,128)}, f32[5,512,128]{2,1,0:T(8,128)S(1)}, u32[]{:S(2)}, u32[]{:S(2)}) collective-permute-start(f32[5,512,128]{2,1,0:T(8,128)} %bitcast.7), channel_id=1, source_target_pairs={{16,0},{0,16},{17,1},{1,17},{18,2},{2,18},{19,3},{3,19},{20,4},{4,... | collective-permute-start | bytes 3932168 | tf_op jit(solution)/shard_map/ppermute | solution.py:266
  3.6 1.4 %copy-start = (f32[5,128,4,128]{3,2,1,0:T(4,128)S(1)}, f32[5,128,4,128]{3,2,1,0:T(4,128)}, u32[]{:S(2)}) copy-start(f32[5,128,4,128]{3,2,1,0:T(4,128)} %param.10) | copy-start | bytes 3932164
  5.0 6.2 %copy-start.1 = (f32[5,128,4,128]{3,2,1,0:T(4,128)S(1)}, f32[5,128,4,128]{3,2,1,0:T(4,128)}, u32[]{:S(2)}) copy-start(f32[5,128,4,128]{3,2,1,0:T(4,128)} %param.10) | copy-start | bytes 3932164
  5.0 6.2 %copy-start.8 = (f32[5,5]{1,0:T(8,128)S(1)}, f32[5,5]{1,0:T(8,128)}, u32[]{:S(2)}) copy-start(f32[5,5]{1,0:T(8,128)} %refs_4_.1) | copy-start | bytes 304
  6.0 16.5 %collective-permute-start.3 = (f32[5,128,128]{2,1,0:T(8,128)}, f32[5,128,128]{2,1,0:T(8,128)}, u32[]{:S(2)}, u32[]{:S(2)}) collective-permute-start(f32[5,128,128]{2,1,0:T(8,128)} %get-tuple-element.15), channel_id=1, source_target_pairs={{0,14},{2,0},{4,2},{6,4},{8,6},{10,8},{12,10},{14,12},{1,15},{3,1}... | collective-permute-start | bytes 983048 | tf_op jit(solution)/shard_map/ppermute | solution.py:282
  10.6 13.0 %collective-permute-start.2 = (f32[5,128,128]{2,1,0:T(8,128)S(1)}, f32[5,128,128]{2,1,0:T(8,128)}, u32[]{:S(2)}, u32[]{:S(2)}) collective-permute-start(f32[5,128,128]{2,1,0:T(8,128)S(1)} %get-tuple-element.14), channel_id=1, source_target_pairs={{0,2},{2,4},{4,6},{6,8},{8,10},{10,12},{12,14},{14,0},{1,3},{3,5},... | collective-permute-start | bytes 983048 | tf_op jit(solution)/shard_map/ppermute | solution.py:281
  10.6 13.0 %collective-permute-start.4 = (f32[128,128]{1,0:T(8,128)S(1)}, f32[128,128]{1,0:T(8,128)S(1)}, u32[]{:S(2)}, u32[]{:S(2)}) collective-permute-start(f32[128,128]{1,0:T(8,128)S(1)} %get-tuple-element.16), channel_id=1, source_target_pairs={{0,1},{1,0},{2,3},{3,2},{4,5},{5,4},{6,7},{7,6},{8,9},{9,8},{10,11... | collective-permute-start | bytes 196616 | tf_op jit(solution)/shard_map/ppermute | solution.py:286
  10.6 28.5 %collective-permute-start = (f32[512,128]{1,0:T(8,128)}, f32[512,128]{1,0:T(8,128)S(1)}, u32[]{:S(2)}, u32[]{:S(2)}) collective-permute-start(f32[512,128]{1,0:T(8,128)} %bitcast.11), channel_id=1, source_target_pairs={{16,0},{0,16},{17,1},{1,17},{18,2},{2,18},{19,3},{3,19},{20,4},{4,... | collective-permute-start | bytes 786440 | tf_op jit(solution)/shard_map/ppermute | solution.py:266
  11.2 1.3 %copy-start.9 = (f32[5,128,4,128]{3,2,1,0:T(4,128)S(1)}, f32[5,128,4,128]{3,2,1,0:T(4,128)}, u32[]{:S(2)}) copy-start(f32[5,128,4,128]{3,2,1,0:T(4,128)} %param.11) | copy-start | bytes 3932164
  12.5 1.0 %copy-start.10 = (bf16[2,256,384]{2,1,0:T(8,128)(2,1)S(1)}, bf16[2,256,384]{2,1,0:T(8,128)(2,1)}, u32[]{:S(2)}) copy-start(bf16[2,256,384]{2,1,0:T(8,128)(2,1)} %constant.24.clone.table) | copy-start | bytes 1179652
  16.7 7.0 %copy-start.5 = (f32[5,5]{1,0:T(8,128)S(1)}, f32[5,5]{1,0:T(8,128)}, u32[]{:S(2)}) copy-start(f32[5,5]{1,0:T(8,128)} %jac_axial.1) | copy-start | bytes 304
  16.7 7.0 %copy-start.6 = (f32[5,5]{1,0:T(8,128)S(1)}, f32[5,5]{1,0:T(8,128)}, u32[]{:S(2)}) copy-start(f32[5,5]{1,0:T(8,128)} %jac_radial.1) | copy-start | bytes 304
  16.7 7.0 %copy-start.7 = (f32[5,5]{1,0:T(8,128)S(1)}, f32[5,5]{1,0:T(8,128)}, u32[]{:S(2)}) copy-start(f32[5,5]{1,0:T(8,128)} %jac_swirl.1) | copy-start | bytes 304
  23.6 9.8 %copy-start.2 = (bf16[2,1,256,384]{3,2,1,0:T(8,128)(2,1)S(1)}, bf16[2,1,256,384]{3,2,1,0:T(8,128)(2,1)}, u32[]{:S(2)}) copy-start(bf16[2,1,256,384]{3,2,1,0:T(8,128)(2,1)} %constant.25.clone.refs_3_) | copy-start | bytes 1179652
  33.5 5.6 %copy-start.3 = (f32[128,4,128]{2,1,0:T(4,128)S(1)}, f32[128,4,128]{2,1,0:T(4,128)}, u32[]{:S(2)}) copy-start(f32[128,4,128]{2,1,0:T(4,128)} %param.12) | copy-start | bytes 786436
  33.5 5.6 %copy-start.4 = (bf16[2,256,256]{2,1,0:T(8,128)(2,1)S(1)}, bf16[2,256,256]{2,1,0:T(8,128)(2,1)}, u32[]{:S(2)}) copy-start(bf16[2,256,256]{2,1,0:T(8,128)(2,1)} %constant.26.clone.refs_5_) | copy-start | bytes 786436
  35.2 8.0 %collective-permute-start.5 = (f32[384,128]{1,0:T(8,128)S(1)}, f32[384,128]{1,0:T(8,128)S(1)}, u32[]{:S(2)}, u32[]{:S(2)}) collective-permute-start(f32[384,128]{1,0:T(8,128)S(1)} %get-tuple-element.19), channel_id=1, source_target_pairs={{0,16},{16,0},{1,17},{17,1},{2,18},{18,2},{3,19},{19,3},{4,20},{20... | collective-permute-start | bytes 589832 | tf_op jit(solution)/shard_map/ppermute | solution.py:269
  37.3 1.3 %collective-permute-start.6 = (f32[128,128]{1,0:T(8,128)S(1)}, f32[128,128]{1,0:T(8,128)S(1)}, u32[]{:S(2)}, u32[]{:S(2)}) collective-permute-start(f32[128,128]{1,0:T(8,128)S(1)} %get-tuple-element.21), channel_id=1, source_target_pairs={{0,1},{1,0},{2,3},{3,2},{4,5},{5,4},{6,7},{7,6},{8,9},{9,8},{10,11... | collective-permute-start | bytes 196616 | tf_op jit(solution)/shard_map/ppermute | solution.py:339
  38.5 4.6 %collective-permute-start.7 = (f32[128,128]{1,0:T(8,128)S(1)}, f32[128,128]{1,0:T(8,128)S(1)}, u32[]{:S(2)}, u32[]{:S(2)}) collective-permute-start(f32[128,128]{1,0:T(8,128)S(1)} %collective-permute-done.6), channel_id=1, source_target_pairs={{0,17},{1,16},{16,1},{17,0},{2,19},{3,18},{18,3},{19,2},{4,21},{5,... | collective-permute-start | bytes 196616 | tf_op jit(solution)/shard_map/ppermute | solution.py:340

commit v9 on v8

--- a/solution.py
+++ b/solution.py
@@ -287,7 +287,11 @@
     else:
         inner = lax.ppermute(edges, "rad", [(i, i + 1) for i in range(rad_size - 1)])
         outer = lax.ppermute(edges, "rad", [(i + 1, i) for i in range(rad_size - 1)])
-    wake_recv = [fetch(wk, s) for s in range(1, groups)]
+    if groups == 2 and rad_size == 2:
+        sibling_wake = lax.ppermute(wk, "rad", [(0, 1), (1, 0)])
+        wake_recv = [lax.ppermute(sibling_wake, ("mode", "rad"), [(i, 3 - i) for i in range(4)])]
+    else:
+        wake_recv = [fetch(wk, s) for s in range(1, groups)]
 
     field_shape = (fields, rows, lanes)
     angle_shape = (steps, count, cols)

time: 44.3 us -> 44.3 us (level)
  Pallas kernels: 13.6 us -> 13 us
  waiting for transfers between devices: 13.7 us -> 14.2 us
    ppermute x1, waiting for transfers between devices: 5.85 us -> 0.4 us  [body(): above = lax.ppermute(first, 'ax', down)]
    ppermute x1, waiting for transfers between devices: 0.01 us -> 5.24 us  [body(): below = lax.ppermute(last, 'ax', up)]
    pallas_call x1, Pallas kernels: 1.05 us -> 0.41 us  [body(): pl.pallas_call(functools.partial(pack_kernel, fields, modes, cells_ax), o...]
    ppermute x2 -> x1, starting transfers between devices: 3.54 us -> 3 us  [fetch(): lax.ppermute(value, 'mode', [((i + s) % groups, i) for i in range(groups)])]
    ppermute x1, starting transfers between devices: 0.01 us -> 0.51 us  [body(): inner = outer = lax.ppermute(edges, 'rad', [(0, 1), (1, 0)])]
    ppermute x2 -> x1, waiting for transfers between devices: 6.3 us -> 6.4 us  [fetch(): lax.ppermute(value, 'mode', [((i + s) % groups, i) for i in range(groups)])]
  transfers between devices with their start and end apart: 8 -> 9, of which waited for: 5 -> 6; matrix products, arithmetic and copies ran while one was open for 3% -> 3% of each run, Pallas kernels for 31% -> 30%
where the time goes in v9:
time: 44.3 us; the launch traced here: 43.9 us
  waiting for transfers between devices  14.2 us (32%)
  Pallas kernels  13 us (29%)
  starting transfers between devices  10.5 us (24%)
  local copies, waits for them, and re-layouts  3.7 us (8%)
  other arithmetic  1.86 us (4%)
  between operations  0.76 us (2%)
    pallas_call x4, Pallas kernels, call(): pl.pallas_call(kernel, grid_spec=pltpu.PrefetchScalarGridSpec(num_scalar_...  12.6 us
    ppermute x1, waiting for transfers between devices, fetch(): lax.ppermute(value, 'mode', [((i + s) % groups, i) for i in range(groups)])  6.4 us
    ppermute x1, waiting for transfers between devices, body(): below = lax.ppermute(last, 'ax', up)  5.24 us
    ppermute x1, starting transfers between devices, body(): above = lax.ppermute(first, 'ax', down)  4.61 us
    unnamed x22, local copies, waits for them, and re-layouts  3.7 us
    ppermute x1, starting transfers between devices, fetch(): lax.ppermute(value, 'mode', [((i + s) % groups, i) for i in range(groups)])  3 us
    ppermute x1, starting transfers between devices, deliver(): lax.ppermute(value, 'mode', [(i, (i + s) % groups) for i in range(groups)])  2.12 us
    ppermute x1, waiting for transfers between devices, body(): sibling = lax.ppermute(parts[1][1], 'rad', [(0, 1), (1, 0)])  1.25 us
  transfers between devices with their start and end apart: 9, of which 6 were waited for; matrix products, arithmetic and copies ran while one was open for 3% of the time, Pallas kernels for 30%

profile of v9, /device:TPU:0, one launch (start us, length us, event | category | flops | bytes accessed | tf_op | source)
XLA Modules:
  0.0 43.9 jit_solution(14988287886085054912)
XLA Ops:
  0.6 3.0 %collective-permute-start.2 = (f32[5,512,128]{2,1,0:T(8,128)}, f32[5,512,128]{2,1,0:T(8,128)S(1)}, u32[]{:S(2)}, u32[]{:S(2)}) collective-permute-start(f32[5,512,128]{2,1,0:T(8,128)} %bitcast.7), channel_id=1, source_target_pairs={{16,0},{0,16},{17,1},{1,17},{18,2},{2,18},{19,3},{3,19},{20,4},{4,... | collective-permute-start | bytes 3932168 | tf_op jit(solution)/shard_map/ppermute | solution.py:266
  3.6 0.0 copy-start
  3.6 1.3 %copy-done = f32[5,128,4,128]{3,2,1,0:T(4,128)S(1)} copy-done((f32[5,128,4,128]{3,2,1,0:T(4,128)S(1)}, f32[5,128,4,128]{3,2,1,0:T(4,128)}, u32[]{:S(2)}) %copy-start) | copy-done | bytes 1310744
  5.0 0.0 copy-start.1
  5.0 0.0 copy-start.8
  5.0 0.4 shard_map.114
  5.4 4.6 %collective-permute-start.4 = (f32[5,128,128]{2,1,0:T(8,128)S(1)}, f32[5,128,128]{2,1,0:T(8,128)}, u32[]{:S(2)}, u32[]{:S(2)}) collective-permute-start(f32[5,128,128]{2,1,0:T(8,128)S(1)} %get-tuple-element.15), channel_id=1, source_target_pairs={{0,14},{2,0},{4,2},{6,4},{8,6},{10,8},{12,10},{14,12},{1,15},{3,1}... | collective-permute-start | bytes 983048 | tf_op jit(solution)/shard_map/ppermute | solution.py:282
  10.0 0.0 collective-permute-start
  10.0 0.0 collective-permute-start.3
  10.0 0.5 %collective-permute-start.5 = (f32[128,128]{1,0:T(8,128)S(1)}, f32[128,128]{1,0:T(8,128)S(1)}, u32[]{:S(2)}, u32[]{:S(2)}) collective-permute-start(f32[128,128]{1,0:T(8,128)S(1)} %get-tuple-element.16), channel_id=1, source_target_pairs={{0,1},{1,0},{2,3},{3,2},{4,5},{5,4},{6,7},{7,6},{8,9},{9,8},{10,11... | collective-permute-start | bytes 196616 | tf_op jit(solution)/shard_map/ppermute | solution.py:286
  10.5 0.1 pad_add_fusion.where
  10.6 0.0 copy-done.1
  10.6 0.0 copy-done.8
  10.6 0.0 copy-start.9
  10.6 1.3 %copy-done.9 = f32[5,128,4,128]{3,2,1,0:T(4,128)S(1)} copy-done((f32[5,128,4,128]{3,2,1,0:T(4,128)S(1)}, f32[5,128,4,128]{3,2,1,0:T(4,128)}, u32[]{:S(2)}) %copy-start.9) | copy-done | bytes 1310744
  11.9 0.0 copy-start.10
  11.9 1.0 %copy-done.10 = bf16[2,256,384]{2,1,0:T(8,128)(2,1)S(1)} copy-done((bf16[2,256,384]{2,1,0:T(8,128)(2,1)S(1)}, bf16[2,256,384]{2,1,0:T(8,128)(2,1)}, u32[]{:S(2)}) %copy-start.10) | copy-done | bytes 393240
  12.9 3.1 %shard_map.113 = (f32[2,256,1280]{2,1,0:T(8,128)S(1)}, f32[2,256,1280]{2,1,0:T(8,128)S(1)}) custom-call(s32[2]{0:T(128)S(1)} %pad_add_fusion.where, f32[5,512,128]{2,1,0:T(8,128)S(1)} %bitcast.9, f32[5,512,128]{2,1,0:T(8,128)S(1)} %bitcast.13, f32[5,5]{1,0:T(8,128)S(1)} %copy-done.8, bf16[2,256,384]{2,1,0:T(8,128)(2,1)S(1)} %copy-done.10), custom_call_target="tpu_custom_call" | custom-call | flops 1006632960 | bytes 8257636 | tf_op jit(solution)/shard_map/pallas_call | solution.py:227
  16.1 0.0 copy-start.5
  16.1 0.0 copy-start.6
  16.1 0.0 copy-start.7
  16.1 0.0 collective-permute-done
  16.1 0.2 collective-permute-start.1
  16.3 0.4 collective-permute-done.4
  16.7 1.0 %broadcast_select_fusion.above = f32[5,128,128]{2,1,0:T(8,128)S(1)} fusion(f32[5,128,128]{2,1,0:T(8,128)} %collective-permute-done.4, pred[]{:T(512)S(6)} %eq.7), kind=kLoop, calls=%fused_computation.1 | loop fusion | flops 81920 | bytes 655361 | tf_op jit(solution)/shard_map/jit(_where)/select_n | solution.py:284
  17.7 5.2 %collective-permute-done.3 = f32[5,128,128]{2,1,0:T(8,128)} collective-permute-done((f32[5,128,128]{2,1,0:T(8,128)S(1)}, f32[5,128,128]{2,1,0:T(8,128)}, u32[]{:S(2)}, u32[]{:S(2)}) %collective-permute-start.3) | collective-permute-done | bytes 327712 | tf_op jit(solution)/shard_map/ppermute | solution.py:281
  23.0 0.0 copy-start.2
  23.0 0.0 collective-permute-done.5.inner.outer
  23.0 0.0 copy-done.5
  23.0 0.0 copy-done.6
  23.0 0.0 copy-done.7
  23.0 4.0 %shard_map.115.refs_4_.refs_3_ = f32[5,512,128]{2,1,0:T(8,128)S(1)} custom-call(s32[2]{0:T(128)S(1)} %pad_add_fusion.where, f32[5,512,128]{2,1,0:T(8,128)S(1)} %bitcast.10, f32[5,128,128]{2,1,0:T(8,128)S(1)} %broadcast_select_fusion.1.below, f32[5,128,128]{2,1,0:T(8,128)S(1)} %broadcast_select_fusion.above, ...), custom_call_target="tpu_custom_call" | custom-call | flops 52428800 | bytes 3408172 | tf_op jit(solution)/shard_map/pallas_call | solution.py:227
  27.0 6.4 %collective-permute-done.2.refs_0_ = f32[5,512,128]{2,1,0:T(8,128)S(1)} collective-permute-done((f32[5,512,128]{2,1,0:T(8,128)}, f32[5,512,128]{2,1,0:T(8,128)S(1)}, u32[]{:S(2)}, u32[]{:S(2)}) %collective-permute-start.2) | collective-permute-done | bytes 1310752 | tf_op jit(solution)/shard_map/ppermute | solution.py:266
  33.4 0.0 copy-done.2
  33.5 0.0 copy-start.3
  33.5 0.0 copy-start.4
  33.5 1.7 %shard_map.116 = (f32[2,256,1280]{2,1,0:T(8,128)S(1)}, f32[384,128]{1,0:T(8,128)S(1)}, f32[128,128]{1,0:T(8,128)S(1)}, f32[384,128]{1,0:T(8,128)S(1)}, f32[128,128]{1,0:T(8,128)S(1)}) custom-call(s32[2]{0:T(128)S(1)} %pad_add_fusion.where, f32[5,512,128]{2,1,0:T(8,128)S(1)} %collective-permute-done.2.refs_0_, f32[2,256,1280]{2,1,0:T(8,128)S(1)} %get-tuple-element.12.refs_1_, ...), custom_call_target="tpu_custom_call" | custom-call | flops 503316480 | bytes 11403264 | tf_op jit(solution)/shard_map/pallas_call | solution.py:227
  35.2 2.1 %collective-permute-start.6 = (f32[384,128]{1,0:T(8,128)S(1)}, f32[384,128]{1,0:T(8,128)S(1)}, u32[]{:S(2)}, u32[]{:S(2)}) collective-permute-start(f32[384,128]{1,0:T(8,128)S(1)} %get-tuple-element.19), channel_id=1, source_target_pairs={{0,16},{16,0},{1,17},{17,1},{2,18},{18,2},{3,19},{19,3},{4,20},{20... | collective-permute-start | bytes 589832 | tf_op jit(solution)/shard_map/ppermute | solution.py:269
  37.3 0.0 collective-permute-start.7
  37.3 1.3 %collective-permute-done.7 = f32[128,128]{1,0:T(8,128)S(1)} collective-permute-done((f32[128,128]{1,0:T(8,128)S(1)}, f32[128,128]{1,0:T(8,128)S(1)}, u32[]{:S(2)}, u32[]{:S(2)}) %collective-permute-start.7) | collective-permute-done | bytes 65568 | tf_op jit(solution)/shard_map/ppermute | solution.py:343
  38.5 0.0 collective-permute-start.8
  38.5 0.2 collective-permute-done.1.refs_1_
  38.7 0.0 copy-done.3
  38.8 0.0 copy-done.4
  38.8 3.7 %shard_map.117 = f32[5,512,128]{2,1,0:T(8,128)} custom-call(s32[2]{0:T(128)S(1)} %pad_add_fusion.where, f32[512,128]{1,0:T(8,128)S(1)} %bitcast.12, f32[512,128]{1,0:T(8,128)S(1)} %collective-permute-done.1.refs_1_, f32[2,256,1280]{2,1,0:T(8,128)S(1)} %get-tuple-element.17.refs_2_, f32[5,512,128]{2,1,0:T(8,128)S(1)} %shard_map.115.refs_4_.refs_3_, ...), custom_call_target="tpu_custom_call" | custom-call | flops 503316480 | bytes 6029412 | tf_op jit(solution)/shard_map/pallas_call | solution.py:227
  42.5 0.6 %collective-permute-done.8 = f32[128,128]{1,0:T(8,128)S(1)} collective-permute-done((f32[128,128]{1,0:T(8,128)S(1)}, f32[128,128]{1,0:T(8,128)S(1)}, u32[]{:S(2)}, u32[]{:S(2)}) %collective-permute-start.8) | collective-permute-done | bytes 65568 | tf_op jit(solution)/shard_map/ppermute | solution.py:344
  43.1 0.0 collective-permute-done.6
  43.2 0.7 %maximum_negate_fusion = f32[512,128]{1,0:T(8,128)} fusion(f32[128,128]{1,0:T(8,128)S(1)} %add.7, f32[384,128]{1,0:T(8,128)S(1)} %add.6), kind=kLoop, calls=%fused_computation | loop fusion | flops 131072 | bytes 524288 | tf_op jit(solution)/shard_map/neg | solution.py:359
  (3 shorter events, 0.1 us)
Async XLA Ops:
  0.6 32.8 %collective-permute-start.2 = (f32[5,512,128]{2,1,0:T(8,128)}, f32[5,512,128]{2,1,0:T(8,128)S(1)}, u32[]{:S(2)}, u32[]{:S(2)}) collective-permute-start(f32[5,512,128]{2,1,0:T(8,128)} %bitcast.7), channel_id=1, source_target_pairs={{16,0},{0,16},{17,1},{1,17},{18,2},{2,18},{19,3},{3,19},{20,4},{4,... | collective-permute-start | bytes 3932168 | tf_op jit(solution)/shard_map/ppermute | solution.py:266
  3.6 1.4 %copy-start = (f32[5,128,4,128]{3,2,1,0:T(4,128)S(1)}, f32[5,128,4,128]{3,2,1,0:T(4,128)}, u32[]{:S(2)}) copy-start(f32[5,128,4,128]{3,2,1,0:T(4,128)} %param.10) | copy-start | bytes 3932164
  5.0 5.6 %copy-start.1 = (f32[5,128,4,128]{3,2,1,0:T(4,128)S(1)}, f32[5,128,4,128]{3,2,1,0:T(4,128)}, u32[]{:S(2)}) copy-start(f32[5,128,4,128]{3,2,1,0:T(4,128)} %param.10) | copy-start | bytes 3932164
  5.0 5.6 %copy-start.8 = (f32[5,5]{1,0:T(8,128)S(1)}, f32[5,5]{1,0:T(8,128)}, u32[]{:S(2)}) copy-start(f32[5,5]{1,0:T(8,128)} %refs_4_.1) | copy-start | bytes 304
  5.4 11.3 %collective-permute-start.4 = (f32[5,128,128]{2,1,0:T(8,128)S(1)}, f32[5,128,128]{2,1,0:T(8,128)}, u32[]{:S(2)}, u32[]{:S(2)}) collective-permute-start(f32[5,128,128]{2,1,0:T(8,128)S(1)} %get-tuple-element.15), channel_id=1, source_target_pairs={{0,14},{2,0},{4,2},{6,4},{8,6},{10,8},{12,10},{14,12},{1,15},{3,1}... | collective-permute-start | bytes 983048 | tf_op jit(solution)/shard_map/ppermute | solution.py:282
  10.0 6.1 %collective-permute-start = (f32[512,128]{1,0:T(8,128)}, f32[512,128]{1,0:T(8,128)}, u32[]{:S(2)}, u32[]{:S(2)}) collective-permute-start(f32[512,128]{1,0:T(8,128)} %bitcast.11), channel_id=1, source_target_pairs={{0,1},{1,0},{2,3},{3,2},{4,5},{5,4},{6,7},{7,6},{8,9},{9,8},{10,11... | collective-permute-start | bytes 786440 | tf_op jit(solution)/shard_map/ppermute | solution.py:291
  10.0 12.9 %collective-permute-start.3 = (f32[5,128,128]{2,1,0:T(8,128)S(1)}, f32[5,128,128]{2,1,0:T(8,128)}, u32[]{:S(2)}, u32[]{:S(2)}) collective-permute-start(f32[5,128,128]{2,1,0:T(8,128)S(1)} %get-tuple-element.14), channel_id=1, source_target_pairs={{0,2},{2,4},{4,6},{6,8},{8,10},{10,12},{12,14},{14,0},{1,3},{3,5},... | collective-permute-start | bytes 983048 | tf_op jit(solution)/shard_map/ppermute | solution.py:281
  10.0 13.0 %collective-permute-start.5 = (f32[128,128]{1,0:T(8,128)S(1)}, f32[128,128]{1,0:T(8,128)S(1)}, u32[]{:S(2)}, u32[]{:S(2)}) collective-permute-start(f32[128,128]{1,0:T(8,128)S(1)} %get-tuple-element.16), channel_id=1, source_target_pairs={{0,1},{1,0},{2,3},{3,2},{4,5},{5,4},{6,7},{7,6},{8,9},{9,8},{10,11... | collective-permute-start | bytes 196616 | tf_op jit(solution)/shard_map/ppermute | solution.py:286
  10.6 1.3 %copy-start.9 = (f32[5,128,4,128]{3,2,1,0:T(4,128)S(1)}, f32[5,128,4,128]{3,2,1,0:T(4,128)}, u32[]{:S(2)}) copy-start(f32[5,128,4,128]{3,2,1,0:T(4,128)} %param.11) | copy-start | bytes 3932164
  11.9 1.0 %copy-start.10 = (bf16[2,256,384]{2,1,0:T(8,128)(2,1)S(1)}, bf16[2,256,384]{2,1,0:T(8,128)(2,1)}, u32[]{:S(2)}) copy-start(bf16[2,256,384]{2,1,0:T(8,128)(2,1)} %constant.24.clone.table) | copy-start | bytes 1179652
  16.1 6.9 %copy-start.5 = (f32[5,5]{1,0:T(8,128)S(1)}, f32[5,5]{1,0:T(8,128)}, u32[]{:S(2)}) copy-start(f32[5,5]{1,0:T(8,128)} %jac_axial.1) | copy-start | bytes 304
  16.1 6.9 %copy-start.6 = (f32[5,5]{1,0:T(8,128)S(1)}, f32[5,5]{1,0:T(8,128)}, u32[]{:S(2)}) copy-start(f32[5,5]{1,0:T(8,128)} %jac_radial.1) | copy-start | bytes 304
  16.1 6.9 %copy-start.7 = (f32[5,5]{1,0:T(8,128)S(1)}, f32[5,5]{1,0:T(8,128)}, u32[]{:S(2)}) copy-start(f32[5,5]{1,0:T(8,128)} %jac_swirl.1) | copy-start | bytes 304
  16.1 22.7 %collective-permute-start.1 = (f32[512,128]{1,0:T(8,128)}, f32[512,128]{1,0:T(8,128)S(1)}, u32[]{:S(2)}, u32[]{:S(2)}) collective-permute-start(f32[512,128]{1,0:T(8,128)} %collective-permute-done), channel_id=1, source_target_pairs={{0,17},{1,16},{16,1},{17,0},{2,19},{3,18},{18,3},{19,2},{4,21},{5,... | collective-permute-start | bytes 786440 | tf_op jit(solution)/shard_map/ppermute | solution.py:292
  23.0 10.5 %copy-start.2 = (bf16[2,1,256,384]{3,2,1,0:T(8,128)(2,1)S(1)}, bf16[2,1,256,384]{3,2,1,0:T(8,128)(2,1)}, u32[]{:S(2)}) copy-start(bf16[2,1,256,384]{3,2,1,0:T(8,128)(2,1)} %constant.25.clone.refs_3_) | copy-start | bytes 1179652
  33.5 5.3 %copy-start.3 = (f32[128,4,128]{2,1,0:T(4,128)S(1)}, f32[128,4,128]{2,1,0:T(4,128)}, u32[]{:S(2)}) copy-start(f32[128,4,128]{2,1,0:T(4,128)} %param.12) | copy-start | bytes 786436
  33.5 5.3 %copy-start.4 = (bf16[2,256,256]{2,1,0:T(8,128)(2,1)S(1)}, bf16[2,256,256]{2,1,0:T(8,128)(2,1)}, u32[]{:S(2)}) copy-start(bf16[2,256,256]{2,1,0:T(8,128)(2,1)} %constant.26.clone.refs_5_) | copy-start | bytes 786436
  35.2 8.0 %collective-permute-start.6 = (f32[384,128]{1,0:T(8,128)S(1)}, f32[384,128]{1,0:T(8,128)S(1)}, u32[]{:S(2)}, u32[]{:S(2)}) collective-permute-start(f32[384,128]{1,0:T(8,128)S(1)} %get-tuple-element.19), channel_id=1, source_target_pairs={{0,16},{16,0},{1,17},{17,1},{2,18},{18,2},{3,19},{19,3},{4,20},{20... | collective-permute-start | bytes 589832 | tf_op jit(solution)/shard_map/ppermute | solution.py:269
  37.3 1.3 %collective-permute-start.7 = (f32[128,128]{1,0:T(8,128)S(1)}, f32[128,128]{1,0:T(8,128)S(1)}, u32[]{:S(2)}, u32[]{:S(2)}) collective-permute-start(f32[128,128]{1,0:T(8,128)S(1)} %get-tuple-element.21), channel_id=1, source_target_pairs={{0,1},{1,0},{2,3},{3,2},{4,5},{5,4},{6,7},{7,6},{8,9},{9,8},{10,11... | collective-permute-start | bytes 196616 | tf_op jit(solution)/shard_map/ppermute | solution.py:343
  38.5 4.6 %collective-permute-start.8 = (f32[128,128]{1,0:T(8,128)S(1)}, f32[128,128]{1,0:T(8,128)S(1)}, u32[]{:S(2)}, u32[]{:S(2)}) collective-permute-start(f32[128,128]{1,0:T(8,128)S(1)} %collective-permute-done.7), channel_id=1, source_target_pairs={{0,17},{1,16},{16,1},{17,0},{2,19},{3,18},{18,3},{19,2},{4,21},{5,... | collective-permute-start | bytes 196616 | tf_op jit(solution)/shard_map/ppermute | solution.py:344

commit v10 on v8

--- a/solution.py
+++ b/solution.py
@@ -319,7 +319,7 @@
         32 * fields * fields * rows * lanes,
     )[0]
 
-    cuts = (0, modes * 3 // 4 // 8 * 8, modes)
+    cuts = (0, modes * 13 // 16 // 8 * 8, modes)
     pieces = len(cuts) - 1
     piece_rows = [(cuts[k + 1] - cuts[k]) * cells_ax for k in range(pieces)]
     joined = call(

time: 44.3 us -> 44.3 us (level)
  transfers between devices with their start and end apart: 8 -> 8, of which waited for: 5 -> 6; matrix products, arithmetic and copies ran while one was open for 3% -> 3% of each run, Pallas kernels for 31% -> 31%
where the time goes in v10:
time: 44.3 us; the launch traced here: 44.1 us
  waiting for transfers between devices  13.9 us (31%)
  Pallas kernels  13.6 us (31%)
  starting transfers between devices  10.2 us (23%)
  local copies, waits for them, and re-layouts  3.7 us (8%)
  other arithmetic  1.87 us (4%)
  between operations  0.75 us (2%)
    pallas_call x4, Pallas kernels, call(): pl.pallas_call(kernel, grid_spec=pltpu.PrefetchScalarGridSpec(num_scalar_...  12.6 us
    ppermute x2, waiting for transfers between devices, fetch(): lax.ppermute(value, 'mode', [((i + s) % groups, i) for i in range(groups)])  6.32 us
    ppermute x1, waiting for transfers between devices, body(): above = lax.ppermute(first, 'ax', down)  5.85 us
    ppermute x1, starting transfers between devices, body(): above = lax.ppermute(first, 'ax', down)  4.56 us
    unnamed x22, local copies, waits for them, and re-layouts  3.7 us
    ppermute x2, starting transfers between devices, fetch(): lax.ppermute(value, 'mode', [((i + s) % groups, i) for i in range(groups)])  3.54 us
    ppermute x1, starting transfers between devices, deliver(): lax.ppermute(value, 'mode', [(i, (i + s) % groups) for i in range(groups)])  2.12 us
    ppermute x1, waiting for transfers between devices, body(): sibling = lax.ppermute(parts[1][1], 'rad', [(0, 1), (1, 0)])  1.23 us
  transfers between devices with their start and end apart: 8, of which 6 were waited for; matrix products, arithmetic and copies ran while one was open for 3% of the time, Pallas kernels for 31%

profile of v10, /device:TPU:0, one launch (start us, length us, event | category | flops | bytes accessed | tf_op | source)
XLA Modules:
  0.0 44.1 jit_solution(4796844149942041397)
XLA Ops:
  0.6 3.0 %collective-permute-start.1 = (f32[5,512,128]{2,1,0:T(8,128)}, f32[5,512,128]{2,1,0:T(8,128)S(1)}, u32[]{:S(2)}, u32[]{:S(2)}) collective-permute-start(f32[5,512,128]{2,1,0:T(8,128)} %bitcast.7), channel_id=1, source_target_pairs={{16,0},{0,16},{17,1},{1,17},{18,2},{2,18},{19,3},{3,19},{20,4},{4,... | collective-permute-start | bytes 3932168 | tf_op jit(solution)/shard_map/ppermute | solution.py:266
  3.6 0.0 copy-start
  3.6 1.3 %copy-done = f32[5,128,4,128]{3,2,1,0:T(4,128)S(1)} copy-done((f32[5,128,4,128]{3,2,1,0:T(4,128)S(1)}, f32[5,128,4,128]{3,2,1,0:T(4,128)}, u32[]{:S(2)}) %copy-start) | copy-done | bytes 1310744
  5.0 0.0 copy-start.1
  5.0 0.0 copy-start.8
  5.0 1.1 %shard_map.114 = (f32[5,128,128]{2,1,0:T(8,128)}, f32[5,128,128]{2,1,0:T(8,128)S(1)}, f32[128,128]{1,0:T(8,128)S(1)}) custom-call(f32[5,512,128]{2,1,0:T(8,128)S(1)} %bitcast.8), custom_call_target="tpu_custom_call" | custom-call | tf_op jit(solution)/shard_map/pallas_call | solution.py:276
  6.0 4.6 %collective-permute-start.3 = (f32[5,128,128]{2,1,0:T(8,128)}, f32[5,128,128]{2,1,0:T(8,128)}, u32[]{:S(2)}, u32[]{:S(2)}) collective-permute-start(f32[5,128,128]{2,1,0:T(8,128)} %get-tuple-element.15), channel_id=1, source_target_pairs={{0,14},{2,0},{4,2},{6,4},{8,6},{10,8},{12,10},{14,12},{1,15},{3,1}... | collective-permute-start | bytes 983048 | tf_op jit(solution)/shard_map/ppermute | solution.py:282
  10.6 0.0 collective-permute-start.2
  10.6 0.0 collective-permute-start.4
  10.6 0.5 %collective-permute-start = (f32[512,128]{1,0:T(8,128)}, f32[512,128]{1,0:T(8,128)S(1)}, u32[]{:S(2)}, u32[]{:S(2)}) collective-permute-start(f32[512,128]{1,0:T(8,128)} %bitcast.11), channel_id=1, source_target_pairs={{16,0},{0,16},{17,1},{1,17},{18,2},{2,18},{19,3},{3,19},{20,4},{4,... | collective-permute-start | bytes 786440 | tf_op jit(solution)/shard_map/ppermute | solution.py:266
  11.1 0.1 pad_add_fusion.where
  11.2 0.0 copy-done.1
  11.2 0.0 copy-done.8
  11.2 0.0 copy-start.9
  11.2 1.3 %copy-done.9 = f32[5,128,4,128]{3,2,1,0:T(4,128)S(1)} copy-done((f32[5,128,4,128]{3,2,1,0:T(4,128)S(1)}, f32[5,128,4,128]{3,2,1,0:T(4,128)}, u32[]{:S(2)}) %copy-start.9) | copy-done | bytes 1310744
  12.5 0.0 copy-start.10
  12.5 1.0 %copy-done.10 = bf16[2,256,384]{2,1,0:T(8,128)(2,1)S(1)} copy-done((bf16[2,256,384]{2,1,0:T(8,128)(2,1)S(1)}, bf16[2,256,384]{2,1,0:T(8,128)(2,1)}, u32[]{:S(2)}) %copy-start.10) | copy-done | bytes 393240
  13.5 3.1 %shard_map.113 = (f32[2,256,1280]{2,1,0:T(8,128)S(1)}, f32[2,256,1280]{2,1,0:T(8,128)S(1)}) custom-call(s32[2]{0:T(128)S(1)} %pad_add_fusion.where, f32[5,512,128]{2,1,0:T(8,128)S(1)} %bitcast.9, f32[5,512,128]{2,1,0:T(8,128)S(1)} %bitcast.13, f32[5,5]{1,0:T(8,128)S(1)} %copy-done.8, bf16[2,256,384]{2,1,0:T(8,128)(2,1)S(1)} %copy-done.10), custom_call_target="tpu_custom_call" | custom-call | flops 1006632960 | bytes 8257636 | tf_op jit(solution)/shard_map/pallas_call | solution.py:227
  16.7 0.0 copy-start.5
  16.7 0.0 copy-start.6
  16.7 0.0 copy-start.7
  16.7 5.8 %collective-permute-done.3 = f32[5,128,128]{2,1,0:T(8,128)} collective-permute-done((f32[5,128,128]{2,1,0:T(8,128)}, f32[5,128,128]{2,1,0:T(8,128)}, u32[]{:S(2)}, u32[]{:S(2)}) %collective-permute-start.3) | collective-permute-done | bytes 327712 | tf_op jit(solution)/shard_map/ppermute | solution.py:282
  22.5 1.0 %broadcast_select_fusion.above = f32[5,128,128]{2,1,0:T(8,128)S(1)} fusion(f32[5,128,128]{2,1,0:T(8,128)} %collective-permute-done.3, pred[]{:T(512)S(6)} %eq.7), kind=kLoop, calls=%fused_computation.1 | loop fusion | flops 81920 | bytes 655361 | tf_op jit(solution)/shard_map/jit(_where)/select_n | solution.py:284
  23.5 0.0 collective-permute-done.2
  23.6 0.0 copy-start.2
  23.6 0.0 collective-permute-done.4.inner.outer
  23.6 0.0 copy-done.5
  23.6 0.0 copy-done.6
  23.6 0.0 copy-done.7
  23.7 4.0 %shard_map.115.refs_4_.refs_3_ = f32[5,512,128]{2,1,0:T(8,128)S(1)} custom-call(s32[2]{0:T(128)S(1)} %pad_add_fusion.where, f32[5,512,128]{2,1,0:T(8,128)S(1)} %bitcast.10, f32[5,128,128]{2,1,0:T(8,128)S(1)} %broadcast_select_fusion.1.below, f32[5,128,128]{2,1,0:T(8,128)S(1)} %broadcast_select_fusion.above, ...), custom_call_target="tpu_custom_call" | custom-call | flops 52428800 | bytes 3408172 | tf_op jit(solution)/shard_map/pallas_call | solution.py:227
  27.7 5.8 %collective-permute-done.1.refs_0_ = f32[5,512,128]{2,1,0:T(8,128)S(1)} collective-permute-done((f32[5,512,128]{2,1,0:T(8,128)}, f32[5,512,128]{2,1,0:T(8,128)S(1)}, u32[]{:S(2)}, u32[]{:S(2)}) %collective-permute-start.1) | collective-permute-done | bytes 1310752 | tf_op jit(solution)/shard_map/ppermute | solution.py:266
  33.4 0.0 copy-done.2
  33.5 0.0 copy-start.3
  33.5 0.0 copy-start.4
  33.5 1.7 %shard_map.116 = (f32[2,256,1280]{2,1,0:T(8,128)S(1)}, f32[416,128]{1,0:T(8,128)S(1)}, f32[96,128]{1,0:T(8,128)S(1)}, f32[416,128]{1,0:T(8,128)S(1)}, f32[96,128]{1,0:T(8,128)S(1)}) custom-call(s32[2]{0:T(128)S(1)} %pad_add_fusion.where, f32[5,512,128]{2,1,0:T(8,128)S(1)} %collective-permute-done.1.refs_0_, f32[2,256,1280]{2,1,0:T(8,128)S(1)} %get-tuple-element.12.refs_1_, ...), custom_call_target="tpu_custom_call" | custom-call | flops 503316480 | bytes 11403264 | tf_op jit(solution)/shard_map/pallas_call | solution.py:227
  35.2 2.1 %collective-permute-start.5 = (f32[416,128]{1,0:T(8,128)S(1)}, f32[416,128]{1,0:T(8,128)S(1)}, u32[]{:S(2)}, u32[]{:S(2)}) collective-permute-start(f32[416,128]{1,0:T(8,128)S(1)} %get-tuple-element.19), channel_id=1, source_target_pairs={{0,16},{16,0},{1,17},{17,1},{2,18},{18,2},{3,19},{19,3},{4,20},{20... | collective-permute-start | bytes 638984 | tf_op jit(solution)/shard_map/ppermute | solution.py:269
  37.3 0.0 collective-permute-start.6
  37.3 1.2 %collective-permute-done.6 = f32[96,128]{1,0:T(8,128)S(1)} collective-permute-done((f32[96,128]{1,0:T(8,128)S(1)}, f32[96,128]{1,0:T(8,128)S(1)}, u32[]{:S(2)}, u32[]{:S(2)}) %collective-permute-start.6) | collective-permute-done | bytes 49184 | tf_op jit(solution)/shard_map/ppermute | solution.py:339
  38.5 0.0 collective-permute-start.7
  38.5 0.6 %collective-permute-done.refs_1_ = f32[512,128]{1,0:T(8,128)S(1)} collective-permute-done((f32[512,128]{1,0:T(8,128)}, f32[512,128]{1,0:T(8,128)S(1)}, u32[]{:S(2)}, u32[]{:S(2)}) %collective-permute-start) | collective-permute-done | bytes 262176 | tf_op jit(solution)/shard_map/ppermute | solution.py:266
  39.1 0.0 copy-done.3
  39.1 0.0 copy-done.4
  39.1 3.7 %shard_map.117 = f32[5,512,128]{2,1,0:T(8,128)} custom-call(s32[2]{0:T(128)S(1)} %pad_add_fusion.where, f32[512,128]{1,0:T(8,128)S(1)} %bitcast.12, f32[512,128]{1,0:T(8,128)S(1)} %collective-permute-done.refs_1_, f32[2,256,1280]{2,1,0:T(8,128)S(1)} %get-tuple-element.17.refs_2_, f32[5,512,128]{2,1,0:T(8,128)S(1)} %shard_map.115.refs_4_.refs_3_, ...), custom_call_target="tpu_custom_call" | custom-call | flops 503316480 | bytes 6029412 | tf_op jit(solution)/shard_map/pallas_call | solution.py:227
  42.8 0.3 collective-permute-done.7
  43.1 0.2 collective-permute-done.5
  43.4 0.7 %maximum_negate_fusion = f32[512,128]{1,0:T(8,128)} fusion(f32[96,128]{1,0:T(8,128)S(1)} %add.7, f32[416,128]{1,0:T(8,128)S(1)} %add.6), kind=kLoop, calls=%fused_computation | loop fusion | flops 131072 | bytes 524288 | tf_op jit(solution)/shard_map/neg | solution.py:355
  (3 shorter events, 0.1 us)
Async XLA Ops:
  0.6 32.8 %collective-permute-start.1 = (f32[5,512,128]{2,1,0:T(8,128)}, f32[5,512,128]{2,1,0:T(8,128)S(1)}, u32[]{:S(2)}, u32[]{:S(2)}) collective-permute-start(f32[5,512,128]{2,1,0:T(8,128)} %bitcast.7), channel_id=1, source_target_pairs={{16,0},{0,16},{17,1},{1,17},{18,2},{2,18},{19,3},{3,19},{20,4},{4,... | collective-permute-start | bytes 3932168 | tf_op jit(solution)/shard_map/ppermute | solution.py:266
  3.6 1.4 %copy-start = (f32[5,128,4,128]{3,2,1,0:T(4,128)S(1)}, f32[5,128,4,128]{3,2,1,0:T(4,128)}, u32[]{:S(2)}) copy-start(f32[5,128,4,128]{3,2,1,0:T(4,128)} %param.10) | copy-start | bytes 3932164
  5.0 6.2 %copy-start.1 = (f32[5,128,4,128]{3,2,1,0:T(4,128)S(1)}, f32[5,128,4,128]{3,2,1,0:T(4,128)}, u32[]{:S(2)}) copy-start(f32[5,128,4,128]{3,2,1,0:T(4,128)} %param.10) | copy-start | bytes 3932164
  5.0 6.2 %copy-start.8 = (f32[5,5]{1,0:T(8,128)S(1)}, f32[5,5]{1,0:T(8,128)}, u32[]{:S(2)}) copy-start(f32[5,5]{1,0:T(8,128)} %refs_4_.1) | copy-start | bytes 304
  6.0 16.5 %collective-permute-start.3 = (f32[5,128,128]{2,1,0:T(8,128)}, f32[5,128,128]{2,1,0:T(8,128)}, u32[]{:S(2)}, u32[]{:S(2)}) collective-permute-start(f32[5,128,128]{2,1,0:T(8,128)} %get-tuple-element.15), channel_id=1, source_target_pairs={{0,14},{2,0},{4,2},{6,4},{8,6},{10,8},{12,10},{14,12},{1,15},{3,1}... | collective-permute-start | bytes 983048 | tf_op jit(solution)/shard_map/ppermute | solution.py:282
  10.6 13.0 %collective-permute-start.2 = (f32[5,128,128]{2,1,0:T(8,128)S(1)}, f32[5,128,128]{2,1,0:T(8,128)}, u32[]{:S(2)}, u32[]{:S(2)}) collective-permute-start(f32[5,128,128]{2,1,0:T(8,128)S(1)} %get-tuple-element.14), channel_id=1, source_target_pairs={{0,2},{2,4},{4,6},{6,8},{8,10},{10,12},{12,14},{14,0},{1,3},{3,5},... | collective-permute-start | bytes 983048 | tf_op jit(solution)/shard_map/ppermute | solution.py:281
  10.6 13.0 %collective-permute-start.4 = (f32[128,128]{1,0:T(8,128)S(1)}, f32[128,128]{1,0:T(8,128)S(1)}, u32[]{:S(2)}, u32[]{:S(2)}) collective-permute-start(f32[128,128]{1,0:T(8,128)S(1)} %get-tuple-element.16), channel_id=1, source_target_pairs={{0,1},{1,0},{2,3},{3,2},{4,5},{5,4},{6,7},{7,6},{8,9},{9,8},{10,11... | collective-permute-start | bytes 196616 | tf_op jit(solution)/shard_map/ppermute | solution.py:286
  10.6 28.5 %collective-permute-start = (f32[512,128]{1,0:T(8,128)}, f32[512,128]{1,0:T(8,128)S(1)}, u32[]{:S(2)}, u32[]{:S(2)}) collective-permute-start(f32[512,128]{1,0:T(8,128)} %bitcast.11), channel_id=1, source_target_pairs={{16,0},{0,16},{17,1},{1,17},{18,2},{2,18},{19,3},{3,19},{20,4},{4,... | collective-permute-start | bytes 786440 | tf_op jit(solution)/shard_map/ppermute | solution.py:266
  11.2 1.3 %copy-start.9 = (f32[5,128,4,128]{3,2,1,0:T(4,128)S(1)}, f32[5,128,4,128]{3,2,1,0:T(4,128)}, u32[]{:S(2)}) copy-start(f32[5,128,4,128]{3,2,1,0:T(4,128)} %param.11) | copy-start | bytes 3932164
  12.5 1.0 %copy-start.10 = (bf16[2,256,384]{2,1,0:T(8,128)(2,1)S(1)}, bf16[2,256,384]{2,1,0:T(8,128)(2,1)}, u32[]{:S(2)}) copy-start(bf16[2,256,384]{2,1,0:T(8,128)(2,1)} %constant.24.clone.table) | copy-start | bytes 1179652
  16.7 7.0 %copy-start.5 = (f32[5,5]{1,0:T(8,128)S(1)}, f32[5,5]{1,0:T(8,128)}, u32[]{:S(2)}) copy-start(f32[5,5]{1,0:T(8,128)} %jac_axial.1) | copy-start | bytes 304
  16.7 7.0 %copy-start.6 = (f32[5,5]{1,0:T(8,128)S(1)}, f32[5,5]{1,0:T(8,128)}, u32[]{:S(2)}) copy-start(f32[5,5]{1,0:T(8,128)} %jac_radial.1) | copy-start | bytes 304
  16.7 7.0 %copy-start.7 = (f32[5,5]{1,0:T(8,128)S(1)}, f32[5,5]{1,0:T(8,128)}, u32[]{:S(2)}) copy-start(f32[5,5]{1,0:T(8,128)} %jac_swirl.1) | copy-start | bytes 304
  23.6 9.8 %copy-start.2 = (bf16[2,1,256,384]{3,2,1,0:T(8,128)(2,1)S(1)}, bf16[2,1,256,384]{3,2,1,0:T(8,128)(2,1)}, u32[]{:S(2)}) copy-start(bf16[2,1,256,384]{3,2,1,0:T(8,128)(2,1)} %constant.25.clone.refs_3_) | copy-start | bytes 1179652
  33.5 5.6 %copy-start.3 = (f32[128,4,128]{2,1,0:T(4,128)S(1)}, f32[128,4,128]{2,1,0:T(4,128)}, u32[]{:S(2)}) copy-start(f32[128,4,128]{2,1,0:T(4,128)} %param.12) | copy-start | bytes 786436
  33.5 5.6 %copy-start.4 = (bf16[2,256,256]{2,1,0:T(8,128)(2,1)S(1)}, bf16[2,256,256]{2,1,0:T(8,128)(2,1)}, u32[]{:S(2)}) copy-start(bf16[2,256,256]{2,1,0:T(8,128)(2,1)} %constant.26.clone.refs_5_) | copy-start | bytes 786436
  35.2 8.2 %collective-permute-start.5 = (f32[416,128]{1,0:T(8,128)S(1)}, f32[416,128]{1,0:T(8,128)S(1)}, u32[]{:S(2)}, u32[]{:S(2)}) collective-permute-start(f32[416,128]{1,0:T(8,128)S(1)} %get-tuple-element.19), channel_id=1, source_target_pairs={{0,16},{16,0},{1,17},{17,1},{2,18},{18,2},{3,19},{19,3},{4,20},{20... | collective-permute-start | bytes 638984 | tf_op jit(solution)/shard_map/ppermute | solution.py:269
  37.3 1.2 %collective-permute-start.6 = (f32[96,128]{1,0:T(8,128)S(1)}, f32[96,128]{1,0:T(8,128)S(1)}, u32[]{:S(2)}, u32[]{:S(2)}) collective-permute-start(f32[96,128]{1,0:T(8,128)S(1)} %get-tuple-element.21), channel_id=1, source_target_pairs={{0,1},{1,0},{2,3},{3,2},{4,5},{5,4},{6,7},{7,6},{8,9},{9,8},{10,11... | collective-permute-start | bytes 147464 | tf_op jit(solution)/shard_map/ppermute | solution.py:339
  38.5 4.6 %collective-permute-start.7 = (f32[96,128]{1,0:T(8,128)S(1)}, f32[96,128]{1,0:T(8,128)S(1)}, u32[]{:S(2)}, u32[]{:S(2)}) collective-permute-start(f32[96,128]{1,0:T(8,128)S(1)} %collective-permute-done.6), channel_id=1, source_target_pairs={{0,17},{1,16},{16,1},{17,0},{2,19},{3,18},{18,3},{19,2},{4,21},{5,... | collective-permute-start | bytes 147464 | tf_op jit(solution)/shard_map/ppermute | solution.py:340

commit v11 on v10

--- a/solution.py
+++ b/solution.py
@@ -319,7 +319,7 @@
         32 * fields * fields * rows * lanes,
     )[0]
 
-    cuts = (0, modes * 13 // 16 // 8 * 8, modes)
+    cuts = (0, modes * 11 // 16 // 8 * 8, modes)
     pieces = len(cuts) - 1
     piece_rows = [(cuts[k + 1] - cuts[k]) * cells_ax for k in range(pieces)]
     joined = call(

time: 44.3 us -> 44.4 us (level)
  transfers between devices with their start and end apart: 8 -> 8, of which waited for: 6 -> 5; matrix products, arithmetic and copies ran while one was open for 3% -> 3% of each run, Pallas kernels for 31% -> 31%
where the time goes in v11:
time: 44.4 us; the launch traced here: 44.1 us
  waiting for transfers between devices  14 us (32%)
  Pallas kernels  13.6 us (31%)
  starting transfers between devices  10.2 us (23%)
  local copies, waits for them, and re-layouts  3.7 us (8%)
  other arithmetic  1.87 us (4%)
  between operations  0.77 us (2%)
    pallas_call x4, Pallas kernels, call(): pl.pallas_call(kernel, grid_spec=pltpu.PrefetchScalarGridSpec(num_scalar_...  12.6 us
    ppermute x2, waiting for transfers between devices, fetch(): lax.ppermute(value, 'mode', [((i + s) % groups, i) for i in range(groups)])  6.28 us
    ppermute x1, waiting for transfers between devices, body(): above = lax.ppermute(first, 'ax', down)  5.85 us
    ppermute x1, starting transfers between devices, body(): above = lax.ppermute(first, 'ax', down)  4.56 us
    unnamed x22, local copies, waits for them, and re-layouts  3.7 us
    ppermute x2, starting transfers between devices, fetch(): lax.ppermute(value, 'mode', [((i + s) % groups, i) for i in range(groups)])  3.54 us
    ppermute x1, starting transfers between devices, deliver(): lax.ppermute(value, 'mode', [(i, (i + s) % groups) for i in range(groups)])  2.12 us
    ppermute x1, waiting for transfers between devices, body(): sibling = lax.ppermute(parts[1][1], 'rad', [(0, 1), (1, 0)])  1.27 us
  transfers between devices with their start and end apart: 8, of which 5 were waited for; matrix products, arithmetic and copies ran while one was open for 3% of the time, Pallas kernels for 31%

profile of v11, /device:TPU:0, one launch (start us, length us, event | category | flops | bytes accessed | tf_op | source)
XLA Modules:
  0.0 44.1 jit_solution(3777475271347049114)
XLA Ops:
  0.6 3.0 %collective-permute-start.1 = (f32[5,512,128]{2,1,0:T(8,128)}, f32[5,512,128]{2,1,0:T(8,128)S(1)}, u32[]{:S(2)}, u32[]{:S(2)}) collective-permute-start(f32[5,512,128]{2,1,0:T(8,128)} %bitcast.7), channel_id=1, source_target_pairs={{16,0},{0,16},{17,1},{1,17},{18,2},{2,18},{19,3},{3,19},{20,4},{4,... | collective-permute-start | bytes 3932168 | tf_op jit(solution)/shard_map/ppermute | solution.py:266
  3.6 0.0 copy-start
  3.6 1.3 %copy-done = f32[5,128,4,128]{3,2,1,0:T(4,128)S(1)} copy-done((f32[5,128,4,128]{3,2,1,0:T(4,128)S(1)}, f32[5,128,4,128]{3,2,1,0:T(4,128)}, u32[]{:S(2)}) %copy-start) | copy-done | bytes 1310744
  5.0 0.0 copy-start.1
  5.0 0.0 copy-start.8
  5.0 1.1 %shard_map.114 = (f32[5,128,128]{2,1,0:T(8,128)}, f32[5,128,128]{2,1,0:T(8,128)S(1)}, f32[128,128]{1,0:T(8,128)S(1)}) custom-call(f32[5,512,128]{2,1,0:T(8,128)S(1)} %bitcast.8), custom_call_target="tpu_custom_call" | custom-call | tf_op jit(solution)/shard_map/pallas_call | solution.py:276
  6.0 4.6 %collective-permute-start.3 = (f32[5,128,128]{2,1,0:T(8,128)}, f32[5,128,128]{2,1,0:T(8,128)}, u32[]{:S(2)}, u32[]{:S(2)}) collective-permute-start(f32[5,128,128]{2,1,0:T(8,128)} %get-tuple-element.15), channel_id=1, source_target_pairs={{0,14},{2,0},{4,2},{6,4},{8,6},{10,8},{12,10},{14,12},{1,15},{3,1}... | collective-permute-start | bytes 983048 | tf_op jit(solution)/shard_map/ppermute | solution.py:282
  10.6 0.0 collective-permute-start.2
  10.6 0.0 collective-permute-start.4
  10.6 0.5 %collective-permute-start = (f32[512,128]{1,0:T(8,128)}, f32[512,128]{1,0:T(8,128)S(1)}, u32[]{:S(2)}, u32[]{:S(2)}) collective-permute-start(f32[512,128]{1,0:T(8,128)} %bitcast.11), channel_id=1, source_target_pairs={{16,0},{0,16},{17,1},{1,17},{18,2},{2,18},{19,3},{3,19},{20,4},{4,... | collective-permute-start | bytes 786440 | tf_op jit(solution)/shard_map/ppermute | solution.py:266
  11.1 0.1 pad_add_fusion.where
  11.2 0.0 copy-done.1
  11.2 0.0 copy-done.8
  11.2 0.0 copy-start.9
  11.2 1.3 %copy-done.9 = f32[5,128,4,128]{3,2,1,0:T(4,128)S(1)} copy-done((f32[5,128,4,128]{3,2,1,0:T(4,128)S(1)}, f32[5,128,4,128]{3,2,1,0:T(4,128)}, u32[]{:S(2)}) %copy-start.9) | copy-done | bytes 1310744
  12.5 0.0 copy-start.10
  12.5 1.0 %copy-done.10 = bf16[2,256,384]{2,1,0:T(8,128)(2,1)S(1)} copy-done((bf16[2,256,384]{2,1,0:T(8,128)(2,1)S(1)}, bf16[2,256,384]{2,1,0:T(8,128)(2,1)}, u32[]{:S(2)}) %copy-start.10) | copy-done | bytes 393240
  13.5 3.1 %shard_map.113 = (f32[2,256,1280]{2,1,0:T(8,128)S(1)}, f32[2,256,1280]{2,1,0:T(8,128)S(1)}) custom-call(s32[2]{0:T(128)S(1)} %pad_add_fusion.where, f32[5,512,128]{2,1,0:T(8,128)S(1)} %bitcast.9, f32[5,512,128]{2,1,0:T(8,128)S(1)} %bitcast.13, f32[5,5]{1,0:T(8,128)S(1)} %copy-done.8, bf16[2,256,384]{2,1,0:T(8,128)(2,1)S(1)} %copy-done.10), custom_call_target="tpu_custom_call" | custom-call | flops 1006632960 | bytes 8257636 | tf_op jit(solution)/shard_map/pallas_call | solution.py:227
  16.7 0.0 copy-start.5
  16.7 0.0 copy-start.6
  16.7 0.0 copy-start.7
  16.7 5.8 %collective-permute-done.3 = f32[5,128,128]{2,1,0:T(8,128)} collective-permute-done((f32[5,128,128]{2,1,0:T(8,128)}, f32[5,128,128]{2,1,0:T(8,128)}, u32[]{:S(2)}, u32[]{:S(2)}) %collective-permute-start.3) | collective-permute-done | bytes 327712 | tf_op jit(solution)/shard_map/ppermute | solution.py:282
  22.5 1.0 %broadcast_select_fusion.above = f32[5,128,128]{2,1,0:T(8,128)S(1)} fusion(f32[5,128,128]{2,1,0:T(8,128)} %collective-permute-done.3, pred[]{:T(512)S(6)} %eq.7), kind=kLoop, calls=%fused_computation.1 | loop fusion | flops 81920 | bytes 655361 | tf_op jit(solution)/shard_map/jit(_where)/select_n | solution.py:284
  23.5 0.0 collective-permute-done.2
  23.6 0.0 copy-start.2
  23.6 0.0 collective-permute-done.4.inner.outer
  23.6 0.0 copy-done.5
  23.6 0.0 copy-done.6
  23.6 0.0 copy-done.7
  23.7 4.0 %shard_map.115.refs_4_.refs_3_ = f32[5,512,128]{2,1,0:T(8,128)S(1)} custom-call(s32[2]{0:T(128)S(1)} %pad_add_fusion.where, f32[5,512,128]{2,1,0:T(8,128)S(1)} %bitcast.10, f32[5,128,128]{2,1,0:T(8,128)S(1)} %broadcast_select_fusion.1.below, f32[5,128,128]{2,1,0:T(8,128)S(1)} %broadcast_select_fusion.above, ...), custom_call_target="tpu_custom_call" | custom-call | flops 52428800 | bytes 3408172 | tf_op jit(solution)/shard_map/pallas_call | solution.py:227
  27.7 5.8 %collective-permute-done.1.refs_0_ = f32[5,512,128]{2,1,0:T(8,128)S(1)} collective-permute-done((f32[5,512,128]{2,1,0:T(8,128)}, f32[5,512,128]{2,1,0:T(8,128)S(1)}, u32[]{:S(2)}, u32[]{:S(2)}) %collective-permute-start.1) | collective-permute-done | bytes 1310752 | tf_op jit(solution)/shard_map/ppermute | solution.py:266
  33.4 0.0 copy-done.2
  33.5 0.0 copy-start.3
  33.5 0.0 copy-start.4
  33.5 1.7 %shard_map.116 = (f32[2,256,1280]{2,1,0:T(8,128)S(1)}, f32[352,128]{1,0:T(8,128)S(1)}, f32[160,128]{1,0:T(8,128)S(1)}, f32[352,128]{1,0:T(8,128)S(1)}, f32[160,128]{1,0:T(8,128)S(1)}) custom-call(s32[2]{0:T(128)S(1)} %pad_add_fusion.where, f32[5,512,128]{2,1,0:T(8,128)S(1)} %collective-permute-done.1.refs_0_, f32[2,256,1280]{2,1,0:T(8,128)S(1)} %get-tuple-element.12.refs_1_, ...), custom_call_target="tpu_custom_call" | custom-call | flops 503316480 | bytes 11403264 | tf_op jit(solution)/shard_map/pallas_call | solution.py:227
  35.2 2.1 %collective-permute-start.5 = (f32[352,128]{1,0:T(8,128)S(1)}, f32[352,128]{1,0:T(8,128)S(1)}, u32[]{:S(2)}, u32[]{:S(2)}) collective-permute-start(f32[352,128]{1,0:T(8,128)S(1)} %get-tuple-element.19), channel_id=1, source_target_pairs={{0,16},{16,0},{1,17},{17,1},{2,18},{18,2},{3,19},{19,3},{4,20},{20... | collective-permute-start | bytes 540680 | tf_op jit(solution)/shard_map/ppermute | solution.py:269
  37.3 0.0 collective-permute-start.6
  37.3 1.3 %collective-permute-done.6 = f32[160,128]{1,0:T(8,128)S(1)} collective-permute-done((f32[160,128]{1,0:T(8,128)S(1)}, f32[160,128]{1,0:T(8,128)S(1)}, u32[]{:S(2)}, u32[]{:S(2)}) %collective-permute-start.6) | collective-permute-done | bytes 81952 | tf_op jit(solution)/shard_map/ppermute | solution.py:339
  38.6 0.0 collective-permute-start.7
  38.6 0.5 %collective-permute-done.refs_1_ = f32[512,128]{1,0:T(8,128)S(1)} collective-permute-done((f32[512,128]{1,0:T(8,128)}, f32[512,128]{1,0:T(8,128)S(1)}, u32[]{:S(2)}, u32[]{:S(2)}) %collective-permute-start) | collective-permute-done | bytes 262176 | tf_op jit(solution)/shard_map/ppermute | solution.py:266
  39.1 0.0 copy-done.3
  39.1 0.0 copy-done.4
  39.1 3.7 %shard_map.117 = f32[5,512,128]{2,1,0:T(8,128)} custom-call(s32[2]{0:T(128)S(1)} %pad_add_fusion.where, f32[512,128]{1,0:T(8,128)S(1)} %bitcast.12, f32[512,128]{1,0:T(8,128)S(1)} %collective-permute-done.refs_1_, f32[2,256,1280]{2,1,0:T(8,128)S(1)} %get-tuple-element.17.refs_2_, f32[5,512,128]{2,1,0:T(8,128)S(1)} %shard_map.115.refs_4_.refs_3_, ...), custom_call_target="tpu_custom_call" | custom-call | flops 503316480 | bytes 6029412 | tf_op jit(solution)/shard_map/pallas_call | solution.py:227
  42.8 0.6 %collective-permute-done.7 = f32[160,128]{1,0:T(8,128)S(1)} collective-permute-done((f32[160,128]{1,0:T(8,128)S(1)}, f32[160,128]{1,0:T(8,128)S(1)}, u32[]{:S(2)}, u32[]{:S(2)}) %collective-permute-start.7) | collective-permute-done | bytes 81952 | tf_op jit(solution)/shard_map/ppermute | solution.py:340
  43.4 0.0 collective-permute-done.5
  43.4 0.7 %maximum_negate_fusion = f32[512,128]{1,0:T(8,128)} fusion(f32[160,128]{1,0:T(8,128)S(1)} %add.7, f32[352,128]{1,0:T(8,128)S(1)} %add.6), kind=kLoop, calls=%fused_computation | loop fusion | flops 131072 | bytes 524288 | tf_op jit(solution)/shard_map/neg | solution.py:355
  (3 shorter events, 0.1 us)
Async XLA Ops:
  0.6 32.8 %collective-permute-start.1 = (f32[5,512,128]{2,1,0:T(8,128)}, f32[5,512,128]{2,1,0:T(8,128)S(1)}, u32[]{:S(2)}, u32[]{:S(2)}) collective-permute-start(f32[5,512,128]{2,1,0:T(8,128)} %bitcast.7), channel_id=1, source_target_pairs={{16,0},{0,16},{17,1},{1,17},{18,2},{2,18},{19,3},{3,19},{20,4},{4,... | collective-permute-start | bytes 3932168 | tf_op jit(solution)/shard_map/ppermute | solution.py:266
  3.6 1.4 %copy-start = (f32[5,128,4,128]{3,2,1,0:T(4,128)S(1)}, f32[5,128,4,128]{3,2,1,0:T(4,128)}, u32[]{:S(2)}) copy-start(f32[5,128,4,128]{3,2,1,0:T(4,128)} %param.10) | copy-start | bytes 3932164
  5.0 6.2 %copy-start.1 = (f32[5,128,4,128]{3,2,1,0:T(4,128)S(1)}, f32[5,128,4,128]{3,2,1,0:T(4,128)}, u32[]{:S(2)}) copy-start(f32[5,128,4,128]{3,2,1,0:T(4,128)} %param.10) | copy-start | bytes 3932164
  5.0 6.2 %copy-start.8 = (f32[5,5]{1,0:T(8,128)S(1)}, f32[5,5]{1,0:T(8,128)}, u32[]{:S(2)}) copy-start(f32[5,5]{1,0:T(8,128)} %refs_4_.1) | copy-start | bytes 304
  6.0 16.5 %collective-permute-start.3 = (f32[5,128,128]{2,1,0:T(8,128)}, f32[5,128,128]{2,1,0:T(8,128)}, u32[]{:S(2)}, u32[]{:S(2)}) collective-permute-start(f32[5,128,128]{2,1,0:T(8,128)} %get-tuple-element.15), channel_id=1, source_target_pairs={{0,14},{2,0},{4,2},{6,4},{8,6},{10,8},{12,10},{14,12},{1,15},{3,1}... | collective-permute-start | bytes 983048 | tf_op jit(solution)/shard_map/ppermute | solution.py:282
  10.6 13.0 %collective-permute-start.2 = (f32[5,128,128]{2,1,0:T(8,128)S(1)}, f32[5,128,128]{2,1,0:T(8,128)}, u32[]{:S(2)}, u32[]{:S(2)}) collective-permute-start(f32[5,128,128]{2,1,0:T(8,128)S(1)} %get-tuple-element.14), channel_id=1, source_target_pairs={{0,2},{2,4},{4,6},{6,8},{8,10},{10,12},{12,14},{14,0},{1,3},{3,5},... | collective-permute-start | bytes 983048 | tf_op jit(solution)/shard_map/ppermute | solution.py:281
  10.6 13.0 %collective-permute-start.4 = (f32[128,128]{1,0:T(8,128)S(1)}, f32[128,128]{1,0:T(8,128)S(1)}, u32[]{:S(2)}, u32[]{:S(2)}) collective-permute-start(f32[128,128]{1,0:T(8,128)S(1)} %get-tuple-element.16), channel_id=1, source_target_pairs={{0,1},{1,0},{2,3},{3,2},{4,5},{5,4},{6,7},{7,6},{8,9},{9,8},{10,11... | collective-permute-start | bytes 196616 | tf_op jit(solution)/shard_map/ppermute | solution.py:286
  10.6 28.5 %collective-permute-start = (f32[512,128]{1,0:T(8,128)}, f32[512,128]{1,0:T(8,128)S(1)}, u32[]{:S(2)}, u32[]{:S(2)}) collective-permute-start(f32[512,128]{1,0:T(8,128)} %bitcast.11), channel_id=1, source_target_pairs={{16,0},{0,16},{17,1},{1,17},{18,2},{2,18},{19,3},{3,19},{20,4},{4,... | collective-permute-start | bytes 786440 | tf_op jit(solution)/shard_map/ppermute | solution.py:266
  11.2 1.3 %copy-start.9 = (f32[5,128,4,128]{3,2,1,0:T(4,128)S(1)}, f32[5,128,4,128]{3,2,1,0:T(4,128)}, u32[]{:S(2)}) copy-start(f32[5,128,4,128]{3,2,1,0:T(4,128)} %param.11) | copy-start | bytes 3932164
  12.5 1.0 %copy-start.10 = (bf16[2,256,384]{2,1,0:T(8,128)(2,1)S(1)}, bf16[2,256,384]{2,1,0:T(8,128)(2,1)}, u32[]{:S(2)}) copy-start(bf16[2,256,384]{2,1,0:T(8,128)(2,1)} %constant.24.clone.table) | copy-start | bytes 1179652
  16.7 7.0 %copy-start.5 = (f32[5,5]{1,0:T(8,128)S(1)}, f32[5,5]{1,0:T(8,128)}, u32[]{:S(2)}) copy-start(f32[5,5]{1,0:T(8,128)} %jac_axial.1) | copy-start | bytes 304
  16.7 7.0 %copy-start.6 = (f32[5,5]{1,0:T(8,128)S(1)}, f32[5,5]{1,0:T(8,128)}, u32[]{:S(2)}) copy-start(f32[5,5]{1,0:T(8,128)} %jac_radial.1) | copy-start | bytes 304
  16.7 7.0 %copy-start.7 = (f32[5,5]{1,0:T(8,128)S(1)}, f32[5,5]{1,0:T(8,128)}, u32[]{:S(2)}) copy-start(f32[5,5]{1,0:T(8,128)} %jac_swirl.1) | copy-start | bytes 304
  23.6 9.8 %copy-start.2 = (bf16[2,1,256,384]{3,2,1,0:T(8,128)(2,1)S(1)}, bf16[2,1,256,384]{3,2,1,0:T(8,128)(2,1)}, u32[]{:S(2)}) copy-start(bf16[2,1,256,384]{3,2,1,0:T(8,128)(2,1)} %constant.25.clone.refs_3_) | copy-start | bytes 1179652
  33.5 5.6 %copy-start.3 = (f32[128,4,128]{2,1,0:T(4,128)S(1)}, f32[128,4,128]{2,1,0:T(4,128)}, u32[]{:S(2)}) copy-start(f32[128,4,128]{2,1,0:T(4,128)} %param.12) | copy-start | bytes 786436
  33.5 5.6 %copy-start.4 = (bf16[2,256,256]{2,1,0:T(8,128)(2,1)S(1)}, bf16[2,256,256]{2,1,0:T(8,128)(2,1)}, u32[]{:S(2)}) copy-start(bf16[2,256,256]{2,1,0:T(8,128)(2,1)} %constant.26.clone.refs_5_) | copy-start | bytes 786436
  35.2 8.2 %collective-permute-start.5 = (f32[352,128]{1,0:T(8,128)S(1)}, f32[352,128]{1,0:T(8,128)S(1)}, u32[]{:S(2)}, u32[]{:S(2)}) collective-permute-start(f32[352,128]{1,0:T(8,128)S(1)} %get-tuple-element.19), channel_id=1, source_target_pairs={{0,16},{16,0},{1,17},{17,1},{2,18},{18,2},{3,19},{19,3},{4,20},{20... | collective-permute-start | bytes 540680 | tf_op jit(solution)/shard_map/ppermute | solution.py:269
  37.3 1.3 %collective-permute-start.6 = (f32[160,128]{1,0:T(8,128)S(1)}, f32[160,128]{1,0:T(8,128)S(1)}, u32[]{:S(2)}, u32[]{:S(2)}) collective-permute-start(f32[160,128]{1,0:T(8,128)S(1)} %get-tuple-element.21), channel_id=1, source_target_pairs={{0,1},{1,0},{2,3},{3,2},{4,5},{5,4},{6,7},{7,6},{8,9},{9,8},{10,11... | collective-permute-start | bytes 245768 | tf_op jit(solution)/shard_map/ppermute | solution.py:339
  38.6 4.8 %collective-permute-start.7 = (f32[160,128]{1,0:T(8,128)S(1)}, f32[160,128]{1,0:T(8,128)S(1)}, u32[]{:S(2)}, u32[]{:S(2)}) collective-permute-start(f32[160,128]{1,0:T(8,128)S(1)} %collective-permute-done.6), channel_id=1, source_target_pairs={{0,17},{1,16},{16,1},{17,0},{2,19},{3,18},{18,3},{19,2},{4,21},{5,... | collective-permute-start | bytes 245768 | tf_op jit(solution)/shard_map/ppermute | solution.py:340
